TPU v7x, 32 devices: a whole 2x2x4 slice. The times are simulated.
32 devices in a mesh: wide: 8 (over y, x, core), narrow: 4 (over z).
Axes of the slice: x: 2, y: 2, z: 4, core: 2. Of those that a mesh axis runs over, the one named last changes fastest.
Arguments:
- tokens: bfloat16 [2, 4, 2048, 960], P(None, 'narrow', 'wide'), may hold values from -6 to 6
- lengths: int32 [2, 4, 4], P(None, 'narrow'), may hold values from 1 to 1024, 2048 in all within a row
- block_plan: int32 [2, 4, 16], P(None, 'narrow'), may hold values from 0 to 15, each once within a row
- attn_gain: float32 [960], replicated, may hold values from 0.1 to 1.9
- w_query: bfloat16 [960, 960], P('wide'), may hold values from -0.25 to 0.25
- w_key: bfloat16 [960, 320], P('wide'), may hold values from -0.25 to 0.25
- w_value: bfloat16 [960, 320], P('wide'), may hold values from -0.1875 to 0.1875
- w_out: bfloat16 [960, 960], P('wide'), may hold values from -1 to 1
- ffn_gain: float32 [960], replicated, may hold values from 0.1 to 1.9
- w_gate: bfloat16 [960, 2560], P('wide'), may hold values from -0.1875 to 0.1875
- w_up: bfloat16 [960, 2560], P('wide'), may hold values from -0.1875 to 0.1875
- w_down: bfloat16 [2560, 960], P('wide'), may hold values from -0.125 to 0.125
- cotangent: bfloat16 [2, 4, 2048, 960], P(None, 'narrow', 'wide'), may hold values from -6 to 6
Outputs:
- layer_out: bfloat16 [2, 4, 2048, 960], P(None, 'narrow', 'wide')
- grad_tokens: float32 [2, 4, 2048, 960], P(None, 'narrow', 'wide')
- grad_attn_gain: float32 [960], replicated
- grad_query: float32 [960, 960], P('wide')
- grad_key: float32 [960, 320], P('wide')
- grad_value: float32 [960, 320], P('wide')
- grad_out: float32 [960, 960], P('wide')
- grad_ffn_gain: float32 [960], replicated
- grad_gate: float32 [960, 2560], P('wide')
- grad_up: float32 [960, 2560], P('wide')
- grad_down: float32 [2560, 960], P('wide')
Inputs may be any that keep to these rules, and one draw needn't show every extreme that they name: In each row the 4 lengths add up to 2048, the documents follow one another from position 0, and the longest is exactly 1024 tokens. For each micro-batch and row the plan names every block of the row once: slots j * 128 to j * 128 + 127 hold the tokens from position block_plan[j] * 128 on.
All inputs are finite; a program needn't handle non-finite values.
Results may differ from a plain program's by a relative error of at most 0.023.
Values may be sent and summed in bfloat16 or wider, within the bound.
A program may use at most 256 MiB of HBM per device.

v0:
```python
import functools

import jax
import jax.numpy as jnp
from jax import lax
from jax.sharding import PartitionSpec as P

HDIM = 64
BLOCK = 128


EPS = 1e-05
ROPE_BASE = 100000.0
NEG_FILL = -1e30


def places(block_plan_row, length_row, block_size):
    in_block = jnp.arange(block_size, dtype=jnp.int32)
    position = (block_plan_row[:, None] * block_size + in_block[None, :]).reshape(-1)
    doc_ends = jnp.cumsum(length_row)
    is_after = position[:, None] >= doc_ends[None, :]
    document = jnp.sum(is_after.astype(jnp.int32), axis=1)
    doc_begin = jnp.sum(jnp.where(is_after, length_row[None, :], 0), axis=1)
    return (position, document, position - doc_begin)


def rotary_tables(in_document):
    half_dim = HDIM // 2
    frequency = ROPE_BASE ** (-2.0 * jnp.arange(half_dim, dtype=jnp.float32) / HDIM)
    angles = in_document.astype(jnp.float32)[:, None] * frequency[None, :]
    angles = jnp.concatenate([angles, angles], axis=1)
    return (jnp.cos(angles), jnp.sin(angles))


def rotate(operand, cosine_table, sine_table):
    row_total = operand.shape[0]
    per_head = operand.reshape(row_total, -1, HDIM)
    half_dim = HDIM // 2
    turned = jnp.concatenate([-per_head[..., half_dim:], per_head[..., :half_dim]], axis=-1)
    return (per_head * cosine_table[:, None, :] + turned * sine_table[:, None, :]).reshape(
        row_total, -1
    )


def rms_norm(operand, gain_vec):
    return operand * lax.rsqrt(jnp.mean(operand * operand, axis=-1, keepdims=True) + EPS) * gain_vec


def swiglu(gate_lin, up_lin):
    return gate_lin / (1.0 + jnp.exp(-gate_lin)) * up_lin


def fold_with(source, pieces):
    return tuple(
        (jnp.dot(source, portion, preferred_element_type=jnp.float32) for portion in pieces)
    )


def map_with(gradients, pieces):
    products = [
        lax.dot_general(
            gradient, portion, (((1,), (1,)), ((), ())), preferred_element_type=jnp.float32
        )
        for gradient, portion in zip(gradients, pieces)
    ]
    return functools.reduce(lambda first, second: first + second, products)


def weight_terms(pack):
    normed, grad_qkv, attended, grad_attn, normed_two, grad_gu, hidden, grad_out_rows = pack
    products = []
    for source, target in ((normed, grad_qkv), (attended, grad_attn), (normed_two, grad_gu)):
        columns = source
        products.append(
            lax.dot_general(
                columns, target, (((0,), (0,)), ((), ())), preferred_element_type=jnp.float32
            )
        )
    width_part = lax.psum_scatter(
        jnp.concatenate(products, axis=1).astype(jnp.bfloat16),
        "wide",
        scatter_dimension=0,
        tiled=True,
    ).astype(jnp.float32)
    columns = hidden
    hidden_part = lax.psum_scatter(
        lax.dot_general(
            columns, grad_out_rows, (((0,), (0,)), ((), ())), preferred_element_type=jnp.float32
        ).astype(jnp.bfloat16),
        "wide",
        scatter_dimension=0,
        tiled=True,
    ).astype(jnp.float32)
    return (width_part, hidden_part)


def shards(
    tokens,
    lengths,
    block_plan,
    attn_gain,
    w_query,
    w_key,
    w_value,
    w_out,
    ffn_gain,
    w_gate,
    w_up,
    w_down,
    cotangent,
):
    wide_at = lax.axis_index("wide")
    micro_total = tokens.shape[0]
    slot_count = tokens.shape[2]
    model_width = tokens.shape[3]
    key_width = w_key.shape[1]
    ffn_width = w_gate.shape[1]
    row_length = slot_count * lax.axis_size("wide")
    key_block = min(512, row_length)
    key_blocks = row_length // key_block
    head_count = model_width // HDIM
    kv_count = key_width // HDIM
    group_size = head_count // kv_count
    score_scale = HDIM ** (-0.5)
    outputs = []
    input_grads = []
    gradient_sums = None
    gain_first = jnp.zeros((model_width,), jnp.float32)
    gain_second = jnp.zeros((model_width,), jnp.float32)
    for micro_at in range(micro_total):
        inputs = tokens[micro_at, 0].astype(jnp.float32)
        position, document, in_document = places(
            block_plan[micro_at, 0], lengths[micro_at, 0], BLOCK
        )
        own_position = lax.dynamic_slice_in_dim(position, wide_at * slot_count, slot_count)
        own_document = lax.dynamic_slice_in_dim(document, wide_at * slot_count, slot_count)
        own_local = lax.dynamic_slice_in_dim(in_document, wide_at * slot_count, slot_count)
        allowed = (own_document[:, None] == document[None, :]) & (
            position[None, :] <= own_position[:, None]
        )
        block_mask = allowed.reshape(slot_count, key_blocks, key_block).transpose(1, 0, 2)
        live_blocks = jnp.any(block_mask, axis=(1, 2))
        cosine_table, sine_table = rotary_tables(own_local)
        normed = rms_norm(inputs, attn_gain).astype(jnp.bfloat16)
        query_lin, key_lin, value_lin = fold_with(
            normed,
            (
                lax.all_gather(w_query, "wide", axis=0, tiled=True),
                lax.all_gather(w_key, "wide", axis=0, tiled=True),
                lax.all_gather(w_value, "wide", axis=0, tiled=True),
            ),
        )
        query = rotate(query_lin, cosine_table, sine_table).astype(jnp.bfloat16)
        key_rot = rotate(key_lin, cosine_table, sine_table).astype(jnp.bfloat16)
        value_rows = value_lin.astype(jnp.bfloat16)
        keys_all, values_all = (
            lax.all_gather(key_rot, "wide", axis=0, tiled=True),
            lax.all_gather(value_rows, "wide", axis=0, tiled=True),
        )

        def split_queries(operand):
            return operand.reshape(slot_count, kv_count, group_size, HDIM).transpose(1, 0, 2, 3)

        def split_keys(operand):
            return operand.reshape(key_blocks, key_block, kv_count, HDIM).transpose(2, 0, 1, 3)

        query_groups = split_queries(query)
        key_groups = split_keys(keys_all)
        value_groups = split_keys(values_all)

        def scores_of(group_query, group_keys):

            def scores_one_block(element):
                key_part, active = element
                return lax.cond(
                    active,
                    lambda: jnp.einsum(
                        "qgd,kd->gqk", group_query, key_part, preferred_element_type=jnp.float32
                    ),
                    lambda: jnp.zeros((group_size, slot_count, key_block), jnp.float32),
                )

            products = lax.map(scores_one_block, (group_keys, live_blocks)) * score_scale
            return jnp.where(block_mask[:, None], products, NEG_FILL)

        def forward_group(element):
            group_query, group_keys, group_values = element
            scores = scores_of(group_query, group_keys)
            row_top = jnp.max(scores, axis=(0, 3), keepdims=True)
            raw_weights = jnp.where(block_mask[:, None], jnp.exp(scores - row_top), 0.0)
            denominator = jnp.sum(raw_weights, axis=(0, 3), keepdims=True)
            soft_weights = (raw_weights / denominator).astype(jnp.bfloat16)

            def forward_one_block(inner):
                weight_part, value_part, active = inner
                return lax.cond(
                    active,
                    lambda: jnp.einsum(
                        "gqk,kd->qgd", weight_part, value_part, preferred_element_type=jnp.float32
                    ),
                    lambda: jnp.zeros((slot_count, group_size, HDIM), jnp.float32),
                )

            summed = jnp.sum(
                lax.map(forward_one_block, (soft_weights, group_values, live_blocks)), axis=0
            )
            return (summed, (row_top + jnp.log(denominator))[0, :, :, 0])

        attended_groups, log_totals = lax.map(
            forward_group, (query_groups, key_groups, value_groups)
        )
        attended = (
            attended_groups.transpose(1, 0, 2, 3)
            .reshape(slot_count, model_width)
            .astype(jnp.bfloat16)
        )
        (attn_lin,) = fold_with(attended, (lax.all_gather(w_out, "wide", axis=0, tiled=True),))
        residual = inputs + attn_lin
        normed_two = rms_norm(residual, ffn_gain).astype(jnp.bfloat16)
        gate_lin, up_lin = fold_with(
            normed_two,
            (
                lax.all_gather(w_gate, "wide", axis=0, tiled=True),
                lax.all_gather(w_up, "wide", axis=0, tiled=True),
            ),
        )
        hidden = swiglu(gate_lin, up_lin).astype(jnp.bfloat16)
        (down_lin,) = fold_with(hidden, (lax.all_gather(w_down, "wide", axis=0, tiled=True),))
        outputs.append((residual + down_lin).astype(jnp.bfloat16))
        grad_out_rows = cotangent[micro_at, 0]
        grad_hidden = map_with(
            (grad_out_rows,), lax.all_gather((w_down,), "wide", axis=0, tiled=True)
        )
        unused_hidden, pull_swiglu = jax.vjp(swiglu, gate_lin, up_lin)
        grad_gate_lin, grad_up_lin = pull_swiglu(grad_hidden)
        grad_gate_low = grad_gate_lin.astype(jnp.bfloat16)
        grad_up_low = grad_up_lin.astype(jnp.bfloat16)
        grad_normed_two = map_with(
            (grad_gate_low, grad_up_low), lax.all_gather((w_gate, w_up), "wide", axis=0, tiled=True)
        )
        unused_norm, pull_norm_two = jax.vjp(rms_norm, residual, ffn_gain)
        grad_residual_norm, grad_gain_two = pull_norm_two(grad_normed_two)
        grad_residual = grad_residual_norm + grad_out_rows.astype(jnp.float32)
        grad_attn = grad_residual.astype(jnp.bfloat16)
        grad_attended = map_with(
            (grad_attn,), lax.all_gather((w_out,), "wide", axis=0, tiled=True)
        ).astype(jnp.bfloat16)
        grad_attended_groups = split_queries(grad_attended)

        def backward_group(element):
            group_query, group_keys, group_values, group_grads, group_log = element
            scores = scores_of(group_query, group_keys)
            soft_full = jnp.where(
                block_mask[:, None], jnp.exp(scores - group_log[None, :, :, None]), 0.0
            )

            def first_pass(inner):
                value_part, active = inner
                return lax.cond(
                    active,
                    lambda: jnp.einsum(
                        "qgd,kd->gqk", group_grads, value_part, preferred_element_type=jnp.float32
                    ),
                    lambda: jnp.zeros((group_size, slot_count, key_block), jnp.float32),
                )

            grad_weights = lax.map(first_pass, (group_values, live_blocks))
            inner_sum = jnp.sum(soft_full * grad_weights, axis=(0, 3), keepdims=True)
            grad_scores = (soft_full * (grad_weights - inner_sum)).astype(jnp.bfloat16)
            soft_low = soft_full.astype(jnp.bfloat16)

            def second_pass(inner):
                score_part, weight_part, key_part, active = inner

                def compute():
                    return (
                        jnp.einsum(
                            "gqk,kd->qgd", score_part, key_part, preferred_element_type=jnp.float32
                        ),
                        jnp.einsum(
                            "gqk,qgd->kd",
                            score_part,
                            group_query,
                            preferred_element_type=jnp.float32,
                        ),
                        jnp.einsum(
                            "gqk,qgd->kd",
                            weight_part,
                            group_grads,
                            preferred_element_type=jnp.float32,
                        ),
                    )

                def nothing():
                    return (
                        jnp.zeros((slot_count, group_size, HDIM), jnp.float32),
                        jnp.zeros((key_block, HDIM), jnp.float32),
                        jnp.zeros((key_block, HDIM), jnp.float32),
                    )

                return lax.cond(active, compute, nothing)

            query_parts, key_parts, value_parts = lax.map(
                second_pass, (grad_scores, soft_low, group_keys, live_blocks)
            )
            return (
                jnp.sum(query_parts, axis=0) * score_scale,
                key_parts * score_scale,
                value_parts,
            )

        grad_query_groups, grad_key_groups, grad_value_groups = lax.map(
            backward_group,
            (query_groups, key_groups, value_groups, grad_attended_groups, log_totals),
        )
        grad_query_rot = grad_query_groups.transpose(1, 0, 2, 3).reshape(slot_count, model_width)
        grad_key_all = grad_key_groups.transpose(1, 2, 0, 3).reshape(row_length, key_width)
        grad_value_all = grad_value_groups.transpose(1, 2, 0, 3).reshape(row_length, key_width)
        grad_key_own, grad_value_own = (
            lax.psum_scatter(
                grad_key_all.astype(jnp.bfloat16), "wide", scatter_dimension=0, tiled=True
            ).astype(jnp.float32),
            lax.psum_scatter(
                grad_value_all.astype(jnp.bfloat16), "wide", scatter_dimension=0, tiled=True
            ).astype(jnp.float32),
        )
        unused_rot, pull_query = jax.vjp(
            lambda operand: rotate(operand, cosine_table, sine_table), query_lin
        )
        unused_key, pull_key = jax.vjp(
            lambda operand: rotate(operand, cosine_table, sine_table), key_lin
        )
        grad_query_low = pull_query(grad_query_rot)[0].astype(jnp.bfloat16)
        grad_key_low = pull_key(grad_key_own)[0].astype(jnp.bfloat16)
        grad_value_low = grad_value_own.astype(jnp.bfloat16)
        grad_normed = map_with(
            (grad_query_low, grad_key_low, grad_value_low),
            lax.all_gather((w_query, w_key, w_value), "wide", axis=0, tiled=True),
        )
        unused_first, pull_norm_one = jax.vjp(rms_norm, inputs, attn_gain)
        grad_inputs_norm, grad_gain_one = pull_norm_one(grad_normed)
        input_grads.append(grad_inputs_norm + grad_residual)
        gain_first = gain_first + grad_gain_one
        gain_second = gain_second + grad_gain_two
        record = (
            normed,
            jnp.concatenate([grad_query_low, grad_key_low, grad_value_low], axis=1),
            attended,
            grad_attn,
            normed_two,
            jnp.concatenate([grad_gate_low, grad_up_low], axis=1),
            hidden,
            grad_out_rows,
        )
        partials = weight_terms(record)
        gradient_sums = (
            partials
            if gradient_sums is None
            else (gradient_sums[0] + partials[0], gradient_sums[1] + partials[1])
        )
    width_grads, hidden_grads = (
        lax.psum(gradient_sums[0].astype(jnp.bfloat16), "narrow").astype(jnp.float32),
        lax.psum(gradient_sums[1].astype(jnp.bfloat16), "narrow").astype(jnp.float32),
    )
    gain_one_total, gain_two_total = lax.psum((gain_first, gain_second), ("wide", "narrow"))
    key_end = model_width + key_width
    value_end = key_end + key_width
    out_end = value_end + model_width
    gate_end = out_end + ffn_width
    grad_query = width_grads[:, :model_width]
    grad_key = width_grads[:, model_width:key_end]
    grad_value = width_grads[:, key_end:value_end]
    grad_out = width_grads[:, value_end:out_end]
    grad_gate = width_grads[:, out_end:gate_end]
    grad_up = width_grads[:, gate_end:]
    return (
        jnp.stack(outputs)[:, None],
        jnp.stack(input_grads)[:, None],
        gain_one_total,
        grad_query,
        grad_key,
        grad_value,
        grad_out,
        gain_two_total,
        grad_gate,
        grad_up,
        hidden_grads,
    )


def solution(mesh):
    in_specs = (
        P(None, "narrow", "wide", None),
        P(None, "narrow", None),
        P(None, "narrow", None),
        P(),
        P("wide", None),
        P("wide", None),
        P("wide", None),
        P("wide", None),
        P(),
        P("wide", None),
        P("wide", None),
        P("wide", None),
        P(None, "narrow", "wide", None),
    )
    out_specs = (
        P(None, "narrow", "wide", None),
        P(None, "narrow", "wide", None),
        P(),
        P("wide", None),
        P("wide", None),
        P("wide", None),
        P("wide", None),
        P(),
        P("wide", None),
        P("wide", None),
        P("wide", None),
    )
    return jax.shard_map(shards, mesh=mesh, in_specs=in_specs, out_specs=out_specs, check_vma=False)
```

profile of v0, /device:TPU:0, one launch (start us, length us, event | category | flops | bytes accessed | tf_op | source)
XLA Modules:
  0.0 2147.2 jit_solution(4178803311741932770)
XLA Ops:
  53.3 22.6 %all-gather.28.cloned.1.call-done = bf16[2048,320]{0,1:T(8,128)(2,1)} async-done(((bf16[256,320]{0,1:T(8,128)(2,1)}), bf16[2048,320]{0,1:T(8,128)(2,1)}) %all-gather.28.cloned.1.call-update) | async-done | bytes 1310736 | tf_op jit(solution)/shard_map/all_gather | solution.py:158
  80.6 22.6 %all-gather.12.cloned.1.call-done = bf16[2048,320]{0,1:T(8,128)(2,1)} async-done(((bf16[256,320]{0,1:T(8,128)(2,1)}), bf16[2048,320]{0,1:T(8,128)(2,1)}) %all-gather.12.cloned.1.call-update) | async-done | bytes 1310736 | tf_op jit(solution)/shard_map/all_gather | solution.py:157
  107.7 22.5 %all-gather.16.cloned.1.call-done = bf16[2048,320]{0,1:T(8,128)(2,1)} async-done(((bf16[256,320]{0,1:T(8,128)(2,1)}), bf16[2048,320]{0,1:T(8,128)(2,1)}) %all-gather.16.cloned.1.call-update) | async-done | bytes 1310736 | tf_op jit(solution)/shard_map/all_gather | solution.py:158
  134.8 24.5 %all-gather.14.cloned.1.call-done = bf16[960,960]{1,0:T(8,128)(2,1)} async-done(((bf16[120,960]{1,0:T(8,128)(2,1)}), bf16[960,960]{1,0:T(8,128)(2,1)}) %all-gather.14.cloned.1.call-update) | async-done | bytes 1843216 | tf_op jit(solution)/shard_map/all_gather | solution.py:148
  169.1 229.7 %while.203 = (s32[]{:T(128)}, bf16[5,256,3,64]{1,3,2,0:T(8,128)(2,1)}, f32[5,3,256]{2,1,0:T(4,128)}, bf16[5,4,512,64]{2,3,1,0:T(8,128)(2,1)}, bf16[5,256,3,64]{1...) while((s32[]{:T(128)}, ...), condition=%wide.region_36.37_spmd.clone.clone, body=%wide.region_24.36_spmd.clone.sunk.clone | while | flops 124402944 | bytes 61126176 | solution.py:209
  402.2 199.7 %while.200 = (s32[]{:T(128)}, bf16[5,256,3,64]{1,3,2,0:T(8,128)(2,1)}, f32[5,3,256]{2,1,0:T(4,128)S(1)}, bf16[5,4,512,64]{2,3,1,0:T(8,128)(2,1)}, bf16[5,256,3,6...) while((s32[]{:T(128)}, ...), condition=%wide.region_17.18_spmd.clone.clone, body=%wide.region_5.17_spmd.clone.sunk.clone | while | flops 124402944 | bytes 61128224 | solution.py:209
  654.0 492.7 %while.211 = (s32[]{:T(128)}, f32[5,256,3,64]{1,3,2,0:T(8,128)}, bf16[5,4,512,64]{2,3,1,0:T(8,128)(2,1)}, bf16[5,4,512,64]{2,3,1,0:T(8,128)(2,1)}, bf16[5,4,512,...) while((s32[]{:T(128)}, f32[5,256,3,64]{1,3,2,0:T(8,128)}, ...), condition=%wide.region_74.75_spmd.clone.clone, body=%wide.region_59.74_spmd.clone.sunk.clone | while | flops 275578112 | bytes 122528672 | solution.py:312
  718.5 28.7 %while.210 = (s32[]{:T(128)}, f32[4,256,3,64]{1,3,2,0:T(8,128)}, f32[4,512,64]{1,2,0:T(8,128)}, bf16[4,512,64]{1,2,0:T(8,128)(2,1)}, pred[4]{0:T(512)(128)(4,1)}...) while((s32[]{:T(128)}, f32[4,256,3,64]{1,3,2,0:T(8,128)}, ...), condition=%wide.region_72.72_spmd, body=%wide.region_69.71_spmd.sunk | while | flops 150994944 | bytes 4000460 | solution.py:303
  817.0 28.7 %while.210 = (s32[]{:T(128)}, f32[4,256,3,64]{1,3,2,0:T(8,128)}, f32[4,512,64]{1,2,0:T(8,128)}, bf16[4,512,64]{1,2,0:T(8,128)(2,1)}, pred[4]{0:T(512)(128)(4,1)}...) while((s32[]{:T(128)}, f32[4,256,3,64]{1,3,2,0:T(8,128)}, ...), condition=%wide.region_72.72_spmd, body=%wide.region_69.71_spmd.sunk | while | flops 150994944 | bytes 4000460 | solution.py:303
  915.5 28.7 %while.210 = (s32[]{:T(128)}, f32[4,256,3,64]{1,3,2,0:T(8,128)}, f32[4,512,64]{1,2,0:T(8,128)}, bf16[4,512,64]{1,2,0:T(8,128)(2,1)}, pred[4]{0:T(512)(128)(4,1)}...) while((s32[]{:T(128)}, f32[4,256,3,64]{1,3,2,0:T(8,128)}, ...), condition=%wide.region_72.72_spmd, body=%wide.region_69.71_spmd.sunk | while | flops 150994944 | bytes 4000460 | solution.py:303
  1014.0 28.7 %while.210 = (s32[]{:T(128)}, f32[4,256,3,64]{1,3,2,0:T(8,128)}, f32[4,512,64]{1,2,0:T(8,128)}, bf16[4,512,64]{1,2,0:T(8,128)(2,1)}, pred[4]{0:T(512)(128)(4,1)}...) while((s32[]{:T(128)}, f32[4,256,3,64]{1,3,2,0:T(8,128)}, ...), condition=%wide.region_72.72_spmd, body=%wide.region_69.71_spmd.sunk | while | flops 150994944 | bytes 4000460 | solution.py:303
  1112.5 28.7 %while.210 = (s32[]{:T(128)}, f32[4,256,3,64]{1,3,2,0:T(8,128)}, f32[4,512,64]{1,2,0:T(8,128)}, bf16[4,512,64]{1,2,0:T(8,128)(2,1)}, pred[4]{0:T(512)(128)(4,1)}...) while((s32[]{:T(128)}, f32[4,256,3,64]{1,3,2,0:T(8,128)}, ...), condition=%wide.region_72.72_spmd, body=%wide.region_69.71_spmd.sunk | while | flops 150994944 | bytes 4000460 | solution.py:303
  1158.9 451.3 %while.207 = (s32[]{:T(128)}, f32[5,256,3,64]{1,3,2,0:T(8,128)}, bf16[5,4,512,64]{2,3,1,0:T(8,128)(2,1)}, bf16[5,4,512,64]{2,3,1,0:T(8,128)(2,1)}, bf16[5,4,512,...) while((s32[]{:T(128)}, f32[5,256,3,64]{1,3,2,0:T(8,128)}, ...), condition=%wide.region_54.55_spmd.clone.clone, body=%wide.region_39.54_spmd.clone.sunk.clone | while | flops 275578112 | bytes 122528680 | solution.py:312
  1218.0 26.1 %while.206 = (s32[]{:T(128)}, f32[4,256,3,64]{1,3,2,0:T(8,128)}, f32[4,512,64]{1,2,0:T(8,128)}, bf16[4,512,64]{1,2,0:T(8,128)(2,1)}, pred[4]{0:T(512)(128)(4,1)S...) while((s32[]{:T(128)}, f32[4,256,3,64]{1,3,2,0:T(8,128)}, ...), condition=%wide.region_52.52_spmd, body=%wide.region_49.51_spmd.sunk | while | flops 150994944 | bytes 4000460 | solution.py:303
  1308.2 26.1 %while.206 = (s32[]{:T(128)}, f32[4,256,3,64]{1,3,2,0:T(8,128)}, f32[4,512,64]{1,2,0:T(8,128)}, bf16[4,512,64]{1,2,0:T(8,128)(2,1)}, pred[4]{0:T(512)(128)(4,1)S...) while((s32[]{:T(128)}, f32[4,256,3,64]{1,3,2,0:T(8,128)}, ...), condition=%wide.region_52.52_spmd, body=%wide.region_49.51_spmd.sunk | while | flops 150994944 | bytes 4000460 | solution.py:303
  1398.4 26.1 %while.206 = (s32[]{:T(128)}, f32[4,256,3,64]{1,3,2,0:T(8,128)}, f32[4,512,64]{1,2,0:T(8,128)}, bf16[4,512,64]{1,2,0:T(8,128)(2,1)}, pred[4]{0:T(512)(128)(4,1)S...) while((s32[]{:T(128)}, f32[4,256,3,64]{1,3,2,0:T(8,128)}, ...), condition=%wide.region_52.52_spmd, body=%wide.region_49.51_spmd.sunk | while | flops 150994944 | bytes 4000460 | solution.py:303
  1488.5 26.1 %while.206 = (s32[]{:T(128)}, f32[4,256,3,64]{1,3,2,0:T(8,128)}, f32[4,512,64]{1,2,0:T(8,128)}, bf16[4,512,64]{1,2,0:T(8,128)(2,1)}, pred[4]{0:T(512)(128)(4,1)S...) while((s32[]{:T(128)}, f32[4,256,3,64]{1,3,2,0:T(8,128)}, ...), condition=%wide.region_52.52_spmd, body=%wide.region_49.51_spmd.sunk | while | flops 150994944 | bytes 4000460 | solution.py:303
  1578.7 26.1 %while.206 = (s32[]{:T(128)}, f32[4,256,3,64]{1,3,2,0:T(8,128)}, f32[4,512,64]{1,2,0:T(8,128)}, bf16[4,512,64]{1,2,0:T(8,128)(2,1)}, pred[4]{0:T(512)(128)(4,1)S...) while((s32[]{:T(128)}, f32[4,256,3,64]{1,3,2,0:T(8,128)}, ...), condition=%wide.region_52.52_spmd, body=%wide.region_49.51_spmd.sunk | while | flops 150994944 | bytes 4000460 | solution.py:303
  1696.0 22.5 %concatenate.62 = bf16[960,7680]{1,0:T(8,128)(2,1)} concatenate(bf16[960,1600]{1,0:T(8,128)(2,1)} %convolution_convert_fusion.5, bf16[960,960]{1,0:T(8,128)(2,1)} %convolution_convert_fusion.7, bf16[960,5120]{1,0:T(8,128)(2,1)} %convolution_convert_fusion.1), dimensions={1} | concatenate | bytes 29491200 | tf_op jit(solution)/shard_map/concatenate | solution.py:80
  1751.9 60.2 %reduce-scatter.21.cloned.1.call-done = bf16[320,960]{1,0:T(8,128)(2,1)} async-done(((bf16[2560,960]{1,0:T(8,128)(2,1)}), bf16[320,960]{1,0:T(8,128)(2,1)}) %reduce-scatter.21.cloned.1.call-update) | async-done | bytes 614416 | tf_op jit(solution)/shard_map/reduce_scatter | solution.py:86
  1814.5 104.9 %reduce-scatter.19.cloned.1.call-done = bf16[120,7680]{1,0:T(8,128)(2,1)} async-done(((bf16[960,7680]{1,0:T(8,128)(2,1)}), bf16[120,7680]{1,0:T(8,128)(2,1)}) %reduce-scatter.19.cloned.1.call-update) | async-done | bytes 1843216 | tf_op jit(solution)/shard_map/reduce_scatter | solution.py:79
  1919.4 107.3 %reduce-scatter.17.cloned.1.call-done = bf16[120,7680]{1,0:T(8,128)(2,1)} async-done(((bf16[960,7680]{1,0:T(8,128)(2,1)}), bf16[120,7680]{1,0:T(8,128)(2,1)}) %reduce-scatter.17.cloned.1.call-update) | async-done | bytes 1843216 | tf_op jit(solution)/shard_map/reduce_scatter | solution.py:79
  2039.8 41.9 %all-reduce.8 = (f32[960]{0:T(1024)}, f32[960]{0:T(1024)}) all-reduce(f32[960]{0:T(1024)S(1)} %add.349, f32[960]{0:T(1024)S(1)} %add.351), channel_id=1, replica_groups=mesh['wide'=8,'narrow'=4] {'wide','narrow'}, use_global_device_ids=true, to_apply=%region_80.81 | all-reduce | flops 1920 | bytes 15360 | tf_op jit(solution)/shard_map/psum | solution.py:365
  2085.2 47.0 %all-reduce.12.cloned.1.call-done = (bf16[120,7680]{1,0:T(8,128)(2,1)}, bf16[320,960]{1,0:T(8,128)(2,1)}) async-done(((bf16[120,7680]{1,0:T(8,128)(2,1)}, bf16[320,960]{1,0:T(8,128)(2,1)}), (bf16[120,7680]{1,0:T(8,128)(2,1)}, bf16[320,960]{1,0:T(8,128)(2,1)})) %all-reduce.12.cloned.1.call-update) | async-done | bytes 2457616 | tf_op jit(solution)/shard_map/psum | solution.py:362
  (1803 shorter events, 2502.2 us)
Async XLA Ops:
  7.2 41.5 %all-gather.26.cloned.1.call-start = ((), (), s32[]{:S(2)}) async-start(), calls=%async_computation.15 | async-start | bytes 1474560 | tf_op jit(solution)/shard_map/all_gather | solution.py:157
  20.6 142.6 %copy-start.95 = (f32[256]{0:T(256)}, f32[256]{0:T(256)S(1)}, u32[]{:S(2)}) copy-start(f32[256]{0:T(256)S(1)} %fusion.174) | copy-start | bytes 3076
  22.8 144.7 %copy-start.53 = (f32[256,64]{0,1:T(8,128)}, f32[256,64]{0,1:T(8,128)S(1)}, u32[]{:S(2)}) copy-start(f32[256,64]{0,1:T(8,128)S(1)} %get-tuple-element.1638) | copy-start | bytes 196612
  22.8 144.7 %copy-start.57 = (f32[256,64]{0,1:T(8,128)}, f32[256,64]{0,1:T(8,128)S(1)}, u32[]{:S(2)}) copy-start(f32[256,64]{0,1:T(8,128)S(1)} %get-tuple-element.1637) | copy-start | bytes 196612
  23.6 52.4 %all-gather.28.cloned.1.call-start = ((), (), s32[]{:S(2)}) async-start(), calls=%async_computation.16 | async-start | bytes 1474560 | tf_op jit(solution)/shard_map/all_gather | solution.py:158
  35.5 67.6 %all-gather.12.cloned.1.call-start = ((), (), s32[]{:S(2)}) async-start(), calls=%async_computation.8 | async-start | bytes 1474560 | tf_op jit(solution)/shard_map/all_gather | solution.py:157
  35.8 129.9 %copy-start.97 = (f32[256]{0:T(256)}, f32[256]{0:T(256)S(1)}, u32[]{:S(2)}) copy-start(f32[256]{0:T(256)S(1)} %fusion.172) | copy-start | bytes 3076
  37.0 93.2 %all-gather.16.cloned.1.call-start = ((), (), s32[]{:S(2)}) async-start(), calls=%async_computation.10 | async-start | bytes 1474560 | tf_op jit(solution)/shard_map/all_gather | solution.py:158
  38.2 121.1 %all-gather.14.cloned.1.call-start = ((), (), s32[]{:S(2)}) async-start(), calls=%async_computation.9 | async-start | bytes 2211840 | tf_op jit(solution)/shard_map/all_gather | solution.py:148
  38.8 563.2 %all-gather.18.cloned.1.call-start = ((), (), s32[]{:S(2)}) async-start(), calls=%async_computation.11 | async-start | bytes 2211840 | tf_op jit(solution)/shard_map/all_gather | solution.py:217
  39.4 567.7 %all-gather.20.cloned.1.call-start = ((), (), s32[]{:S(2)}) async-start(), calls=%async_computation.12 | async-start | bytes 5529600 | tf_op jit(solution)/shard_map/all_gather | solution.py:223
  40.1 572.5 %all-gather.22.cloned.1.call-start = ((), (), s32[]{:S(2)}) async-start(), calls=%async_computation.13 | async-start | bytes 5529600 | tf_op jit(solution)/shard_map/all_gather | solution.py:224
  40.9 577.2 %all-gather.24.cloned.1.call-start = ((), (), s32[]{:S(2)}) async-start(), calls=%async_computation.14 | async-start | bytes 5898240 | tf_op jit(solution)/shard_map/all_gather | solution.py:228
  41.6 1595.0 %reduce-scatter.13.cloned.1.call-start = ((), (), s32[]{:S(2)}) async-start(), calls=%async_computation.19 | async-start | bytes 1474560 | tf_op jit(solution)/shard_map/reduce_scatter | solution.py:320
  1150.5 488.1 %reduce-scatter.15.cloned.1.call-start = ((), (), s32[]{:S(2)}) async-start(), calls=%async_computation.20 | async-start | bytes 1474560 | tf_op jit(solution)/shard_map/reduce_scatter | solution.py:323
  1153.1 521.6 %reduce-scatter.9.cloned.1.call-start = ((), (), s32[]{:S(2)}) async-start(), calls=%async_computation.17 | async-start | bytes 1474560 | tf_op jit(solution)/shard_map/reduce_scatter | solution.py:320
  1614.1 78.0 %reduce-scatter.11.cloned.1.call-start = ((), (), s32[]{:S(2)}) async-start(), calls=%async_computation.18 | async-start | bytes 1474560 | tf_op jit(solution)/shard_map/reduce_scatter | solution.py:323
  1616.8 135.1 %reduce-scatter.23.cloned.1.call-start = ((), (), s32[]{:S(2)}) async-start(), calls=%async_computation.24 | async-start | bytes 5898240 | tf_op jit(solution)/shard_map/reduce_scatter | solution.py:86
  1621.4 190.8 %reduce-scatter.21.cloned.1.call-start = ((), (), s32[]{:S(2)}) async-start(), calls=%async_computation.23 | async-start | bytes 5898240 | tf_op jit(solution)/shard_map/reduce_scatter | solution.py:86
  1626.6 292.8 %reduce-scatter.19.cloned.1.call-start = ((), (), s32[]{:S(2)}) async-start(), calls=%async_computation.22 | async-start | bytes 16588800 | tf_op jit(solution)/shard_map/reduce_scatter | solution.py:79
  1664.4 362.4 %reduce-scatter.17.cloned.1.call-start = ((), (), s32[]{:S(2)}) async-start(), calls=%async_computation.21 | async-start | bytes 16588800 | tf_op jit(solution)/shard_map/reduce_scatter | solution.py:79
  1718.6 413.6 %all-reduce.12.cloned.1.call-start = ((), (), s32[]{:S(2)}) async-start(), calls=%async_computation.25 | async-start | bytes 4997120 | tf_op jit(solution)/shard_map/psum | solution.py:362
  1814.5 216.0 %copy-start.73 = (bf16[256,15,64]{0,2,1:T(8,128)(2,1)S(1)}, bf16[256,15,64]{0,2,1:T(8,128)(2,1)}, u32[]{:S(2)}) copy-start(bf16[256,15,64]{0,2,1:T(8,128)(2,1)} %copy-done.72) | copy-start | bytes 1474564
  2037.8 43.9 %copy-start.91 = (f32[256]{0:T(256)S(1)}, f32[256]{0:T(256)}, u32[]{:S(2)}) copy-start(f32[256]{0:T(256)} %copy-done.90) | copy-start | bytes 3076
  (132 other events, 759.5 us)
Sparse Core Ops, SparseCore 0:
  23.7 25.0 all-gather.25
  51.2 24.7 all-gather.27
  78.4 24.7 all-gather.11
  105.5 24.7 all-gather.15
  131.9 27.3 all-gather.13
  161.1 27.3 all-gather.17
  190.3 39.7 all-gather.19
  232.0 39.7 all-gather.21
  273.7 41.1 all-gather.23
  1150.6 37.2 reduce-scatter.12
  1191.2 37.3 reduce-scatter.14
  1614.2 37.2 reduce-scatter.8
  1654.7 37.3 reduce-scatter.10
  1695.3 56.5 reduce-scatter.22
  1755.5 56.5 reduce-scatter.20
  1815.5 103.8 reduce-scatter.18
  1922.8 103.9 reduce-scatter.16
  2030.6 101.5 all-reduce.11
where the time goes:
time: 2170 us; the launch traced here: 2150 us
  local copies, waits for them, and re-layouts  776 us (36%)
  waiting for transfers between devices  453 us (21%)
  matrix products  422 us (19%)
  other arithmetic  282 us (13%)
  loops' own time  133 us (6%)
  blocking collectives  63.7 us (3%)
    reduce_scatter x2, waiting for transfers between devices, weight_terms(): lax.psum_scatter(jnp.concatenate(products, axis=1).astype(jnp.bfloat16),...  212 us
    dynamic_update_slice x240, local copies, waits for them, and re-layouts, scores_of(): lax.map(scores_one_block, (group_keys, live_blocks)) * score_scale  211 us
    dynamic_slice x200, local copies, waits for them, and re-layouts, scores_of(): lax.map(scores_one_block, (group_keys, live_blocks)) * score_scale  184 us
    reduce_scatter x2, waiting for transfers between devices, weight_terms(): lax.psum_scatter(lax.dot_general(columns, grad_out_rows, (((0,), (0,)), (...  81.5 us
    another operation x28, local copies, waits for them, and re-layouts  76.6 us
    dot_general x80, matrix products, scores_one_block(): jnp.einsum('qgd,kd->gqk', group_query, key_part, preferred_element_type=j...  68.4 us
    squeeze x40, local copies, waits for them, and re-layouts, shards(): lax.map(forward_group, (query_groups, key_groups, value_groups))  60.8 us
    reduce_sum x10, other arithmetic, backward_group(): inner_sum = jnp.sum(soft_full * grad_weights, axis=(0, 3), keepdims=True)  59.7 us
  transfers between devices with their start and end apart: 18, of which 11 were waited for; matrix products, arithmetic and copies ran while one was open for 44% of the time, Pallas kernels for 0%

commit v1 on v0

v1 whole, which is shorter than its diff:
```python
import functools

import jax
import jax.numpy as jnp
from jax import lax
from jax.experimental import pallas as pl
from jax.experimental.pallas import tpu as pltpu
from jax.sharding import PartitionSpec as P

HDIM = 64
BLOCK = 128
EPS = 1e-05
ROPE_BASE = 100000.0
NEG_FILL = -1e30
F32 = jnp.float32
BF16 = jnp.bfloat16
VMEM_LIMIT = 56 * 1024 * 1024


def dot(a, b, ca, cb):
    return lax.dot_general(a, b, (((ca,), (cb,)), ((), ())), preferred_element_type=F32)


def live_mask(qpos, start, p):
    kpos = p * BLOCK + lax.broadcasted_iota(jnp.int32, (BLOCK, BLOCK), 0)
    return (kpos <= qpos) & (kpos >= start)


def fwd_kernel(groups, share, info, kvat, q_ref, start_ref, kv_ref, o_ref, lse_ref, qs, m_s, l_s, acc):
    i = pl.program_id(0)
    lo, b = info[0, i], info[1, i]
    lanes = share * BLOCK
    for g in range(groups):
        for h in range(share):
            at = (g * share + h) * HDIM
            qs[g, :, h * BLOCK : (h + 1) * BLOCK] = q_ref[at : at + HDIM, :]
    m_s[...] = jnp.full_like(m_s, NEG_FILL)
    l_s[...] = jnp.zeros_like(l_s)
    acc[...] = jnp.zeros_like(acc)
    qpos = b * BLOCK + lax.broadcasted_iota(jnp.int32, (1, BLOCK), 1)
    start = start_ref[...]

    def step(t, carry):
        p = b - t
        at = kvat[p]
        ok = live_mask(qpos, start, p)
        ok = jnp.concatenate([ok] * share, axis=1)
        for g in range(groups):
            k_t = kv_ref[at, g * HDIM : (g + 1) * HDIM, :]
            v_t = kv_ref[at, (groups + g) * HDIM : (groups + g + 1) * HDIM, :]
            s = jnp.where(ok, dot(k_t, qs[g], 0, 0), NEG_FILL)
            m_old = m_s[g]
            m_new = jnp.maximum(m_old, jnp.max(s, axis=0, keepdims=True))
            w = jnp.exp(s - m_new)
            alpha = jnp.exp(m_old - m_new)
            l_s[g] = l_s[g] * alpha + jnp.sum(w, axis=0, keepdims=True)
            acc[g] = acc[g] * alpha + dot(v_t, w.astype(BF16), 1, 0)
            m_s[g] = m_new
        return carry

    lax.fori_loop(0, b - lo + 1, step, 0)
    for g in range(groups):
        total = l_s[g]
        out = (acc[g] / total).astype(BF16)
        for h in range(share):
            at = (g * share + h) * HDIM
            o_ref[at : at + HDIM, :] = out[:, h * BLOCK : (h + 1) * BLOCK]
        lse_ref[0, g : g + 1, :] = m_s[g] + jnp.log(total)


def attention_fwd(info, kvat, q_t, start, kv, mb):
    width, tokens = q_t.shape
    nb, kvw, _ = kv.shape
    groups = kvw // HDIM // 2
    share = width // HDIM // groups
    nq = info.shape[1]
    lanes = share * BLOCK
    return pl.pallas_call(
        functools.partial(fwd_kernel, groups, share),
        grid_spec=pltpu.PrefetchScalarGridSpec(
            num_scalar_prefetch=2,
            grid=(nq,),
            in_specs=[
                pl.BlockSpec((width, BLOCK), lambda i, *_: (0, mb * nq + i)),
                pl.BlockSpec((1, BLOCK), lambda i, *_: (0, mb * nq + i)),
                pl.BlockSpec((nb, kvw, BLOCK), lambda i, *_: (0, 0, 0)),
            ],
            out_specs=[
                pl.BlockSpec((width, BLOCK), lambda i, *_: (0, i)),
                pl.BlockSpec((1, groups, lanes), lambda i, *_: (i, 0, 0)),
            ],
            scratch_shapes=[
                pltpu.VMEM((groups, HDIM, lanes), BF16),
                pltpu.VMEM((groups, 1, lanes), F32),
                pltpu.VMEM((groups, 1, lanes), F32),
                pltpu.VMEM((groups, HDIM, lanes), F32),
            ],
        ),
        out_shape=[
            jax.ShapeDtypeStruct((width, nq * BLOCK), BF16),
            jax.ShapeDtypeStruct((nq, groups, lanes), F32),
        ],
        compiler_params=pltpu.CompilerParams(vmem_limit_bytes=VMEM_LIMIT),
        cost_estimate=pl.CostEstimate(
            flops=int(5e9), bytes_accessed=int(4e6), transcendentals=int(4e6)
        ),
        name="attention_fwd",
    )(info, kvat, q_t, start, kv)


def bwd_kernel(
    groups, share, info, kvat, q_ref, do_ref, o_ref, lse_ref, start_ref, cos_ref, sin_ref, kv_ref,
    dq_ref, own_ref, send_ref, qs, dos, delta, dq, dkv,
):
    i = pl.program_id(0)
    lo, b = info[0, i], info[1, i]

    @pl.when(i == 0)
    def _():
        dkv[...] = jnp.zeros_like(dkv)

    for g in range(groups):
        for h in range(share):
            at = (g * share + h) * HDIM
            cols = slice(h * BLOCK, (h + 1) * BLOCK)
            d_out = do_ref[at : at + HDIM, :]
            qs[g, :, cols] = q_ref[at : at + HDIM, :]
            dos[g, :, cols] = d_out
            delta[g, :, cols] = jnp.sum(
                d_out.astype(F32) * o_ref[at : at + HDIM, :].astype(F32), axis=0, keepdims=True
            )
    dq[...] = jnp.zeros_like(dq)
    qpos = b * BLOCK + lax.broadcasted_iota(jnp.int32, (1, BLOCK), 1)
    start = start_ref[...]

    def step(t, carry):
        p = b - t
        at = kvat[p]
        ok = live_mask(qpos, start, p)
        ok = jnp.concatenate([ok] * share, axis=1)
        for g in range(groups):
            krows = slice(g * HDIM, (g + 1) * HDIM)
            vrows = slice((groups + g) * HDIM, (groups + g + 1) * HDIM)
            k_t = kv_ref[at, krows, :]
            v_t = kv_ref[at, vrows, :]
            s = jnp.where(ok, dot(k_t, qs[g], 0, 0), NEG_FILL)
            w = jnp.exp(s - lse_ref[0, g : g + 1, :])
            dw = dot(v_t, dos[g], 0, 0)
            ds = (w * (dw - delta[g])).astype(BF16)
            dq[g] += dot(k_t, ds, 1, 0)
            dkv[at, krows, :] += dot(qs[g], ds, 1, 1)
            dkv[at, vrows, :] += dot(dos[g], w.astype(BF16), 1, 1)
        return carry

    lax.fori_loop(0, b - lo + 1, step, 0)
    cos, sin = cos_ref[...], sin_ref[...]
    half = HDIM // 2
    for g in range(groups):
        for h in range(share):
            at = (g * share + h) * HDIM
            one = dq[g, :half, h * BLOCK : (h + 1) * BLOCK] * HDIM**-0.5
            two = dq[g, half:, h * BLOCK : (h + 1) * BLOCK] * HDIM**-0.5
            dq_ref[at : at + half, :] = (one * cos + two * sin).astype(BF16)
            dq_ref[at + half : at + HDIM, :] = (two * cos - one * sin).astype(BF16)

    @pl.when(i == pl.num_programs(0) - 1)
    def _():
        n = own_ref.shape[0]
        own_ref[...] = dkv[:n].astype(BF16)
        send_ref[...] = dkv[n:].astype(BF16)


def attention_bwd(info, kvat, q_t, do_t, o_t, lse, start, cos_t, sin_t, kv, mb):
    width = q_t.shape[0]
    nb, kvw, _ = kv.shape
    groups = kvw // HDIM // 2
    share = width // HDIM // groups
    nq = info.shape[1]
    lanes = share * BLOCK
    tok = lambda rows: pl.BlockSpec((rows, BLOCK), lambda i, *_: (0, mb * nq + i))
    return pl.pallas_call(
        functools.partial(bwd_kernel, groups, share),
        grid_spec=pltpu.PrefetchScalarGridSpec(
            num_scalar_prefetch=2,
            grid=(nq,),
            in_specs=[
                tok(width),
                tok(width),
                tok(width),
                pl.BlockSpec((1, groups, lanes), lambda i, *_: (i, 0, 0)),
                tok(1),
                tok(HDIM // 2),
                tok(HDIM // 2),
                pl.BlockSpec((nb, kvw, BLOCK), lambda i, *_: (0, 0, 0)),
            ],
            out_specs=[
                pl.BlockSpec((width, BLOCK), lambda i, *_: (0, i)),
                pl.BlockSpec((nb // 2, kvw, BLOCK), lambda i, *_: (0, 0, 0)),
                pl.BlockSpec((nb // 2, kvw, BLOCK), lambda i, *_: (0, 0, 0)),
            ],
            scratch_shapes=[
                pltpu.VMEM((groups, HDIM, lanes), BF16),
                pltpu.VMEM((groups, HDIM, lanes), BF16),
                pltpu.VMEM((groups, 1, lanes), F32),
                pltpu.VMEM((groups, HDIM, lanes), F32),
                pltpu.VMEM((nb, kvw, BLOCK), F32),
            ],
        ),
        out_shape=[
            jax.ShapeDtypeStruct((width, nq * BLOCK), BF16),
            jax.ShapeDtypeStruct((nb // 2, kvw, BLOCK), BF16),
            jax.ShapeDtypeStruct((nb // 2, kvw, BLOCK), BF16),
        ],
        compiler_params=pltpu.CompilerParams(vmem_limit_bytes=VMEM_LIMIT),
        cost_estimate=pl.CostEstimate(
            flops=int(1e10), bytes_accessed=int(8e6), transcendentals=int(4e6)
        ),
        name="attention_bwd",
    )(info, kvat, q_t, do_t, o_t, lse, start, cos_t, sin_t, kv)


CORE, ALONG_X, ALONG_Y = 1, 2, 4


class Wide:
    def __init__(self, size):
        self.size = size
        self.at = lax.axis_index("wide")
        self.cube = size == 8

    def swap(self, a, bit):
        return lax.ppermute(a, "wide", [(i, i ^ bit) for i in range(self.size)])

    def pieces(self, own, first):
        other = ALONG_X + ALONG_Y - first
        got = {0: own, ALONG_X: self.swap(own, ALONG_X), ALONG_Y: self.swap(own, ALONG_Y)}
        got[ALONG_X + ALONG_Y] = self.swap(got[other], first)
        for m in list(got):
            got[m + CORE] = self.swap(got[m], CORE)
        return got

    def rows(self, own, first):
        if not self.cube:
            return lax.all_gather(own, "wide", axis=0, tiled=True)
        rows, cols = own.shape
        whole = jnp.zeros((self.size, rows, cols), own.dtype)
        for m, piece in self.pieces(own, first).items():
            whole = lax.dynamic_update_slice(whole, piece[None], (self.at ^ m, 0, 0))
        return whole.reshape(self.size * rows, cols)

    def order(self, first):
        other = ALONG_X + ALONG_Y - first
        return [
            c * CORE + a * first + b * other for c in range(2) for a in range(2) for b in range(2)
        ]

    def ordered_rows(self, src_t, first):
        if not self.cube:
            return src_t
        each = src_t.shape[0] // self.size
        return jnp.concatenate(
            [
                lax.dynamic_slice_in_dim(src_t, (self.at ^ m) * each, each)
                for m in self.order(first)
            ]
        )

    def halve(self, own, bit):
        half = own.shape[0] // 2
        got = self.swap(own[half:], bit)
        return (own[:half].astype(F32) + got.astype(F32)).astype(BF16)

    def scatter_chips(self, own, first):
        return self.halve(self.halve(own, first), ALONG_X + ALONG_Y - first)

    def weight_sum(self, src_ord, target, target_dim, first):
        if not self.cube:
            return lax.psum_scatter(
                dot(src_ord, target, 1, target_dim).astype(BF16), "wide", scatter_dimension=0, tiled=True
            )
        half = src_ord.shape[0] // 2
        got = self.swap(dot(src_ord[half:], target, 1, target_dim).astype(BF16), CORE)
        own = (dot(src_ord[:half], target, 1, target_dim) + got.astype(F32)).astype(BF16)
        return self.scatter_chips(own, first)


def row_sum(part, size):
    if size != 4:
        return lax.psum(part, "narrow").astype(F32)
    add = lambda a, b: (a.astype(F32) + b.astype(F32)).astype(BF16)
    part = add(part, lax.ppermute(part, "narrow", [(0, 1), (3, 2)]))
    part = add(part, lax.ppermute(part, "narrow", [(1, 2), (2, 1)]))
    back = lax.ppermute(part, "narrow", [(1, 0), (2, 3)])
    at = lax.axis_index("narrow")
    return jnp.where((at == 1) | (at == 2), part, back).astype(F32)


def turn(v, cos, sin):
    heads = v.reshape(-1, 2, HDIM // 2, v.shape[1])
    one, two = heads[:, 0], heads[:, 1]
    return jnp.stack([one * cos - two * sin, two * cos + one * sin], axis=1).reshape(v.shape)


def turn_back(v, cos, sin):
    return turn(v, cos, -sin)


def shards(sizes, tokens, lengths, block_plan, attn_gain, w_query, w_key, w_value, w_out, ffn_gain,
           w_gate, w_up, w_down, cotangent):
    wide = Wide(sizes["wide"])
    n = wide.size
    micro, _, slots, width = tokens.shape
    total = micro * slots
    kd = w_key.shape[1]
    ff = w_gate.shape[1]
    nq = slots // BLOCK
    nb = nq * n

    plan = block_plan[:, 0]
    sizes_of = lengths[:, 0]
    docs = sizes_of.shape[1]
    upto = jnp.arange(docs)[:, None] >= jnp.arange(docs)[None, :]
    ends = jnp.sum(jnp.where(upto[None], sizes_of[:, None, :], 0), axis=2)
    own_plan = lax.dynamic_slice_in_dim(plan, wide.at * nq, nq, axis=1)
    position = own_plan[:, :, None] * BLOCK + jnp.arange(BLOCK, dtype=jnp.int32)
    start = jnp.sum(
        jnp.where(position[..., None] >= ends[:, None, None, :], sizes_of[:, None, None, :], 0), axis=3
    )
    info = jnp.stack([start[:, :, 0] // BLOCK, own_plan], axis=1)
    slot_block = jnp.arange(nb, dtype=jnp.int32)
    where_is = jnp.sum(
        jnp.where(plan[:, None, :] == slot_block[None, :, None], slot_block[None, None, :], 0), axis=2
    )
    start = start.reshape(1, total)
    local = position.reshape(1, total) - start
    frequency = ROPE_BASE ** (-2.0 * jnp.arange(HDIM // 2, dtype=F32) / HDIM)
    angles = frequency[:, None] * local.astype(F32)
    cos, sin = jnp.cos(angles), jnp.sin(angles)

    if wide.cube:
        kv_order = wide.order(ALONG_X)
        rank = sum(
            jnp.where((where_is // nq) ^ wide.at == m, r, 0) for r, m in enumerate(kv_order)
        )
        kvat = rank * nq + where_is % nq
    else:
        kvat = where_is

    x = tokens.reshape(total, width).astype(F32)
    ct = cotangent.reshape(total, width)

    g_query = wide.rows(w_query, ALONG_X)
    g_kv = wide.rows(jnp.concatenate([w_key, w_value], axis=1), ALONG_Y)
    g_out = wide.rows(w_out, ALONG_Y)
    g_gate = wide.rows(w_gate, ALONG_X)
    g_up = wide.rows(w_up, ALONG_Y)
    g_down = wide.rows(w_down, ALONG_X)

    rr1 = lax.rsqrt(jnp.mean(x * x, axis=1, keepdims=True) + EPS)
    xn = (x * rr1 * attn_gain).astype(BF16)
    kv_t = dot(g_kv, xn, 0, 1)
    key_t = turn(kv_t[:kd], cos, sin).astype(BF16)
    value_t = kv_t[kd:].astype(BF16)
    own_kv = jnp.concatenate([key_t, value_t]).reshape(2 * kd, micro, nq, BLOCK).transpose(1, 2, 0, 3)
    q_t = (turn(dot(g_query, xn, 0, 1), cos, sin).astype(BF16) * HDIM**-0.5).astype(BF16)

    kvs, outs, lses = [], [], []
    for mb in range(micro):
        if wide.cube:
            got = wide.pieces(own_kv[mb], ALONG_X)
            kv = jnp.concatenate([got[m] for m in kv_order])
        else:
            kv = lax.all_gather(own_kv[mb], "wide", axis=0, tiled=True)
        o_t, lse = attention_fwd(info[mb], kvat[mb], q_t, start, kv, mb)
        kvs.append(kv)
        outs.append(o_t)
        lses.append(lse)
    att_t = jnp.concatenate(outs, axis=1)

    res = x + dot(att_t, g_out, 0, 0)
    rr2 = lax.rsqrt(jnp.mean(res * res, axis=1, keepdims=True) + EPS)
    hn = (res * rr2 * ffn_gain).astype(BF16)
    gate = dot(g_gate, hn, 0, 1)
    up = dot(g_up, hn, 0, 1)
    sg = 1.0 / (1.0 + jnp.exp(-gate))
    hidden = (gate * sg * up).astype(BF16)
    out = (res + dot(hidden, g_down, 0, 0)).astype(BF16)

    first_down, first_out, first_q, first_kv = ALONG_X, ALONG_Y, ALONG_X, ALONG_Y
    s_down = wide.weight_sum(wide.ordered_rows(hidden, first_down), ct, 0, first_down)

    d_hidden = dot(g_down, ct, 1, 1)
    d_gate = (d_hidden * up * sg * (1.0 + gate * (1.0 - sg))).astype(BF16)
    d_up = (d_hidden * gate * sg).astype(BF16)
    hn_t = hn.T
    s_gate = wide.weight_sum(wide.ordered_rows(hn_t, ALONG_X), d_gate, 1, ALONG_X)
    s_up = wide.weight_sum(wide.ordered_rows(hn_t, ALONG_Y), d_up, 1, ALONG_Y)
    d_hn = dot(d_gate, g_gate, 0, 1) + dot(d_up, g_up, 0, 1)
    u = d_hn * ffn_gain
    d_res = (
        ct.astype(F32) + rr2 * u - res * rr2**3 * jnp.mean(u * res, axis=1, keepdims=True)
    )
    gain_two = jnp.sum(d_hn * res * rr2, axis=0)
    d_attn = d_res.astype(BF16)
    do_t = dot(g_out, d_attn, 1, 1).astype(BF16)
    s_out = wide.weight_sum(wide.ordered_rows(att_t, first_out), d_attn, 0, first_out)

    dqs, dkvs = [], []
    for mb in range(micro):
        dq_t, own, send = attention_bwd(
            info[mb], kvat[mb], q_t, do_t, outs[mb] if micro == 1 else att_t, lses[mb], start, cos, sin,
            kvs[mb], mb,
        )
        dqs.append(dq_t)
        if wide.cube:
            got = wide.swap(send, CORE)
            dkv = wide.scatter_chips((own.astype(F32) + got.astype(F32)).astype(BF16), ALONG_X)
        else:
            dkv = lax.psum_scatter(
                jnp.concatenate([own, send]), "wide", scatter_dimension=0, tiled=True
            )
        dkvs.append(dkv.transpose(1, 0, 2).reshape(2 * kd, slots))
    dq = jnp.concatenate(dqs, axis=1)
    dkv = jnp.concatenate(dkvs, axis=1)
    dk = turn_back(dkv[:kd].astype(F32), cos, sin).astype(BF16)
    dkv = jnp.concatenate([dk, dkv[kd:]])

    xn_t = xn.T
    s_query = wide.weight_sum(wide.ordered_rows(xn_t, first_q), dq, 1, first_q)
    s_kv = wide.weight_sum(wide.ordered_rows(xn_t, first_kv), dkv, 1, first_kv)

    d_xn = dot(dq, g_query, 0, 1) + dot(dkv, g_kv, 0, 1)
    u = d_xn * attn_gain
    grad_x = d_res + rr1 * u - x * rr1**3 * jnp.mean(u * x, axis=1, keepdims=True)
    gain_one = jnp.sum(d_xn * x * rr1, axis=0)
    gains = lax.psum(jnp.stack([gain_one, gain_two]), ("wide", "narrow"))

    over = functools.partial(row_sum, size=sizes["narrow"])
    s_down, s_gate, s_up, s_out = over(s_down), over(s_gate), over(s_up), over(s_out)
    s_query, s_kv = over(s_query), over(s_kv)
    shape = (micro, 1, slots, width)
    return (
        out.reshape(shape),
        grad_x.reshape(shape),
        gains[0],
        s_query,
        s_kv[:, :kd],
        s_kv[:, kd:],
        s_out,
        gains[1],
        s_gate,
        s_up,
        s_down,
    )


def solution(mesh):
    by_slot = P(None, "narrow", "wide", None)
    by_row = P(None, "narrow", None)
    split = P("wide", None)
    in_specs = (
        by_slot, by_row, by_row, P(), split, split, split, split, P(), split, split, split, by_slot,
    )
    out_specs = (
        by_slot, by_slot, P(), split, split, split, split, P(), split, split, split,
    )
    return jax.shard_map(
        functools.partial(shards, dict(mesh.shape)),
        mesh=mesh,
        in_specs=in_specs,
        out_specs=out_specs,
        check_vma=False,
    )
```

time: 2170 us -> 706 us (0.33)
  local copies, waits for them, and re-layouts: 776 us -> 133 us
  matrix products: 422 us -> 80.1 us
  other arithmetic: 282 us -> 38.2 us
  waiting for transfers between devices: 453 us -> 219 us
  loops' own time: 133 us -> 0 us
  starting transfers between devices: 1.66 us -> 96.5 us
  Pallas kernels: 0 us -> 75.8 us
    dot_general x316 -> x24, matrix products: 422 us -> 80.1 us  [dot(): lax.dot_general(a, b, (((ca,), (cb,)), ((), ())), preferred_element_type=...]
    reduce_scatter x8 -> x0, waiting for transfers between devices: 309 us -> none  [the longest x2 212 us: weight_terms(): lax.psum_scatter(jnp.concatenate(products, axis=1).astype(jnp.bfloat16),...]
    dynamic_update_slice x380 -> x47, local copies, waits for them, and re-layouts: 319 us -> 50 us  [rows(): whole = lax.dynamic_update_slice(whole, piece[None], (self.at ^ m, 0, 0))]
    ppermute x0 -> x98, waiting for transfers between devices: none -> 219 us  [the longest x80 159 us: swap(): return lax.ppermute(a, 'wide', [(i, i ^ bit) for i in range(self.size)])]
    dynamic_slice x202 -> x4, local copies, waits for them, and re-layouts: 185 us -> 3.63 us  [ordered_rows(): lax.dynamic_slice_in_dim(src_t, (self.at ^ m) * each, each)]
    another operation x254 -> x0, loops' own time: 133 us -> none  [the longest x20 49.8 us: scores_of(): lax.map(scores_one_block, (group_keys, live_blocks)) * score_scale]
    reduce_sum x43 -> x4, other arithmetic: 104 us -> 0.57 us  [the longest x1 0.23 us: shards(): rr1 = lax.rsqrt(jnp.mean(x * x, axis=1, keepdims=True) + EPS)]
    ppermute x0 -> x98, starting transfers between devices: none -> 96.5 us  [the longest x80 58.3 us: swap(): return lax.ppermute(a, 'wide', [(i, i ^ bit) for i in range(self.size)])]
  transfers between devices with their start and end apart: 18 -> 98, of which waited for: 11 -> 37; matrix products, arithmetic and copies ran while one was open for 44% -> 31% of each run, Pallas kernels for 0% -> 11%
where the time goes in v1:
time: 706 us; the launch traced here: 697 us
  waiting for transfers between devices  219 us (31%)
  local copies, waits for them, and re-layouts  133 us (19%)
  starting transfers between devices  96.5 us (14%)
  matrix products  80.1 us (11%)
  Pallas kernels  75.8 us (11%)
  blocking collectives  51.8 us (7%)
  other arithmetic  38.2 us (5%)
    ppermute x80, waiting for transfers between devices, swap(): return lax.ppermute(a, 'wide', [(i, i ^ bit) for i in range(self.size)])  159 us
    dot_general x24, matrix products, dot(): lax.dot_general(a, b, (((ca,), (cb,)), ((), ())), preferred_element_type=...  80.1 us
    ppermute x80, starting transfers between devices, swap(): return lax.ppermute(a, 'wide', [(i, i ^ bit) for i in range(self.size)])  58.3 us
    psum x1, blocking collectives, shards(): gains = lax.psum(jnp.stack([gain_one, gain_two]), ('wide', 'narrow'))  51.8 us
    dynamic_update_slice x47, local copies, waits for them, and re-layouts, rows(): whole = lax.dynamic_update_slice(whole, piece[None], (self.at ^ m, 0, 0))  50 us
    pallas_call x2, Pallas kernels, attention_bwd(): pl.pallas_call(functools.partial(bwd_kernel, groups, share), grid_spec=pl...  42.5 us
    ppermute x6, waiting for transfers between devices, row_sum(): back = lax.ppermute(part, 'narrow', [(1, 0), (2, 3)])  35.4 us
    pallas_call x2, Pallas kernels, attention_fwd(): pl.pallas_call(functools.partial(fwd_kernel, groups, share), grid_spec=pl...  33.3 us
  transfers between devices with their start and end apart: 98, of which 37 were waited for; matrix products, arithmetic and copies ran while one was open for 31% of the time, Pallas kernels for 11%

profile of v1, /device:TPU:0, one launch (start us, length us, event | category | flops | bytes accessed | tf_op | source)
XLA Modules:
  0.0 696.9 jit_solution(385443269449463955)
XLA Ops:
  79.4 7.0 %collective-permute-done.30 = bf16[120,960]{1,0:T(8,128)(2,1)} collective-permute-done((bf16[120,960]{1,0:T(8,128)(2,1)S(1)}, bf16[120,960]{1,0:T(8,128)(2,1)}, u32[]{:S(2)}, u32[]{:S(2)}) %collective-permute-start.30) | collective-permute-done | bytes 230432 | tf_op jit(solution)/shard_map/ppermute | solution.py:232
  94.8 7.5 %collective-permute-done.49 = bf16[320,960]{1,0:T(8,128)(2,1)S(1)} collective-permute-done((bf16[320,960]{1,0:T(8,128)(2,1)S(1)}, bf16[320,960]{1,0:T(8,128)(2,1)S(1)}, u32[]{:S(2)}, u32[]{:S(2)}) %collective-permute-start.49) | collective-permute-done | bytes 614432 | tf_op jit(solution)/shard_map/ppermute | solution.py:232
  109.8 6.6 collective-permute-done.35
  147.8 5.9 collective-permute-done.23
  166.4 6.7 collective-permute-done.44
  180.0 24.4 %collective-permute-done.37 = bf16[120,2560]{1,0:T(8,128)(2,1)} collective-permute-done((bf16[120,2560]{1,0:T(8,128)(2,1)S(1)}, bf16[120,2560]{1,0:T(8,128)(2,1)}, u32[]{:S(2)}, u32[]{:S(2)}) %collective-permute-start.37) | collective-permute-done | bytes 614432 | tf_op jit(solution)/shard_map/ppermute | solution.py:232
  218.0 14.0 %attention_fwd.2 = (bf16[960,256]{1,0:T(8,128)(2,1)}, f32[2,5,384]{2,1,0:T(8,128)}) custom-call(s32[2,2]{1,0:T(2,128)} %bitcast.285, s32[16]{0:T(128)} %get-tuple-element.176.kvat, bf16[960,512]{1,0:T(8,128)(2,1)} %bitcast.261, s32[1,512]{1,0:T(1,128)} %bitcast.272, bf16[16,640,128]{2,1,0:T(8,128)(2,1)} %copy-done.75), custom_call_target="tpu_custom_call" | custom-call | flops 5000000000 | bytes 4000000 | tf_op jit(solution)/shard_map/attention_fwd/pallas_call | solution.py:78
  233.8 19.3 %attention_fwd.3 = (bf16[960,256]{1,0:T(8,128)(2,1)}, f32[2,5,384]{2,1,0:T(8,128)}) custom-call(s32[2,2]{1,0:T(2,128)} %bitcast.287, s32[16]{0:T(128)} %get-tuple-element.175.kvat, bf16[960,512]{1,0:T(8,128)(2,1)} %bitcast.262, s32[1,512]{1,0:T(1,128)} %bitcast.273, bf16[16,640,128]{2,1,0:T(8,128)(2,1)} %constant_dynamic-update-slice_fusion.8.kv_ref), custom_call_target="tpu_custom_call" | custom-call | flops 5000000000 | bytes 4000000 | tf_op jit(solution)/shard_map/attention_fwd/pallas_call | solution.py:78
  273.8 8.2 %multiply_convert_fusion.1 = (bf16[2560,512]{1,0:T(8,128)(2,1)S(1)}, bf16[2560,512]{1,0:T(8,128)(2,1)S(1)}, bf16[2560,512]{1,0:T(8,128)(2,1)S(1)}) fusion(f32[2560,512]{1,0:T(8,128)S(1)} %fusion.102, f32[2560,512]{1,0:T(8,128)S(1)} %fusion.101, bf16[960,2560]{1,0:T(8,128)(2,1)} %bitcast.55, bf16[512,960]{0,1:T(8,128)(2,1)S(1)} %multiply_convert_fusion.4), kind=kOutput, calls=%fused_computation.2 | convolution fusion | flops 2537553920 | bytes 24248320 | tf_op jit(solution)/shard_map/dot_general | solution.py:21
  282.1 8.1 %add_convert_fusion.10 = bf16[512,960]{0,1:T(8,128)(2,1)} fusion(f32[512,960]{0,1:T(8,128)S(1)} %get-tuple-element.178, bf16[2560,512]{1,0:T(8,128)(2,1)S(1)} %get-tuple-element.117, bf16[2560,960]{1,0:T(8,128)(2,1)} %bitcast.73), kind=kOutput, calls=%fused_computation.24 | convolution fusion | flops 2517565440 | bytes 10485760 | tf_op jit(solution)/shard_map/dot_general | solution.py:21
  312.9 24.5 %attention_bwd.3 = (bf16[960,256]{1,0:T(8,128)(2,1)}, bf16[8,640,128]{2,1,0:T(8,128)(2,1)}, bf16[8,640,128]{2,1,0:T(8,128)(2,1)}) custom-call(s32[2,2]{1,0:T(2,128)} %bitcast.288, s32[16]{0:T(128)} %get-tuple-element.175.kvat, bf16[960,512]{1,0:T(8,128)(2,1)} %bitcast.263, bf16[960,512]{1,0:T(8,128)(2,1)} %convolution_convert_fusion.3.do_ref, ...), custom_call_target="tpu_custom_call" | custom-call | flops 10000000000 | bytes 8000000 | tf_op jit(solution)/shard_map/attention_bwd/pallas_call | solution.py:181
  337.5 18.0 %attention_bwd.2 = (bf16[960,256]{1,0:T(8,128)(2,1)}, bf16[8,640,128]{2,1,0:T(8,128)(2,1)}, bf16[8,640,128]{2,1,0:T(8,128)(2,1)}) custom-call(s32[2,2]{1,0:T(2,128)} %bitcast.286, s32[16]{0:T(128)} %get-tuple-element.176.kvat, bf16[960,512]{1,0:T(8,128)(2,1)} %bitcast.264, bf16[960,512]{1,0:T(8,128)(2,1)} %convolution_convert_fusion.3.do_ref, ...), custom_call_target="tpu_custom_call" | custom-call | flops 10000000000 | bytes 8000000 | tf_op jit(solution)/shard_map/attention_bwd/pallas_call | solution.py:181
  374.2 6.6 collective-permute-done.75
  385.5 10.8 %collective-permute-done.76 = bf16[120,960]{1,0:T(8,128)(2,1)S(1)} collective-permute-done((bf16[120,960]{1,0:T(8,128)(2,1)S(1)}, bf16[120,960]{1,0:T(8,128)(2,1)S(1)}, u32[]{:S(2)}, u32[]{:S(2)}) %collective-permute-start.76) | collective-permute-done | bytes 230432 | tf_op jit(solution)/shard_map/ppermute | solution.py:232
  396.3 7.5 %collective-permute-start.77 = (bf16[120,960]{1,0:T(8,128)(2,1)S(1)}, bf16[120,960]{1,0:T(8,128)(2,1)}, u32[]{:S(2)}, u32[]{:S(2)}) collective-permute-start(bf16[120,960]{1,0:T(8,128)(2,1)S(1)} %add_convert_fusion.31), channel_id=1, source_target_pairs={{0,1},{3,2},{4,5},{7,6},{8,9},{11,10},{12,13},{15,14},{16,17},{19,... | collective-permute-start | bytes 691208 | tf_op jit(solution)/shard_map/ppermute | solution.py:291
  418.7 5.8 collective-permute-done.61
  449.8 51.8 %psum.7 = f32[2,960]{1,0:T(2,128)S(1)} all-reduce(f32[2,960]{1,0:T(2,128)S(1)} %pad_maximum_fusion.34), channel_id=1, replica_groups=mesh['wide'=8,'narrow'=4] {'wide','narrow'}, use_global_device_ids=true, to_apply=%region_9.10 | all-reduce | flops 1920 | bytes 15360 | tf_op jit(solution)/shard_map/psum | solution.py:436
  528.4 22.8 %collective-permute-done.70 = bf16[120,640]{1,0:T(8,128)(2,1)S(1)} collective-permute-done((bf16[120,640]{1,0:T(8,128)(2,1)S(1)}, bf16[120,640]{1,0:T(8,128)(2,1)S(1)}, u32[]{:S(2)}, u32[]{:S(2)}) %collective-permute-start.70) | collective-permute-done | bytes 153632 | tf_op jit(solution)/shard_map/ppermute | solution.py:232
  582.0 14.9 %collective-permute-done.81 = bf16[240,2560]{1,0:T(8,128)(2,1)} collective-permute-done((bf16[240,2560]{1,0:T(8,128)(2,1)}, bf16[240,2560]{1,0:T(8,128)(2,1)}, u32[]{:S(2)}, u32[]{:S(2)}) %collective-permute-start.81) | collective-permute-done | bytes 1228832 | tf_op jit(solution)/shard_map/ppermute | solution.py:232
  610.7 6.4 collective-permute-start.95
  633.2 12.2 %collective-permute-done.89 = bf16[120,2560]{1,0:T(8,128)(2,1)S(1)} collective-permute-done((bf16[120,2560]{1,0:T(8,128)(2,1)S(1)}, bf16[120,2560]{1,0:T(8,128)(2,1)S(1)}, u32[]{:S(2)}, u32[]{:S(2)}) %collective-permute-start.89) | collective-permute-done | bytes 614432 | tf_op jit(solution)/shard_map/ppermute | solution.py:291
  646.3 6.9 collective-permute-done.83
  658.7 17.0 %collective-permute-done.97 = bf16[320,960]{1,0:T(8,128)(2,1)S(1)} collective-permute-done((bf16[320,960]{1,0:T(8,128)(2,1)S(1)}, bf16[320,960]{1,0:T(8,128)(2,1)S(1)}, u32[]{:S(2)}, u32[]{:S(2)}) %collective-permute-start.97) | collective-permute-done | bytes 614432 | tf_op jit(solution)/shard_map/ppermute | solution.py:293
  676.8 12.0 %collective-permute-done.91 = bf16[120,2560]{1,0:T(8,128)(2,1)S(1)} collective-permute-done((bf16[120,2560]{1,0:T(8,128)(2,1)S(1)}, bf16[120,2560]{1,0:T(8,128)(2,1)S(1)}, u32[]{:S(2)}, u32[]{:S(2)}) %collective-permute-start.91) | collective-permute-done | bytes 614432 | tf_op jit(solution)/shard_map/ppermute | solution.py:293
  (574 shorter events, 369.1 us)
Async XLA Ops:
  8.1 51.6 %collective-permute-start.10 = (bf16[120,640]{1,0:T(8,128)(2,1)}, bf16[120,640]{1,0:T(8,128)(2,1)}, u32[]{:S(2)}, u32[]{:S(2)}) collective-permute-start(bf16[120,640]{1,0:T(8,128)(2,1)} %get-tuple-element.113), channel_id=1, source_target_pairs={{0,4},{4,0},{8,12},{12,8},{16,20},{20,16},{24,28},{28,24},{1,5},{5... | collective-permute-start | bytes 460808 | tf_op jit(solution)/shard_map/ppermute | solution.py:232
  8.7 38.9 %collective-permute-start.1 = (bf16[120,960]{1,0:T(8,128)(2,1)}, bf16[120,960]{1,0:T(8,128)(2,1)}, u32[]{:S(2)}, u32[]{:S(2)}) collective-permute-start(bf16[120,960]{1,0:T(8,128)(2,1)} %param.17), channel_id=1, source_target_pairs={{0,16},{4,20},{8,24},{12,28},{16,0},{20,4},{24,8},{28,12},{1,17},{... | collective-permute-start | bytes 691208 | tf_op jit(solution)/shard_map/ppermute | solution.py:232
  47.6 41.0 %collective-permute-start.31 = (bf16[120,960]{1,0:T(8,128)(2,1)}, bf16[120,960]{1,0:T(8,128)(2,1)}, u32[]{:S(2)}, u32[]{:S(2)}) collective-permute-start(bf16[120,960]{1,0:T(8,128)(2,1)} %param.20), channel_id=1, source_target_pairs={{0,4},{4,0},{8,12},{12,8},{16,20},{20,16},{24,28},{28,24},{1,5},{5... | collective-permute-start | bytes 691208 | tf_op jit(solution)/shard_map/ppermute | solution.py:232
  50.1 53.6 %collective-permute-start.42 = (bf16[120,2560]{1,0:T(8,128)(2,1)}, bf16[120,2560]{1,0:T(8,128)(2,1)}, u32[]{:S(2)}, u32[]{:S(2)}) collective-permute-start(bf16[120,2560]{1,0:T(8,128)(2,1)} %param.23), channel_id=1, source_target_pairs={{0,8},{4,12},{8,0},{12,4},{16,24},{20,28},{24,16},{28,20},{1,9},{5... | collective-permute-start | bytes 1843208 | tf_op jit(solution)/shard_map/ppermute | solution.py:232
  58.1 48.9 %collective-permute-start.43 = (bf16[120,2560]{1,0:T(8,128)(2,1)}, bf16[120,2560]{1,0:T(8,128)(2,1)}, u32[]{:S(2)}, u32[]{:S(2)}) collective-permute-start(bf16[120,2560]{1,0:T(8,128)(2,1)} %param.23), channel_id=1, source_target_pairs={{0,16},{4,20},{8,24},{12,28},{16,0},{20,4},{24,8},{28,12},{1,17},{... | collective-permute-start | bytes 1843208 | tf_op jit(solution)/shard_map/ppermute | solution.py:232
  72.7 101.3 %collective-permute-start.45 = (bf16[120,2560]{1,0:T(8,128)(2,1)}, bf16[120,2560]{1,0:T(8,128)(2,1)}, u32[]{:S(2)}, u32[]{:S(2)}) collective-permute-start(bf16[120,2560]{1,0:T(8,128)(2,1)} %param.23), channel_id=1, source_target_pairs={{0,4},{4,0},{8,12},{12,8},{16,20},{20,16},{24,28},{28,24},{1,5},{5... | collective-permute-start | bytes 1843208 | tf_op jit(solution)/shard_map/ppermute | solution.py:232
  164.7 48.2 %collective-permute-start.52 = (bf16[320,960]{1,0:T(8,128)(2,1)S(1)}, bf16[320,960]{1,0:T(8,128)(2,1)S(1)}, u32[]{:S(2)}, u32[]{:S(2)}) collective-permute-start(bf16[320,960]{1,0:T(8,128)(2,1)S(1)} %copy-done.34), channel_id=1, source_target_pairs={{0,4},{4,0},{8,12},{12,8},{16,20},{20,16},{24,28},{28,24},{1,5},{5... | collective-permute-start | bytes 1843208 | tf_op jit(solution)/shard_map/ppermute | solution.py:232
  165.3 41.1 %collective-permute-start.38 = (bf16[120,2560]{1,0:T(8,128)(2,1)S(1)}, bf16[120,2560]{1,0:T(8,128)(2,1)S(1)}, u32[]{:S(2)}, u32[]{:S(2)}) collective-permute-start(bf16[120,2560]{1,0:T(8,128)(2,1)S(1)} %copy-done.43), channel_id=1, source_target_pairs={{0,4},{4,0},{8,12},{12,8},{16,20},{20,16},{24,28},{28,24},{1,5},{5... | collective-permute-start | bytes 1843208 | tf_op jit(solution)/shard_map/ppermute | solution.py:232
  174.0 37.8 %collective-permute-start.51 = (bf16[320,960]{1,0:T(8,128)(2,1)S(1)}, bf16[320,960]{1,0:T(8,128)(2,1)S(1)}, u32[]{:S(2)}, u32[]{:S(2)}) collective-permute-start(bf16[320,960]{1,0:T(8,128)(2,1)S(1)} %copy-done.38), channel_id=1, source_target_pairs={{0,8},{4,12},{8,0},{12,4},{16,24},{20,28},{24,16},{28,20},{1,9},{5... | collective-permute-start | bytes 1843208 | tf_op jit(solution)/shard_map/ppermute | solution.py:232
  177.3 36.9 %collective-permute-start.53 = (bf16[320,960]{1,0:T(8,128)(2,1)S(1)}, bf16[320,960]{1,0:T(8,128)(2,1)S(1)}, u32[]{:S(2)}, u32[]{:S(2)}) collective-permute-start(bf16[320,960]{1,0:T(8,128)(2,1)S(1)} %copy-done.36), channel_id=1, source_target_pairs={{0,4},{4,0},{8,12},{12,8},{16,20},{20,16},{24,28},{28,24},{1,5},{5... | collective-permute-start | bytes 1843208 | tf_op jit(solution)/shard_map/ppermute | solution.py:232
  212.9 52.2 %collective-permute-start.48 = (bf16[120,2560]{1,0:T(8,128)(2,1)S(1)}, bf16[120,2560]{1,0:T(8,128)(2,1)}, u32[]{:S(2)}, u32[]{:S(2)}) collective-permute-start(bf16[120,2560]{1,0:T(8,128)(2,1)S(1)} %collective-permute-done.44), channel_id=1, source_target_pairs={{0,4},{4,0},{8,12},{12,8},{16,20},{20,16},{24,28},{28,24},{1,5},{5... | collective-permute-start | bytes 1843208 | tf_op jit(solution)/shard_map/ppermute | solution.py:232
  214.1 45.1 %collective-permute-start.55 = (bf16[320,960]{1,0:T(8,128)(2,1)S(1)}, bf16[320,960]{1,0:T(8,128)(2,1)S(1)}, u32[]{:S(2)}, u32[]{:S(2)}) collective-permute-start(bf16[320,960]{1,0:T(8,128)(2,1)S(1)} %collective-permute-done.51), channel_id=1, source_target_pairs={{0,4},{4,0},{8,12},{12,8},{16,20},{20,16},{24,28},{28,24},{1,5},{5... | collective-permute-start | bytes 1843208 | tf_op jit(solution)/shard_map/ppermute | solution.py:232
  215.2 56.7 %collective-permute-start.41 = (bf16[120,2560]{1,0:T(8,128)(2,1)}, bf16[120,2560]{1,0:T(8,128)(2,1)}, u32[]{:S(2)}, u32[]{:S(2)}) collective-permute-start(bf16[120,2560]{1,0:T(8,128)(2,1)} %collective-permute-done.37), channel_id=1, source_target_pairs={{0,4},{4,0},{8,12},{12,8},{16,20},{20,16},{24,28},{28,24},{1,5},{5... | collective-permute-start | bytes 1843208 | tf_op jit(solution)/shard_map/ppermute | solution.py:232
  294.3 209.7 %collective-permute-start.92 = (bf16[1280,960]{0,1:T(8,128)(2,1)}, bf16[1280,960]{0,1:T(8,128)(2,1)}, u32[]{:S(2)}, u32[]{:S(2)}) collective-permute-start(bf16[1280,960]{0,1:T(8,128)(2,1)} %convolution_convert_fusion.2), channel_id=1, source_target_pairs={{0,4},{4,0},{8,12},{12,8},{16,20},{20,16},{24,28},{28,24},{1,5},{5... | collective-permute-start | bytes 7372808 | tf_op jit(solution)/shard_map/ppermute | solution.py:232
  302.0 219.9 %collective-permute-start.86 = (bf16[480,2560]{1,0:T(8,128)(2,1)}, bf16[480,2560]{1,0:T(8,128)(2,1)}, u32[]{:S(2)}, u32[]{:S(2)}) collective-permute-start(bf16[480,2560]{1,0:T(8,128)(2,1)} %convolution_convert_fusion), channel_id=1, source_target_pairs={{0,4},{4,0},{8,12},{12,8},{16,20},{20,16},{24,28},{28,24},{1,5},{5... | collective-permute-start | bytes 7372808 | tf_op jit(solution)/shard_map/ppermute | solution.py:232
  312.9 50.0 %collective-permute-start.74 = (bf16[480,960]{1,0:T(8,128)(2,1)S(1)}, bf16[480,960]{1,0:T(8,128)(2,1)S(1)}, u32[]{:S(2)}, u32[]{:S(2)}) collective-permute-start(bf16[480,960]{1,0:T(8,128)(2,1)S(1)} %convolution_convert_fusion.4), channel_id=1, source_target_pairs={{0,4},{4,0},{8,12},{12,8},{16,20},{20,16},{24,28},{28,24},{1,5},{5... | collective-permute-start | bytes 2764808 | tf_op jit(solution)/shard_map/ppermute | solution.py:232
  373.2 38.6 %collective-permute-start.60 = (bf16[4,640,128]{2,1,0:T(8,128)(2,1)}, bf16[4,640,128]{2,1,0:T(8,128)(2,1)}, u32[]{:S(2)}, u32[]{:S(2)}) collective-permute-start(bf16[4,640,128]{2,1,0:T(8,128)(2,1)} %slice.257), channel_id=1, source_target_pairs={{0,8},{4,12},{8,0},{12,4},{16,24},{20,28},{24,16},{28,20},{1,9},{5... | collective-permute-start | bytes 1966088 | tf_op jit(solution)/shard_map/ppermute | solution.py:232
  410.3 148.1 %collective-permute-start.80 = (bf16[480,2560]{1,0:T(8,128)(2,1)}, bf16[480,2560]{1,0:T(8,128)(2,1)}, u32[]{:S(2)}, u32[]{:S(2)}) collective-permute-start(bf16[480,2560]{1,0:T(8,128)(2,1)} %convolution_convert_fusion.1), channel_id=1, source_target_pairs={{0,4},{4,0},{8,12},{12,8},{16,20},{20,16},{24,28},{28,24},{1,5},{5... | collective-permute-start | bytes 7372808 | tf_op jit(solution)/shard_map/ppermute | solution.py:232
  424.5 77.7 %collective-permute-start.79 = (bf16[120,960]{1,0:T(8,128)(2,1)}, bf16[120,960]{1,0:T(8,128)(2,1)}, u32[]{:S(2)}, u32[]{:S(2)}) collective-permute-start(bf16[120,960]{1,0:T(8,128)(2,1)} %add_convert_fusion.29), channel_id=1, source_target_pairs={{1,0},{2,3},{5,4},{6,7},{9,8},{10,11},{13,12},{14,15},{17,16},{18,... | collective-permute-start | bytes 691208 | tf_op jit(solution)/shard_map/ppermute | solution.py:293
  440.9 66.1 %collective-permute-start.68 = (bf16[480,640]{1,0:T(8,128)(2,1)}, bf16[480,640]{1,0:T(8,128)(2,1)}, u32[]{:S(2)}, u32[]{:S(2)}) collective-permute-start(bf16[480,640]{1,0:T(8,128)(2,1)} %convolution_convert_fusion.6), channel_id=1, source_target_pairs={{0,4},{4,0},{8,12},{12,8},{16,20},{20,16},{24,28},{28,24},{1,5},{5... | collective-permute-start | bytes 1843208 | tf_op jit(solution)/shard_map/ppermute | solution.py:232
  502.2 52.0 %collective-permute-start.62 = (bf16[480,960]{1,0:T(8,128)(2,1)}, bf16[480,960]{1,0:T(8,128)(2,1)}, u32[]{:S(2)}, u32[]{:S(2)}) collective-permute-start(bf16[480,960]{1,0:T(8,128)(2,1)} %convolution_convert_fusion.5), channel_id=1, source_target_pairs={{0,4},{4,0},{8,12},{12,8},{16,20},{20,16},{24,28},{28,24},{1,5},{5... | collective-permute-start | bytes 2764808 | tf_op jit(solution)/shard_map/ppermute | solution.py:232
  518.5 52.4 %collective-permute-start.93 = (bf16[640,960]{0,1:T(8,128)(2,1)}, bf16[640,960]{0,1:T(8,128)(2,1)}, u32[]{:S(2)}, u32[]{:S(2)}) collective-permute-start(bf16[640,960]{0,1:T(8,128)(2,1)} %copy.158), channel_id=1, source_target_pairs={{0,8},{4,12},{8,0},{12,4},{16,24},{20,28},{24,16},{28,20},{1,9},{5... | collective-permute-start | bytes 3686408 | tf_op jit(solution)/shard_map/ppermute | solution.py:232
  527.0 51.2 %collective-permute-start.87 = (bf16[240,2560]{1,0:T(8,128)(2,1)}, bf16[240,2560]{1,0:T(8,128)(2,1)}, u32[]{:S(2)}, u32[]{:S(2)}) collective-permute-start(bf16[240,2560]{1,0:T(8,128)(2,1)} %slice.285), channel_id=1, source_target_pairs={{0,16},{4,20},{8,24},{12,28},{16,0},{20,4},{24,8},{28,12},{1,17},{... | collective-permute-start | bytes 3686408 | tf_op jit(solution)/shard_map/ppermute | solution.py:232
  657.4 38.0 %collective-permute-start.85 = (bf16[120,2560]{1,0:T(8,128)(2,1)S(1)}, bf16[120,2560]{1,0:T(8,128)(2,1)S(1)}, u32[]{:S(2)}, u32[]{:S(2)}) collective-permute-start(bf16[120,2560]{1,0:T(8,128)(2,1)S(1)} %add_convert_fusion.19), channel_id=1, source_target_pairs={{1,0},{2,3},{5,4},{6,7},{9,8},{10,11},{13,12},{14,15},{17,16},{18,... | collective-permute-start | bytes 1843208 | tf_op jit(solution)/shard_map/ppermute | solution.py:293
  (163 other events, 2519.8 us)

commit v2 on v1

--- a/solution.py
+++ b/solution.py
@@ -110,7 +110,7 @@
 
 def bwd_kernel(
     groups, share, info, kvat, q_ref, do_ref, o_ref, lse_ref, start_ref, cos_ref, sin_ref, kv_ref,
-    dq_ref, own_ref, send_ref, qs, dos, delta, dq, dkv,
+    dq_ref, dkv_ref, qs, dos, delta, dq, dkv,
 ):
     i = pl.program_id(0)
     lo, b = info[0, i], info[1, i]
@@ -165,9 +165,7 @@
 
     @pl.when(i == pl.num_programs(0) - 1)
     def _():
-        n = own_ref.shape[0]
-        own_ref[...] = dkv[:n].astype(BF16)
-        send_ref[...] = dkv[n:].astype(BF16)
+        dkv_ref[...] = dkv[...].astype(BF16)
 
 
 def attention_bwd(info, kvat, q_t, do_t, o_t, lse, start, cos_t, sin_t, kv, mb):
@@ -195,8 +193,7 @@
             ],
             out_specs=[
                 pl.BlockSpec((width, BLOCK), lambda i, *_: (0, i)),
-                pl.BlockSpec((nb // 2, kvw, BLOCK), lambda i, *_: (0, 0, 0)),
-                pl.BlockSpec((nb // 2, kvw, BLOCK), lambda i, *_: (0, 0, 0)),
+                pl.BlockSpec((nb, kvw, BLOCK), lambda i, *_: (0, 0, 0)),
             ],
             scratch_shapes=[
                 pltpu.VMEM((groups, HDIM, lanes), BF16),
@@ -208,8 +205,7 @@
         ),
         out_shape=[
             jax.ShapeDtypeStruct((width, nq * BLOCK), BF16),
-            jax.ShapeDtypeStruct((nb // 2, kvw, BLOCK), BF16),
-            jax.ShapeDtypeStruct((nb // 2, kvw, BLOCK), BF16),
+            jax.ShapeDtypeStruct((nb, kvw, BLOCK), BF16),
         ],
         compiler_params=pltpu.CompilerParams(vmem_limit_bytes=VMEM_LIMIT),
         cost_estimate=pl.CostEstimate(
@@ -220,68 +216,370 @@
 
 
 CORE, ALONG_X, ALONG_Y = 1, 2, 4
-
-
-class Wide:
-    def __init__(self, size):
-        self.size = size
-        self.at = lax.axis_index("wide")
-        self.cube = size == 8
-
-    def swap(self, a, bit):
-        return lax.ppermute(a, "wide", [(i, i ^ bit) for i in range(self.size)])
-
-    def pieces(self, own, first):
-        other = ALONG_X + ALONG_Y - first
-        got = {0: own, ALONG_X: self.swap(own, ALONG_X), ALONG_Y: self.swap(own, ALONG_Y)}
-        got[ALONG_X + ALONG_Y] = self.swap(got[other], first)
-        for m in list(got):
-            got[m + CORE] = self.swap(got[m], CORE)
-        return got
-
-    def rows(self, own, first):
-        if not self.cube:
-            return lax.all_gather(own, "wide", axis=0, tiled=True)
-        rows, cols = own.shape
-        whole = jnp.zeros((self.size, rows, cols), own.dtype)
-        for m, piece in self.pieces(own, first).items():
-            whole = lax.dynamic_update_slice(whole, piece[None], (self.at ^ m, 0, 0))
-        return whole.reshape(self.size * rows, cols)
-
-    def order(self, first):
-        other = ALONG_X + ALONG_Y - first
+FAR = ALONG_X + ALONG_Y
+CUBE = 8
+LAG = 2
+LAGS = 1
+SEM = pltpu.SemaphoreType.DMA
+
+
+def meet(peers):
+    barrier = pltpu.get_barrier_semaphore()
+    for peer in peers:
+        pl.semaphore_signal(barrier, inc=1, device_id=peer, device_id_type=pl.DeviceIdType.MESH)
+    pl.semaphore_wait(barrier, len(peers))
+
+
+def gather_kernel(count, chunks, planes, *refs):
+    ins, outs = refs[:count], refs[count : 2 * count]
+    sent, came = refs[2 * count :]
+    at, row = lax.axis_index("wide"), lax.axis_index("narrow")
+    peer = {bit: (at ^ bit, row) for bit in (CORE, ALONG_X, ALONG_Y)}
+    if planes:
+        peer["row"] = (at, row ^ 1)
+
+    def part(ref, c, half):
+        return ref.at[chunks[c][1 + half]]
+
+    def copy(c, m, half, way, slot):
+        a = chunks[c][0]
+        there = part(outs[a].at[at ^ m], c, half)
+        return pltpu.make_async_remote_copy(
+            src_ref=there if m else part(ins[a], c, half),
+            dst_ref=there,
+            send_sem=sent.at[c, slot],
+            recv_sem=came.at[c, m if way == "row" else m ^ way, half],
+            device_id=peer[way],
+            device_id_type=pl.DeviceIdType.MESH,
+        )
+
+    def run(mine):
+        other = 1 - mine
+        used = [0] * len(chunks)
+        begun = []
+
+        def push(c, m, half, way):
+            r = copy(c, m, half, way, used[c])
+            used[c] += 1
+            r.start()
+            begun.append(r)
+
+        def take(c, m, half, *ways):
+            copy(c, m ^ CORE, half, CORE, 0).wait_recv()
+            for way in ways:
+                push(c, m, half, way)
+
+        def first(c):
+            push(c, 0, mine, ALONG_X)
+            push(c, 0, mine, ALONG_Y)
+            if not planes:
+                push(c, 0, other, ALONG_X)
+                push(c, 0, other, ALONG_Y)
+
+        def second(c):
+            if planes:
+                take(c, ALONG_Y, mine, ALONG_X, CORE)
+                push(c, 0, other, ALONG_Y)
+                take(c, ALONG_X, mine, "row", CORE)
+            else:
+                take(c, ALONG_X, mine, ALONG_Y, CORE)
+                take(c, ALONG_Y, other, ALONG_X, CORE)
+                take(c, ALONG_Y, mine, CORE)
+                take(c, ALONG_X, other, CORE)
+            push(c, 0, 0, CORE)
+            push(c, 0, 1, CORE)
+
+        def third(c):
+            take(c, FAR, mine, *(("row", CORE) if planes else (CORE,)))
+            if planes:
+                take(c, ALONG_Y, other, CORE)
+                take(c, ALONG_X, other, CORE)
+            else:
+                take(c, FAR, other, CORE)
+
+        def fourth(c):
+            if planes:
+                take(c, FAR, other, CORE)
+
+        def fifth(c):
+            for half in range(2):
+                take(c, CORE, half, CORE)
+            for m in (ALONG_X, ALONG_Y, FAR):
+                for half in range(2):
+                    take(c, m + CORE, half)
+
+        def sixth(c):
+            for half in range(2):
+                take(c, 0, half)
+
+        steps = (first, second, third, fourth, fifth, sixth)
+        for t in range(len(chunks) + LAG * (len(steps) - 1)):
+            for s, step in enumerate(steps):
+                if 0 <= t - LAG * s < len(chunks):
+                    step(t - LAG * s)
+        for r in begun:
+            r.wait_send()
+
+    meet(list(peer.values()))
+    if planes:
+        for mine in range(2):
+            pl.when(row % 2 == mine)(functools.partial(run, mine))
+    else:
+        run(0)
+
+
+def gather(arrays, chunks, planes, collective_id):
+    count = len(arrays)
+    return pl.pallas_call(
+        functools.partial(gather_kernel, count, chunks, planes),
+        in_specs=[pl.BlockSpec(memory_space=pl.ANY)] * count,
+        out_specs=[pl.BlockSpec(memory_space=pl.ANY)] * count,
+        out_shape=[jax.ShapeDtypeStruct((8,) + a.shape, a.dtype) for a in arrays],
+        scratch_shapes=[
+            SEM((len(chunks), 16)),
+            SEM((len(chunks), 8, 2)),
+        ],
+        compiler_params=pltpu.CompilerParams(collective_id=collective_id, has_side_effects=True),
+        name="gather_rows" if planes else "gather_keys",
+    )(*arrays)
+
+
+def weight_chunks(shapes, most=160 * 1024):
+    chunks = []
+    for a, (rows, cols) in enumerate(shapes):
+        n = 1
+        while rows * cols // n > most and rows % (32 * n) == 0:
+            n *= 2
+        k = 1
+        while rows // n * cols // k > most and cols % (256 * k) == 0:
+            k *= 2
+        for i in range(n):
+            lo, hi = rows // n * i, rows // n * (i + 1)
+            mid = lo + -(-(hi - lo) // 32) * 16
+            for j in range(k):
+                c = pl.ds(cols // k * j, cols // k)
+                chunks.append((a, (pl.ds(lo, mid - lo), c), (pl.ds(mid, hi - mid), c)))
+    return chunks
+
+
+def key_chunks(count, blocks, rows, parts=2):
+    return [
+        (a, (pl.ds(0, blocks // 2), pl.ds(rows // parts * i, rows // parts)),
+         (pl.ds(blocks // 2, blocks // 2), pl.ds(rows // parts * i, rows // parts)))
+        for a in range(count) for i in range(parts)
+    ]
+
+
+def sum_kernel(count, chunks, rows_too, *refs):
+    refs = list(refs)
+    take = lambda n: [refs.pop(0) for _ in range(n)]
+    ins = take(count)
+    gain = take(1)[0] if rows_too else None
+    outs = take(count)
+    total = take(1)[0] if rows_too else None
+    n = len(chunks)
+    held, core_in, one_in, two_in, line_in, last = (take(n) for _ in range(6))
+    load, sent, came, stored = take(4)
+    if rows_too:
+        gain_buf, gain_sent, gain_came = take(3)
+    at, row = lax.axis_index("wide"), lax.axis_index("narrow")
+    way = {bit: (at ^ bit, row) for bit in (CORE, ALONG_X, ALONG_Y)}
+    peers = [way[CORE], way[ALONG_X], way[ALONG_Y]]
+    if rows_too:
+        near, across = (at, row ^ 1), (at, row ^ 3)
+        peers += [near, across]
+    middle = (row == 1) | (row == 2)
+
+    def send(c, slot, src, dst, to):
+        return pltpu.make_async_remote_copy(
+            src_ref=src, dst_ref=dst, send_sem=sent.at[c, slot], recv_sem=came.at[c, slot],
+            device_id=to, device_id_type=pl.DeviceIdType.MESH,
+        )
+
+    def add(dst, src):
+        rows = dst.shape[-2]
+        most = rows // 16
+        step = 16 * max(k for k in (1, 2, 3, 4) if most % k == 0)
+
+        def body(i, carry):
+            cut = pl.ds(pl.multiple_of(i * step, 16), step)
+            dst[cut, :] = dst[cut, :] + src[cut, :]
+            return carry
+
+        lax.fori_loop(0, most * 16 // step, body, 0)
+        if rows % 16:
+            cut = slice(most * 16, rows)
+            dst[cut, :] = dst[cut, :] + src[cut, :]
+
+    def orders(c):
+        first = chunks[c][2]
+        other = FAR - first
+        return first, other, (0, other, first, FAR)
+
+    def core_copies(c):
+        a, cut, _ = chunks[c]
         return [
-            c * CORE + a * first + b * other for c in range(2) for a in range(2) for b in range(2)
+            send(c, i, ins[a].at[(at ^ CORE ^ m,) + cut], core_in[c].at[i], way[CORE])
+            for i, m in enumerate(orders(c)[2])
         ]
 
-    def ordered_rows(self, src_t, first):
-        if not self.cube:
-            return src_t
-        each = src_t.shape[0] // self.size
-        return jnp.concatenate(
-            [
-                lax.dynamic_slice_in_dim(src_t, (self.at ^ m) * each, each)
-                for m in self.order(first)
-            ]
+    def loads(c):
+        a, cut, _ = chunks[c]
+        return [
+            pltpu.make_async_copy(ins[a].at[(at ^ m,) + cut], held[c].at[i], load.at[c, i])
+            for i, m in enumerate(orders(c)[2])
+        ]
+
+    def first_copy(c):
+        return send(c, 4, held[c].at[pl.ds(2, 2)], one_in[c], way[orders(c)[0]])
+
+    def second_copy(c):
+        return send(c, 5, held[c].at[1], two_in[c], way[orders(c)[1]])
+
+    def inward(c):
+        return send(c, 6, held[c].at[0], line_in[c].at[0], near)
+
+    def over(c):
+        return send(c, 7, held[c].at[0], line_in[c].at[1], across)
+
+    def outward(c):
+        return send(c, 6, line_in[c].at[1], line_in[c].at[0], near)
+
+    def store(c):
+        a, cut, _ = chunks[c]
+        return pltpu.make_async_copy(last[c], outs[a].at[cut], stored.at[c])
+
+    def s0(c):
+        for r in core_copies(c) + loads(c):
+            r.start()
+
+    def s1(c):
+        for r in loads(c):
+            r.wait()
+        for r in core_copies(c):
+            r.wait_recv()
+        for i in (2, 3, 0, 1):
+            add(held[c].at[i], core_in[c].at[i])
+            if i == 3:
+                first_copy(c).start()
+
+    def s2(c):
+        first_copy(c).wait_recv()
+        add(held[c].at[1], one_in[c].at[1])
+        second_copy(c).start()
+        add(held[c].at[0], one_in[c].at[0])
+
+    def s3(c):
+        second_copy(c).wait_recv()
+        add(held[c].at[0], two_in[c])
+        if rows_too:
+            pl.when(~middle)(lambda: inward(c).start())
+        else:
+            last[c][...] = held[c][0].astype(last[c].dtype)
+            store(c).start()
+
+    def s4(c):
+        @pl.when(middle)
+        def _():
+            inward(c).wait_recv()
+            add(held[c].at[0], line_in[c].at[0])
+            over(c).start()
+
+    def s5(c):
+        @pl.when(middle)
+        def _():
+            over(c).wait_recv()
+            add(line_in[c].at[1], held[c].at[0])
+            outward(c).start()
+            last[c][...] = line_in[c][1].astype(last[c].dtype)
+            store(c).start()
+
+    def s6(c):
+        @pl.when(~middle)
+        def _():
+            outward(c).wait_recv()
+            last[c][...] = line_in[c][0].astype(last[c].dtype)
+            store(c).start()
+
+    meet(peers)
+    gain_ways = []
+    if rows_too:
+        gain_ways = [way[CORE], way[ALONG_X], way[ALONG_Y], near, across]
+        gain_buf[0] = gain[...]
+
+    def gain_copy(i):
+        return pltpu.make_async_remote_copy(
+            src_ref=gain_buf.at[2 * i], dst_ref=gain_buf.at[2 * i + 1], send_sem=gain_sent.at[i],
+            recv_sem=gain_came.at[i], device_id=gain_ways[i], device_id_type=pl.DeviceIdType.MESH,
         )
 
-    def halve(self, own, bit):
-        half = own.shape[0] // 2
-        got = self.swap(own[half:], bit)
-        return (own[:half].astype(F32) + got.astype(F32)).astype(BF16)
-
-    def scatter_chips(self, own, first):
-        return self.halve(self.halve(own, first), ALONG_X + ALONG_Y - first)
-
-    def weight_sum(self, src_ord, target, target_dim, first):
-        if not self.cube:
-            return lax.psum_scatter(
-                dot(src_ord, target, 1, target_dim).astype(BF16), "wide", scatter_dimension=0, tiled=True
-            )
-        half = src_ord.shape[0] // 2
-        got = self.swap(dot(src_ord[half:], target, 1, target_dim).astype(BF16), CORE)
-        own = (dot(src_ord[:half], target, 1, target_dim) + got.astype(F32)).astype(BF16)
-        return self.scatter_chips(own, first)
+    steps = (s0, s1, s2, s3) + ((s4, s5, s6) if rows_too else ())
+    for t in range(n + LAGS * (len(steps) - 1)):
+        for s, step in enumerate(steps):
+            if 0 <= t - LAGS * s < n:
+                step(t - LAGS * s)
+        if 1 <= t <= len(gain_ways):
+            gain_copy(t - 1).wait_recv()
+            gain_buf[2 * t] = gain_buf[2 * t - 2] + gain_buf[2 * t - 1]
+        if t < len(gain_ways):
+            gain_copy(t).start()
+    for c in range(n):
+        for r in core_copies(c):
+            r.wait_send()
+        first_copy(c).wait_send()
+        second_copy(c).wait_send()
+        if rows_too:
+            inward(c).wait_send()
+            pl.when(middle)(lambda: over(c).wait_send())
+        store(c).wait()
+    for i in range(len(gain_ways)):
+        gain_copy(i).wait_send()
+    if rows_too:
+        total[...] = gain_buf[2 * len(gain_ways)]
+
+
+def sums(arrays, chunks, collective_id, gain=None):
+    count, n = len(arrays), len(chunks)
+    rows_too = gain is not None
+    kind = F32 if rows_too else arrays[0].dtype
+    anywhere = pl.BlockSpec(memory_space=pl.ANY)
+    vmem = pl.BlockSpec(memory_space=pltpu.VMEM)
+    size = [(c[1][0].size, c[1][1].size) for c in chunks]
+    dtype = arrays[0].dtype
+    room = lambda *lead: [pltpu.VMEM(lead + s, dtype) for s in size]
+    line = room(2) if rows_too else [pltpu.VMEM((8, 128), dtype)] * n
+    scratch = room(4) + room(4) + room(2) + room() + line + [pltpu.VMEM(s, kind) for s in size]
+    scratch += [SEM((n, 4)), SEM((n, 8)), SEM((n, 8)), SEM((n,))]
+    outs = [jax.ShapeDtypeStruct(a.shape[1:], kind) for a in arrays]
+    if rows_too:
+        scratch += [pltpu.VMEM((11,) + gain.shape, F32), SEM((5,)), SEM((5,))]
+        outs.append(jax.ShapeDtypeStruct(gain.shape, F32))
+    return pl.pallas_call(
+        functools.partial(sum_kernel, count, chunks, rows_too),
+        in_specs=[anywhere] * count + [vmem] * rows_too,
+        out_specs=[anywhere] * count + [vmem] * rows_too,
+        out_shape=outs,
+        scratch_shapes=scratch,
+        compiler_params=pltpu.CompilerParams(
+            collective_id=collective_id, has_side_effects=True, vmem_limit_bytes=62 * 1024 * 1024
+        ),
+        name="sum_weights" if rows_too else "sum_keys",
+    )(*arrays, *([gain] if rows_too else []))
+
+
+def sum_chunks(shapes, most=180 * 1024):
+    chunks = []
+    for a, (rows, cols) in enumerate(shapes):
+        n = k = 1
+        while rows // n * cols > most and rows % (32 * n) == 0:
+            n *= 2
+        while rows // n * cols // k > most and cols % (256 * k) == 0:
+            k *= 2
+        for i in range(n):
+            for j in range(k):
+                first = (ALONG_X, ALONG_Y)[len(chunks) % 2]
+                chunks.append((a, (pl.ds(rows // n * i, rows // n), pl.ds(cols // k * j, cols // k)), first))
+    return chunks
 
 
 def row_sum(part, size):
@@ -307,8 +605,8 @@
 
 def shards(sizes, tokens, lengths, block_plan, attn_gain, w_query, w_key, w_value, w_out, ffn_gain,
            w_gate, w_up, w_down, cotangent):
-    wide = Wide(sizes["wide"])
-    n = wide.size
+    n = sizes["wide"]
+    at = lax.axis_index("wide")
     micro, _, slots, width = tokens.shape
     total = micro * slots
     kd = w_key.shape[1]
@@ -321,7 +619,7 @@
     docs = sizes_of.shape[1]
     upto = jnp.arange(docs)[:, None] >= jnp.arange(docs)[None, :]
     ends = jnp.sum(jnp.where(upto[None], sizes_of[:, None, :], 0), axis=2)
-    own_plan = lax.dynamic_slice_in_dim(plan, wide.at * nq, nq, axis=1)
+    own_plan = lax.dynamic_slice_in_dim(plan, at * nq, nq, axis=1)
     position = own_plan[:, :, None] * BLOCK + jnp.arange(BLOCK, dtype=jnp.int32)
     start = jnp.sum(
         jnp.where(position[..., None] >= ends[:, None, None, :], sizes_of[:, None, None, :], 0), axis=3
@@ -337,42 +635,55 @@
     angles = frequency[:, None] * local.astype(F32)
     cos, sin = jnp.cos(angles), jnp.sin(angles)
 
-    if wide.cube:
-        kv_order = wide.order(ALONG_X)
-        rank = sum(
-            jnp.where((where_is // nq) ^ wide.at == m, r, 0) for r, m in enumerate(kv_order)
-        )
-        kvat = rank * nq + where_is % nq
-    else:
-        kvat = where_is
+    cube = n == CUBE and sizes["narrow"] == 4 and nq % 2 == 0
+
+    def whole_rows(*shards_of):
+        if cube:
+            got = gather(shards_of, weight_chunks([a.shape for a in shards_of]), True, 1)
+        else:
+            got = [lax.all_gather(a, "wide", axis=0) for a in shards_of]
+        return [a.reshape(-1, a.shape[2]) for a in got]
+
+    def whole_keys(*own):
+        if cube:
+            got = gather(own, key_chunks(len(own), nq, own[0].shape[1]), False, 2)
+        else:
+            got = [lax.all_gather(a, "wide", axis=0) for a in own]
+        return [a.reshape((nb,) + a.shape[2:]) for a in got]
+
+    def key_sums(*parts):
+        shaped = [a.reshape(n, -1, BLOCK) for a in parts]
+        if cube:
+            got = sums(shaped, sum_chunks([a.shape[1:] for a in shaped], 100 * 1024), 3)
+        else:
+            got = [lax.psum_scatter(a, "wide", scatter_dimension=0) for a in shaped]
+        return [a.reshape((nq,) + p.shape[1:]) for a, p in zip(got, parts)]
+
+    def weight_sums(gain, *parts):
+        shaped = [a.reshape(n, -1, a.shape[1]) for a in parts]
+        if cube:
+            *got, gain = sums(shaped, sum_chunks([a.shape[1:] for a in shaped]), 4, gain)
+            return got, gain
+        got = [lax.psum_scatter(a, "wide", scatter_dimension=0) for a in shaped]
+        return [row_sum(a, sizes["narrow"]) for a in got], lax.psum(gain, ("wide", "narrow"))
 
     x = tokens.reshape(total, width).astype(F32)
     ct = cotangent.reshape(total, width)
 
-    g_query = wide.rows(w_query, ALONG_X)
-    g_kv = wide.rows(jnp.concatenate([w_key, w_value], axis=1), ALONG_Y)
-    g_out = wide.rows(w_out, ALONG_Y)
-    g_gate = wide.rows(w_gate, ALONG_X)
-    g_up = wide.rows(w_up, ALONG_Y)
-    g_down = wide.rows(w_down, ALONG_X)
-
+    g_query, g_key, g_value, g_out, g_gate, g_up, g_down = whole_rows(
+        w_query, w_key, w_value, w_out, w_gate, w_up, w_down
+    )
     rr1 = lax.rsqrt(jnp.mean(x * x, axis=1, keepdims=True) + EPS)
     xn = (x * rr1 * attn_gain).astype(BF16)
-    kv_t = dot(g_kv, xn, 0, 1)
-    key_t = turn(kv_t[:kd], cos, sin).astype(BF16)
-    value_t = kv_t[kd:].astype(BF16)
+    key_t = turn(dot(g_key, xn, 0, 1), cos, sin).astype(BF16)
+    value_t = dot(g_value, xn, 0, 1).astype(BF16)
     own_kv = jnp.concatenate([key_t, value_t]).reshape(2 * kd, micro, nq, BLOCK).transpose(1, 2, 0, 3)
     q_t = (turn(dot(g_query, xn, 0, 1), cos, sin).astype(BF16) * HDIM**-0.5).astype(BF16)
 
-    kvs, outs, lses = [], [], []
+    kvs = whole_keys(*[own_kv[mb] for mb in range(micro)])
+    outs, lses = [], []
     for mb in range(micro):
-        if wide.cube:
-            got = wide.pieces(own_kv[mb], ALONG_X)
-            kv = jnp.concatenate([got[m] for m in kv_order])
-        else:
-            kv = lax.all_gather(own_kv[mb], "wide", axis=0, tiled=True)
-        o_t, lse = attention_fwd(info[mb], kvat[mb], q_t, start, kv, mb)
-        kvs.append(kv)
+        o_t, lse = attention_fwd(info[mb], where_is[mb], q_t, start, kvs[mb], mb)
         outs.append(o_t)
         lses.append(lse)
     att_t = jnp.concatenate(outs, axis=1)
@@ -386,15 +697,9 @@
     hidden = (gate * sg * up).astype(BF16)
     out = (res + dot(hidden, g_down, 0, 0)).astype(BF16)
 
-    first_down, first_out, first_q, first_kv = ALONG_X, ALONG_Y, ALONG_X, ALONG_Y
-    s_down = wide.weight_sum(wide.ordered_rows(hidden, first_down), ct, 0, first_down)
-
     d_hidden = dot(g_down, ct, 1, 1)
     d_gate = (d_hidden * up * sg * (1.0 + gate * (1.0 - sg))).astype(BF16)
     d_up = (d_hidden * gate * sg).astype(BF16)
-    hn_t = hn.T
-    s_gate = wide.weight_sum(wide.ordered_rows(hn_t, ALONG_X), d_gate, 1, ALONG_X)
-    s_up = wide.weight_sum(wide.ordered_rows(hn_t, ALONG_Y), d_up, 1, ALONG_Y)
     d_hn = dot(d_gate, g_gate, 0, 1) + dot(d_up, g_up, 0, 1)
     u = d_hn * ffn_gain
     d_res = (
@@ -403,49 +708,43 @@
     gain_two = jnp.sum(d_hn * res * rr2, axis=0)
     d_attn = d_res.astype(BF16)
     do_t = dot(g_out, d_attn, 1, 1).astype(BF16)
-    s_out = wide.weight_sum(wide.ordered_rows(att_t, first_out), d_attn, 0, first_out)
 
     dqs, dkvs = [], []
     for mb in range(micro):
-        dq_t, own, send = attention_bwd(
-            info[mb], kvat[mb], q_t, do_t, outs[mb] if micro == 1 else att_t, lses[mb], start, cos, sin,
-            kvs[mb], mb,
+        dq_t, dkv = attention_bwd(
+            info[mb], where_is[mb], q_t, do_t, att_t, lses[mb], start, cos, sin, kvs[mb], mb
         )
         dqs.append(dq_t)
-        if wide.cube:
-            got = wide.swap(send, CORE)
-            dkv = wide.scatter_chips((own.astype(F32) + got.astype(F32)).astype(BF16), ALONG_X)
-        else:
-            dkv = lax.psum_scatter(
-                jnp.concatenate([own, send]), "wide", scatter_dimension=0, tiled=True
-            )
-        dkvs.append(dkv.transpose(1, 0, 2).reshape(2 * kd, slots))
+        dkvs.append(dkv)
     dq = jnp.concatenate(dqs, axis=1)
-    dkv = jnp.concatenate(dkvs, axis=1)
+    dkv = jnp.concatenate([a.transpose(1, 0, 2).reshape(2 * kd, slots) for a in key_sums(*dkvs)], axis=1)
     dk = turn_back(dkv[:kd].astype(F32), cos, sin).astype(BF16)
-    dkv = jnp.concatenate([dk, dkv[kd:]])
-
-    xn_t = xn.T
-    s_query = wide.weight_sum(wide.ordered_rows(xn_t, first_q), dq, 1, first_q)
-    s_kv = wide.weight_sum(wide.ordered_rows(xn_t, first_kv), dkv, 1, first_kv)
-
-    d_xn = dot(dq, g_query, 0, 1) + dot(dkv, g_kv, 0, 1)
+    dv = dkv[kd:]
+
+    d_xn = dot(dq, g_query, 0, 1) + dot(dk, g_key, 0, 1) + dot(dv, g_value, 0, 1)
     u = d_xn * attn_gain
     grad_x = d_res + rr1 * u - x * rr1**3 * jnp.mean(u * x, axis=1, keepdims=True)
     gain_one = jnp.sum(d_xn * x * rr1, axis=0)
-    gains = lax.psum(jnp.stack([gain_one, gain_two]), ("wide", "narrow"))
-
-    over = functools.partial(row_sum, size=sizes["narrow"])
-    s_down, s_gate, s_up, s_out = over(s_down), over(s_gate), over(s_up), over(s_out)
-    s_query, s_kv = over(s_query), over(s_kv)
+
+    part = lambda a, b, ca, cb: dot(a, b, ca, cb).astype(BF16)
+    (s_down, s_gate, s_up, s_out, s_query, s_key, s_value), gains = weight_sums(
+        jnp.stack([gain_one, gain_two]),
+        part(hidden, ct, 1, 0),
+        part(hn, d_gate, 0, 1),
+        part(hn, d_up, 0, 1),
+        part(att_t, d_attn, 1, 0),
+        part(xn, dq, 0, 1),
+        part(xn, dk, 0, 1),
+        part(xn, dv, 0, 1),
+    )
     shape = (micro, 1, slots, width)
     return (
         out.reshape(shape),
         grad_x.reshape(shape),
         gains[0],
         s_query,
-        s_kv[:, :kd],
-        s_kv[:, kd:],
+        s_key,
+        s_value,
         s_out,
         gains[1],
         s_gate,

time: 706 us -> 511 us (0.72)
  Pallas kernels: 75.8 us -> 353 us
  waiting for transfers between devices: 219 us -> 0 us
  starting transfers between devices: 96.5 us -> 0 us
  local copies, waits for them, and re-layouts: 133 us -> 67.8 us
  blocking collectives: 51.8 us -> 0 us
  other arithmetic: 38.2 us -> 14.8 us
  matrix products: 80.1 us -> 68.7 us
    pallas_call x0 -> x4, Pallas kernels: none -> 257 us  [the longest x2 157 us: sums(): pl.pallas_call(functools.partial(sum_kernel, count, chunks, rows_too), in...]
    ppermute x98 -> x0, waiting for transfers between devices: 219 us -> none  [the longest x80 159 us: swap(): return lax.ppermute(a, 'wide', [(i, i ^ bit) for i in range(self.size)])]
    ppermute x98 -> x0, starting transfers between devices: 96.5 us -> none  [the longest x80 58.3 us: swap(): return lax.ppermute(a, 'wide', [(i, i ^ bit) for i in range(self.size)])]
    psum x1 -> x0, blocking collectives: 51.8 us -> none  [shards(): gains = lax.psum(jnp.stack([gain_one, gain_two]), ('wide', 'narrow'))]
    dynamic_update_slice x47 -> x0, local copies, waits for them, and re-layouts: 50 us -> none  [rows(): whole = lax.dynamic_update_slice(whole, piece[None], (self.at ^ m, 0, 0))]
    convert_element_type x35 -> x0, other arithmetic: 28.7 us -> none  [the longest x14 13 us: halve(): return (own[:half].astype(F32) + got.astype(F32)).astype(BF16)]
    convert_element_type x0 -> x3, local copies, waits for them, and re-layouts: none -> 11.6 us  [shards(): part = lambda a, b, ca, cb: dot(a, b, ca, cb).astype(BF16)]
    dot_general x24 -> x21, matrix products: 80.1 us -> 68.7 us  [dot(): lax.dot_general(a, b, (((ca,), (cb,)), ((), ())), preferred_element_type=...]
  transfers between devices with their start and end apart: 98 -> 0, of which waited for: 37 -> 0; matrix products, arithmetic and copies ran while one was open for 31% -> 0% of each run, Pallas kernels for 11% -> 0%
where the time goes in v2:
time: 511 us; the launch traced here: 506 us
  Pallas kernels  353 us (69%)
  matrix products  68.7 us (13%)
  local copies, waits for them, and re-layouts  67.8 us (13%)
  other arithmetic  14.8 us (3%)
    pallas_call x2, Pallas kernels, sums(): pl.pallas_call(functools.partial(sum_kernel, count, chunks, rows_too), in...  157 us
    pallas_call x2, Pallas kernels, gather(): pl.pallas_call(functools.partial(gather_kernel, count, chunks, planes), i...  99.7 us
    dot_general x21, matrix products, dot(): lax.dot_general(a, b, (((ca,), (cb,)), ((), ())), preferred_element_type=...  68.7 us
    pallas_call x2, Pallas kernels, attention_bwd(): pl.pallas_call(functools.partial(bwd_kernel, groups, share), grid_spec=pl...  53.4 us
    pallas_call x2, Pallas kernels, attention_fwd(): pl.pallas_call(functools.partial(fwd_kernel, groups, share), grid_spec=pl...  42.5 us
    unnamed x110, local copies, waits for them, and re-layouts  28.1 us
    convert_element_type x3, local copies, waits for them, and re-layouts, shards(): part = lambda a, b, ca, cb: dot(a, b, ca, cb).astype(BF16)  11.6 us

profile of v2, /device:TPU:0, one launch (start us, length us, event | category | flops | bytes accessed | tf_op | source)
XLA Modules:
  0.0 505.8 jit_solution(7841624909622765265)
XLA Ops:
  18.8 71.0 %gather_rows.1 = (bf16[8,120,960]{2,1,0:T(8,128)(2,1)}, bf16[8,120,320]{2,1,0:T(8,128)(2,1)}, bf16[8,120,320]{2,1,0:T(8,128)(2,1)}, bf16[8,120,960]{2,1,0:T(8,12...) custom-call(bf16[120,960]{1,0:T(8,128)(2,1)} %refs_0_.1, ...), custom_call_target="tpu_custom_call" | custom-call | tf_op jit(solution)/shard_map/gather_rows/pallas_call | solution.py:333
  89.8 2.7 convolution_convert_fusion.8
  104.0 4.3 copy.104
  108.3 3.0 fusion.2
  112.7 28.7 %gather_keys.1 = (bf16[8,2,640,128]{3,2,1,0:T(8,128)(2,1)}, bf16[8,2,640,128]{3,2,1,0:T(8,128)(2,1)}) custom-call(bf16[2,640,128]{2,1,0:T(8,128)(2,1)} %get-tuple-element.136.refs_0_, bf16[2,640,128]{2,1,0:T(8,128)(2,1)} %get-tuple-element.135.refs_1_), custom_call_target="tpu_custom_call" | custom-call | tf_op jit(solution)/shard_map/gather_keys/pallas_call | solution.py:333
  141.4 19.3 %attention_fwd.3 = (bf16[960,256]{1,0:T(8,128)(2,1)}, f32[2,5,384]{2,1,0:T(8,128)}) custom-call(s32[2,2]{1,0:T(2,128)} %bitcast.195, s32[16]{0:T(128)} %get-tuple-element.148.kvat, bf16[960,512]{1,0:T(8,128)(2,1)} %bitcast.166, s32[1,512]{1,0:T(1,128)} %bitcast.180, bf16[16,640,128]{2,1,0:T(8,128)(2,1)} %bitcast.211), custom_call_target="tpu_custom_call" | custom-call | flops 5000000000 | bytes 4000000 | tf_op jit(solution)/shard_map/attention_fwd/pallas_call | solution.py:78
  160.7 23.3 %attention_fwd.2 = (bf16[960,256]{1,0:T(8,128)(2,1)}, f32[2,5,384]{2,1,0:T(8,128)}) custom-call(s32[2,2]{1,0:T(2,128)} %bitcast.193, s32[16]{0:T(128)} %get-tuple-element.149.kvat, bf16[960,512]{1,0:T(8,128)(2,1)} %bitcast.167, s32[1,512]{1,0:T(1,128)} %bitcast.181, bf16[16,640,128]{2,1,0:T(8,128)(2,1)} %bitcast.209), custom_call_target="tpu_custom_call" | custom-call | flops 5000000000 | bytes 4000000 | tf_op jit(solution)/shard_map/attention_fwd/pallas_call | solution.py:78
  187.9 3.0 fusion.14
  190.9 4.7 fusion.13
  195.7 8.8 %multiply_convert_fusion = (bf16[2560,512]{1,0:T(8,128)(2,1)S(1)}, bf16[2560,512]{1,0:T(8,128)(2,1)}, bf16[2560,512]{1,0:T(8,128)(2,1)}) fusion(f32[2560,512]{1,0:T(8,128)} %fusion.13, f32[2560,512]{1,0:T(8,128)S(1)} %fusion.14, bf16[2560,960]{1,0:T(8,128)(2,1)S(1)} %bitcast.199, bf16[512,960]{0,1:T(8,128)(2,1)S(1)} %bitcast.141), kind=kOutput, calls=%fused_computation.3 | convolution fusion | flops 2537553920 | bytes 24248320 | tf_op jit(solution)/shard_map/dot_general | solution.py:21
  204.6 6.4 %add_convert_fusion = bf16[512,960]{0,1:T(8,128)(2,1)} fusion(f32[512,960]{0,1:T(8,128)S(1)} %get-tuple-element.151, bf16[2560,512]{1,0:T(8,128)(2,1)} %get-tuple-element.128, bf16[2560,960]{1,0:T(8,128)(2,1)S(1)} %bitcast.200), kind=kOutput, calls=%fused_computation.15 | convolution fusion | flops 2517565440 | bytes 10485760 | tf_op jit(solution)/shard_map/dot_general | solution.py:21
  211.0 2.7 fusion.15
  213.7 4.3 multiply_reduce_fusion
  218.0 3.3 reshape.456
  229.3 24.3 %attention_bwd.3 = (bf16[960,256]{1,0:T(8,128)(2,1)}, bf16[16,640,128]{2,1,0:T(8,128)(2,1)}) custom-call(s32[2,2]{1,0:T(2,128)} %bitcast.196, s32[16]{0:T(128)} %get-tuple-element.148.kvat, bf16[960,512]{1,0:T(8,128)(2,1)} %bitcast.168, bf16[960,512]{1,0:T(8,128)(2,1)} %convolution_convert_fusion.5.do_ref, bf16[960,512]{1,0:T(8,128)(2,1)} %copy-done.26, ...), custom_call_target="tpu_custom_call" | custom-call | flops 10000000000 | bytes 8000000 | tf_op jit(solution)/shard_map/attention_bwd/pallas_call | solution.py:179
  253.7 29.1 %attention_bwd.2 = (bf16[960,256]{1,0:T(8,128)(2,1)}, bf16[16,640,128]{2,1,0:T(8,128)(2,1)}) custom-call(s32[2,2]{1,0:T(2,128)} %bitcast.194, s32[16]{0:T(128)} %get-tuple-element.149.kvat, bf16[960,512]{1,0:T(8,128)(2,1)} %bitcast.169, bf16[960,512]{1,0:T(8,128)(2,1)} %convolution_convert_fusion.5.do_ref, bf16[960,512]{1,0:T(8,128)(2,1)} %copy-done.26, ...), custom_call_target="tpu_custom_call" | custom-call | flops 10000000000 | bytes 8000000 | tf_op jit(solution)/shard_map/attention_bwd/pallas_call | solution.py:179
  282.7 32.2 %sum_keys.1 = (bf16[1280,128]{1,0:T(8,128)(2,1)}, bf16[1280,128]{1,0:T(8,128)(2,1)}) custom-call(bf16[8,1280,128]{2,1,0:T(8,128)(2,1)} %bitcast.154, bf16[8,1280,128]{2,1,0:T(8,128)(2,1)} %bitcast.153), custom_call_target="tpu_custom_call" | custom-call | tf_op jit(solution)/shard_map/sum_keys/pallas_call | solution.py:557
  334.5 2.5 convolution_convert_fusion.3
  342.0 3.1 copy.118
  345.2 4.5 convolution_convert_fusion.2
  349.6 8.2 %copy.114 = bf16[2560,960]{1,0:T(8,128)(2,1)} copy(bf16[2560,960]{0,1:T(8,128)(2,1)} %convolution_convert_fusion.2) | data formatting | bytes 9830400 | tf_op jit(solution)/shard_map/convert_element_type | solution.py:729
  357.8 6.4 %convolution_convert_fusion = bf16[960,2560]{1,0:T(8,128)(2,1)} fusion(bf16[512,960]{0,1:T(8,128)(2,1)S(1)} %copy-done.20, bf16[2560,512]{1,0:T(8,128)(2,1)} %copy-done.36), kind=kOutput, calls=%fused_computation | convolution fusion | flops 2519040000 | bytes 8519680 | tf_op jit(solution)/shard_map/dot_general | solution.py:21
  364.2 4.4 convolution_convert_fusion.1
  368.6 125.0 %sum_weights.1 = (f32[320,960]{1,0:T(8,128)}, f32[120,2560]{1,0:T(8,128)}, f32[120,2560]{1,0:T(8,128)}, f32[120,960]{1,0:T(8,128)}, f32[120,960]{1,0:T(8,128)}, ...) custom-call(bf16[8,320,960]{2,1,0:T(8,128)(2,1)} %bitcast.136, bf16[8,120,2560]{2,1,0:T(8,128)(2,1)} %bitcast.140, ...), custom_call_target="tpu_custom_call" | custom-call | tf_op jit(solution)/shard_map/sum_weights/pallas_call | solution.py:557
  (170 shorter events, 79.0 us)
Async XLA Ops:
  0.6 11.0 %copy-start = (bf16[2,1,256,960]{2,3,1,0:T(8,128)(2,1)S(1)}, bf16[2,1,256,960]{2,3,1,0:T(8,128)(2,1)}, u32[]{:S(2)}) copy-start(bf16[2,1,256,960]{2,3,1,0:T(8,128)(2,1)} %param.13) | copy-start | bytes 2949124
  4.6 9.1 %copy-start.32 = (s32[2,2,128]{2,1,0:T(2,128)}, s32[2,2,128]{2,1,0:T(2,128)S(1)}, u32[]{:S(2)}) copy-start(s32[2,2,128]{2,1,0:T(2,128)S(1)} %select_reduce_fusion.1) | copy-start | bytes 6148
  11.7 99.6 %copy-start.16 = (f32[32,512]{1,0:T(8,128)}, f32[32,512]{1,0:T(8,128)S(1)}, u32[]{:S(2)}) copy-start(f32[32,512]{1,0:T(8,128)S(1)} %get-tuple-element.141.cos_ref) | copy-start | bytes 196612
  11.7 99.6 %copy-start.22 = (f32[32,512]{1,0:T(8,128)}, f32[32,512]{1,0:T(8,128)S(1)}, u32[]{:S(2)}) copy-start(f32[32,512]{1,0:T(8,128)S(1)} %get-tuple-element.140.sin_ref) | copy-start | bytes 196612
  13.7 2.7 copy-start.18
  17.6 206.0 %copy-start.6 = (bf16[120,8,2,256]{3,1,2,0:T(8,128)(2,1)}, bf16[120,8,2,256]{3,1,2,0:T(8,128)(2,1)S(1)}, u32[]{:S(2)}) copy-start(bf16[120,8,2,256]{3,1,2,0:T(8,128)(2,1)S(1)} %copy.124) | copy-start | bytes 2949124
  160.7 24.5 %copy-start.23 = (bf16[960,256]{1,0:T(8,128)(2,1)S(1)}, bf16[960,256]{1,0:T(8,128)(2,1)}, u32[]{:S(2)}) copy-start(bf16[960,256]{1,0:T(8,128)(2,1)} %get-tuple-element.44) | copy-start | bytes 1474564
  185.2 2.7 slice-start.2
  186.9 26.8 %copy-start.3 = (f32[512,960]{0,1:T(8,128)}, f32[512,960]{0,1:T(8,128)S(1)}, u32[]{:S(2)}) copy-start(f32[512,960]{0,1:T(8,128)S(1)} %get-tuple-element.151) | copy-start | bytes 5898244
  187.0 4.0 slice-start.4
  187.9 3.0 copy-start.19
  187.9 3.0 slice-start.5
  187.9 7.7 %slice-start = ((s8[5242880]{0:T(1024)(128)(4,1)}), s8[4194304]{0:T(1024)(128)(4,1)S(1)}, s32[]{:S(2)}) async-start(s8[5242880]{0:T(1024)(128)(4,1)} %bitcast.197), calls=%async_computation | async-start | bytes 8388608
  190.9 4.7 slice-start.1
  204.5 9.2 %copy-start.36 = (bf16[2560,512]{1,0:T(8,128)(2,1)}, bf16[2560,512]{1,0:T(8,128)(2,1)S(1)}, u32[]{:S(2)}) copy-start(bf16[2560,512]{1,0:T(8,128)(2,1)S(1)} %get-tuple-element.126) | copy-start | bytes 7864324
  204.5 6.5 %copy-start.38 = (bf16[2560,512]{1,0:T(8,128)(2,1)S(1)}, bf16[2560,512]{1,0:T(8,128)(2,1)}, u32[]{:S(2)}) copy-start(bf16[2560,512]{1,0:T(8,128)(2,1)} %get-tuple-element.127) | copy-start | bytes 7864324
  223.7 3.5 copy-start.35
  325.4 3.8 copy-start.9
  342.0 3.1 copy-start.7
  342.0 3.1 copy-start.37
  349.6 8.2 %copy-start.20 = (bf16[512,960]{0,1:T(8,128)(2,1)S(1)}, bf16[512,960]{0,1:T(8,128)(2,1)}, u32[]{:S(2)}) copy-start(bf16[512,960]{0,1:T(8,128)(2,1)} %copy-done.19) | copy-start | bytes 2949124
  357.8 6.4 %copy-start.39 = (bf16[2560,512]{1,0:T(8,128)(2,1)S(1)}, bf16[2560,512]{1,0:T(8,128)(2,1)}, u32[]{:S(2)}) copy-start(bf16[2560,512]{1,0:T(8,128)(2,1)} %get-tuple-element.127) | copy-start | bytes 7864324
  493.6 8.6 %copy-start.15 = (f32[120,2560]{1,0:T(8,128)S(1)}, f32[120,2560]{1,0:T(8,128)}, u32[]{:S(2)}) copy-start(f32[120,2560]{1,0:T(8,128)} %get-tuple-element.175) | copy-start | bytes 3686404
  498.4 4.8 copy-start.14
  (22 other events, 41.6 us)

commit v3 on v2

v3 whole, which is shorter than its diff:
```python
import functools

import jax
import jax.numpy as jnp
from jax import lax
from jax.experimental import pallas as pl
from jax.experimental.pallas import tpu as pltpu
from jax.sharding import PartitionSpec as P

HDIM = 64
BLOCK = 128
EPS = 1e-05
ROPE_BASE = 100000.0
NEG_FILL = -1e30
F32 = jnp.float32
BF16 = jnp.bfloat16
VMEM_LIMIT = 56 * 1024 * 1024


def dot(a, b, ca, cb):
    return lax.dot_general(a, b, (((ca,), (cb,)), ((), ())), preferred_element_type=F32)


def live_mask(qpos, start, p):
    kpos = p * BLOCK + lax.broadcasted_iota(jnp.int32, (BLOCK, BLOCK), 0)
    return (kpos <= qpos) & (kpos >= start)


STEP = 2


def pick(kv_ref, kvat, mb, qpos, start, b, t, share):
    nq = kv_ref.shape[2]
    blocks = [b - STEP * t - i for i in range(STEP)]
    slots = [kvat[mb, jnp.maximum(p, 0)] for p in blocks]
    at = [(lax.div(s, nq), lax.rem(s, nq)) for s in slots]
    ok = jnp.concatenate([live_mask(qpos, start, p) for p in blocks], axis=0)

    def keys(g):
        rows = slice(g * HDIM, (g + 1) * HDIM)
        return jnp.concatenate([kv_ref[d, 0, s, rows, :] for d, s in at], axis=1)

    return keys, at, jnp.concatenate([ok] * share, axis=1)


def fwd_kernel(groups, share, info, kvat, q_ref, start_ref, kv_ref, o_ref, lse_ref, qs, m_s, l_s, acc, s_s, w_s):
    mb, i = pl.program_id(0), pl.program_id(1)
    lo, b = info[mb, 0, i], info[mb, 1, i]
    nq = kv_ref.shape[2]
    lanes = share * BLOCK
    for g in range(groups):
        for h in range(share):
            at = (g * share + h) * HDIM
            qs[g, :, h * BLOCK : (h + 1) * BLOCK] = q_ref[at : at + HDIM, :]
    m_s[...] = jnp.full_like(m_s, NEG_FILL)
    l_s[...] = jnp.zeros_like(l_s)
    acc[...] = jnp.zeros_like(acc)
    qpos = b * BLOCK + lax.broadcasted_iota(jnp.int32, (1, BLOCK), 1)
    start = start_ref[...]

    def step(t, carry):
        keys, at, ok = pick(kv_ref, kvat, mb, qpos, start, b, t, share)
        for g in range(groups):
            s_s[g] = jnp.where(ok, dot(keys(g), qs[g], 0, 0), NEG_FILL)
        alphas = []
        for g in range(groups):
            s = s_s[g]
            m_old = m_s[g]
            m_new = jnp.maximum(m_old, jnp.max(s, axis=0, keepdims=True))
            w = jnp.exp(s - m_new)
            alpha = jnp.exp(m_old - m_new)
            l_s[g] = l_s[g] * alpha + jnp.sum(w, axis=0, keepdims=True)
            m_s[g] = m_new
            w_s[g] = w.astype(BF16)
            alphas.append(alpha)
        for g in range(groups):
            acc[g] = acc[g] * alphas[g] + dot(keys(groups + g), w_s[g], 1, 0)
        return carry

    lax.fori_loop(0, (b - lo + STEP) // STEP, step, 0)
    for g in range(groups):
        total = l_s[g]
        out = (acc[g] / total).astype(BF16)
        for h in range(share):
            at = (g * share + h) * HDIM
            o_ref[at : at + HDIM, :] = out[:, h * BLOCK : (h + 1) * BLOCK]
        lse_ref[0, g : g + 1, :] = m_s[g] + jnp.log(total)


def attention_fwd(info, kvat, q_t, start, kv):
    width = q_t.shape[0]
    n, micro, nq, kvw, _ = kv.shape
    groups = kvw // HDIM // 2
    share = width // HDIM // groups
    lanes = share * BLOCK
    tok = lambda rows: pl.BlockSpec((rows, BLOCK), lambda m, i, *_: (0, m * nq + i))
    return pl.pallas_call(
        functools.partial(fwd_kernel, groups, share),
        grid_spec=pltpu.PrefetchScalarGridSpec(
            num_scalar_prefetch=2,
            grid=(micro, nq),
            in_specs=[
                tok(width),
                tok(1),
                pl.BlockSpec((n, 1, nq, kvw, BLOCK), lambda m, i, *_: (0, m, 0, 0, 0)),
            ],
            out_specs=[
                tok(width),
                pl.BlockSpec((1, groups, lanes), lambda m, i, *_: (m * nq + i, 0, 0)),
            ],
            scratch_shapes=[
                pltpu.VMEM((groups, HDIM, lanes), BF16),
                pltpu.VMEM((groups, 1, lanes), F32),
                pltpu.VMEM((groups, 1, lanes), F32),
                pltpu.VMEM((groups, HDIM, lanes), F32),
                pltpu.VMEM((groups, STEP * BLOCK, lanes), F32),
                pltpu.VMEM((groups, STEP * BLOCK, lanes), BF16),
            ],
        ),
        out_shape=[
            jax.ShapeDtypeStruct(q_t.shape, BF16),
            jax.ShapeDtypeStruct((micro * nq, groups, lanes), F32),
        ],
        compiler_params=pltpu.CompilerParams(vmem_limit_bytes=VMEM_LIMIT),
        cost_estimate=pl.CostEstimate(
            flops=int(1e10), bytes_accessed=int(8e6), transcendentals=int(8e6)
        ),
        name="attention_fwd",
    )(info, kvat, q_t, start, kv)


def bwd_kernel(
    groups, share, info, kvat, q_ref, do_ref, o_ref, lse_ref, start_ref, cos_ref, sin_ref, kv_ref,
    dq_ref, dkv_ref, qs, dos, delta, dq, dkv, s_s, d_s, w_s, ds_s,
):
    mb, i = pl.program_id(0), pl.program_id(1)
    lo, b = info[mb, 0, i], info[mb, 1, i]
    nq = kv_ref.shape[2]

    @pl.when(i == 0)
    def _():
        dkv[...] = jnp.zeros_like(dkv)

    for g in range(groups):
        for h in range(share):
            at = (g * share + h) * HDIM
            cols = slice(h * BLOCK, (h + 1) * BLOCK)
            d_out = do_ref[at : at + HDIM, :]
            qs[g, :, cols] = q_ref[at : at + HDIM, :]
            dos[g, :, cols] = d_out
            delta[g, :, cols] = jnp.sum(
                d_out.astype(F32) * o_ref[at : at + HDIM, :].astype(F32), axis=0, keepdims=True
            )
    dq[...] = jnp.zeros_like(dq)
    qpos = b * BLOCK + lax.broadcasted_iota(jnp.int32, (1, BLOCK), 1)
    start = start_ref[...]

    def step(t, carry):
        keys, at, ok = pick(kv_ref, kvat, mb, qpos, start, b, t, share)
        for g in range(groups):
            s_s[g] = jnp.where(ok, dot(keys(g), qs[g], 0, 0), NEG_FILL)
            d_s[g] = dot(keys(groups + g), dos[g], 0, 0)
        for g in range(groups):
            w = jnp.exp(s_s[g] - lse_ref[0, g : g + 1, :])
            w_s[g] = w.astype(BF16)
            ds_s[g] = (w * (d_s[g] - delta[g])).astype(BF16)
        for g in range(groups):
            dq[g] += dot(keys(g), ds_s[g], 1, 0)
            dk = dot(qs[g], ds_s[g], 1, 1)
            dv = dot(dos[g], w_s[g], 1, 1)
            krows = slice(g * HDIM, (g + 1) * HDIM)
            vrows = slice((groups + g) * HDIM, (groups + g + 1) * HDIM)
            for i in range(STEP):
                cols = slice(i * BLOCK, (i + 1) * BLOCK)
                dkv[at[i][0], at[i][1], krows, :] += dk[:, cols]
                dkv[at[i][0], at[i][1], vrows, :] += dv[:, cols]
        return carry

    lax.fori_loop(0, (b - lo + STEP) // STEP, step, 0)
    cos, sin = cos_ref[...], sin_ref[...]
    half = HDIM // 2
    for g in range(groups):
        for h in range(share):
            at = (g * share + h) * HDIM
            one = dq[g, :half, h * BLOCK : (h + 1) * BLOCK] * HDIM**-0.5
            two = dq[g, half:, h * BLOCK : (h + 1) * BLOCK] * HDIM**-0.5
            dq_ref[at : at + half, :] = (one * cos + two * sin).astype(BF16)
            dq_ref[at + half : at + HDIM, :] = (two * cos - one * sin).astype(BF16)

    @pl.when(i == nq - 1)
    def _():
        dkv_ref[:, 0] = dkv[...].astype(BF16)


def attention_bwd(info, kvat, q_t, do_t, o_t, lse, start, cos_t, sin_t, kv):
    width = q_t.shape[0]
    n, micro, nq, kvw, _ = kv.shape
    groups = kvw // HDIM // 2
    share = width // HDIM // groups
    lanes = share * BLOCK
    tok = lambda rows: pl.BlockSpec((rows, BLOCK), lambda m, i, *_: (0, m * nq + i))
    keys = pl.BlockSpec((n, 1, nq, kvw, BLOCK), lambda m, i, *_: (0, m, 0, 0, 0))
    return pl.pallas_call(
        functools.partial(bwd_kernel, groups, share),
        grid_spec=pltpu.PrefetchScalarGridSpec(
            num_scalar_prefetch=2,
            grid=(micro, nq),
            in_specs=[
                tok(width),
                tok(width),
                tok(width),
                pl.BlockSpec((1, groups, lanes), lambda m, i, *_: (m * nq + i, 0, 0)),
                tok(1),
                tok(HDIM // 2),
                tok(HDIM // 2),
                keys,
            ],
            out_specs=[tok(width), keys],
            scratch_shapes=[
                pltpu.VMEM((groups, HDIM, lanes), BF16),
                pltpu.VMEM((groups, HDIM, lanes), BF16),
                pltpu.VMEM((groups, 1, lanes), F32),
                pltpu.VMEM((groups, HDIM, lanes), F32),
                pltpu.VMEM((n, nq, kvw, BLOCK), F32),
                pltpu.VMEM((groups, STEP * BLOCK, lanes), F32),
                pltpu.VMEM((groups, STEP * BLOCK, lanes), F32),
                pltpu.VMEM((groups, STEP * BLOCK, lanes), BF16),
                pltpu.VMEM((groups, STEP * BLOCK, lanes), BF16),
            ],
        ),
        out_shape=[
            jax.ShapeDtypeStruct(q_t.shape, BF16),
            jax.ShapeDtypeStruct(kv.shape, BF16),
        ],
        compiler_params=pltpu.CompilerParams(vmem_limit_bytes=VMEM_LIMIT),
        cost_estimate=pl.CostEstimate(
            flops=int(2e10), bytes_accessed=int(16e6), transcendentals=int(8e6)
        ),
        name="attention_bwd",
    )(info, kvat, q_t, do_t, o_t, lse, start, cos_t, sin_t, kv)


CORE, ALONG_X, ALONG_Y = 1, 2, 4
FAR = ALONG_X + ALONG_Y
CUBE = 8
LAG = 2
LAGS = 2
SEM = pltpu.SemaphoreType.DMA


def meet(peers):
    barrier = pltpu.get_barrier_semaphore()
    for peer in peers:
        pl.semaphore_signal(barrier, inc=1, device_id=peer, device_id_type=pl.DeviceIdType.MESH)
    pl.semaphore_wait(barrier, len(peers))


def gather_kernel(count, chunks, planes, *refs):
    ins, outs = refs[:count], refs[count : 2 * count]
    sent, came = refs[2 * count :]
    at, row = lax.axis_index("wide"), lax.axis_index("narrow")
    peer = {bit: (at ^ bit, row) for bit in (CORE, ALONG_X, ALONG_Y)}
    if planes:
        peer["row"] = (at, row ^ 1)

    def part(ref, c, half):
        return ref.at[chunks[c][1 + half]]

    def copy(c, m, half, way, slot):
        a = chunks[c][0]
        there = part(outs[a].at[at ^ m], c, half)
        return pltpu.make_async_remote_copy(
            src_ref=there if m else part(ins[a], c, half),
            dst_ref=there,
            send_sem=sent.at[c, slot],
            recv_sem=came.at[c, m if way == "row" else m ^ way, half],
            device_id=peer[way],
            device_id_type=pl.DeviceIdType.MESH,
        )

    def run(mine):
        other = 1 - mine
        used = [0] * len(chunks)
        begun = []

        def push(c, m, half, way):
            r = copy(c, m, half, way, used[c])
            used[c] += 1
            r.start()
            begun.append(r)

        def take(c, m, half, *ways):
            copy(c, m ^ CORE, half, CORE, 0).wait_recv()
            for way in ways:
                push(c, m, half, way)

        def first(c):
            push(c, 0, mine, ALONG_X)
            push(c, 0, mine, ALONG_Y)
            if not planes:
                push(c, 0, other, ALONG_X)
                push(c, 0, other, ALONG_Y)

        def second(c):
            if planes:
                take(c, ALONG_Y, mine, ALONG_X, CORE)
                push(c, 0, other, ALONG_Y)
                take(c, ALONG_X, mine, "row", CORE)
            else:
                take(c, ALONG_X, mine, ALONG_Y, CORE)
                take(c, ALONG_Y, other, ALONG_X, CORE)
                take(c, ALONG_Y, mine, CORE)
                take(c, ALONG_X, other, CORE)
            push(c, 0, 0, CORE)
            push(c, 0, 1, CORE)

        def third(c):
            take(c, FAR, mine, *(("row", CORE) if planes else (CORE,)))
            if planes:
                take(c, ALONG_Y, other, CORE)
                take(c, ALONG_X, other, CORE)
            else:
                take(c, FAR, other, CORE)

        def fourth(c):
            if planes:
                take(c, FAR, other, CORE)

        def fifth(c):
            for half in range(2):
                take(c, CORE, half, CORE)
            for m in (ALONG_X, ALONG_Y, FAR):
                for half in range(2):
                    take(c, m + CORE, half)

        def sixth(c):
            for half in range(2):
                take(c, 0, half)

        steps = (first, second, third, fourth, fifth, sixth)
        for t in range(len(chunks) + LAG * (len(steps) - 1)):
            for s, step in enumerate(steps):
                if 0 <= t - LAG * s < len(chunks):
                    step(t - LAG * s)
        for r in begun:
            r.wait_send()

    meet(list(peer.values()))
    if planes:
        for mine in range(2):
            pl.when(row % 2 == mine)(functools.partial(run, mine))
    else:
        run(0)


def gather(arrays, chunks, planes, collective_id):
    count = len(arrays)
    return pl.pallas_call(
        functools.partial(gather_kernel, count, chunks, planes),
        in_specs=[pl.BlockSpec(memory_space=pl.ANY)] * count,
        out_specs=[pl.BlockSpec(memory_space=pl.ANY)] * count,
        out_shape=[jax.ShapeDtypeStruct((8,) + a.shape, a.dtype) for a in arrays],
        scratch_shapes=[
            SEM((len(chunks), 16)),
            SEM((len(chunks), 8, 2)),
        ],
        compiler_params=pltpu.CompilerParams(collective_id=collective_id, has_side_effects=True),
        name="gather_rows" if planes else "gather_keys",
    )(*arrays)


def weight_chunks(shapes, most=160 * 1024):
    chunks = []
    for a, (rows, cols) in enumerate(shapes):
        n = 1
        while rows * cols // n > most and rows % (32 * n) == 0:
            n *= 2
        k = 1
        while rows // n * cols // k > most and cols % (256 * k) == 0:
            k *= 2
        for i in range(n):
            lo, hi = rows // n * i, rows // n * (i + 1)
            mid = lo + -(-(hi - lo) // 32) * 16
            for j in range(k):
                c = pl.ds(cols // k * j, cols // k)
                chunks.append((a, (pl.ds(lo, mid - lo), c), (pl.ds(mid, hi - mid), c)))
    return chunks


def key_chunks(micro, blocks, rows, parts=2):
    return [
        (0,) + tuple(
            (m, pl.ds(blocks // 2 * h, blocks // 2), pl.ds(rows // parts * i, rows // parts))
            for h in range(2)
        )
        for m in range(micro)
        for i in range(parts)
    ]


def pieces_of(total, size):
    return [(lo, min(size, total - lo)) for lo in range(0, total, size)]


class Unit:
    def __init__(self, source, target, out, rows, cols, first):
        self.source, self.target, self.out = source, target, out
        self.rows, self.cols, self.first = rows, cols, first

    @property
    def shape(self):
        return (self.rows[1], self.cols[1])


def weight_units(sizes, most):
    units = []
    for source, target, out, rows, cols in sizes:
        k = 1
        while cols % (256 * k) == 0 and rows * cols // k > most:
            k *= 2
        high = -(-rows // max(1, round(rows * cols / k / most)) // 16) * 16
        for rows_cut in pieces_of(rows, high):
            for cols_cut in pieces_of(cols, cols // k):
                first = (ALONG_X, ALONG_Y)[len(units) % 2]
                units.append(Unit(source, target, out, rows_cut, cols_cut, first))
    return units


RING = 3


def ring_sizes(units):
    shapes = [u.shape for u in units if u.source is not None]
    return {a: min(RING, shapes.count(a)) for a in shapes}


def sum_kernel(units, n_src, n_tgt, n_out, tail, *refs):
    refs = list(refs)
    take = lambda n: [refs.pop(0) for _ in range(n)]
    far_src, far_tgt = take(n_src), take(n_tgt)
    if tail:
        far_keys, far_w, far_x, far_res = take(1)[0], take(3), *take(2)
        cos_ref, sin_ref, rr_ref, gain_ref, gain_two = take(5)
    outs = take(n_out)
    if tail:
        far_grad, total = take(2)
    n = len(units)
    held, core_in, one_in, two_in, line_in = (take(n) for _ in range(5))
    src, tgt = take(n_src), take(n_tgt)
    lhs = take(1)[0]
    depth = ring_sizes(units)
    rings = dict(zip(depth, take(len(depth))))
    load_src, load_tgt, sent, came, stored = take(5)
    if tail:
        dkv, w, x, res, dx, grad, gain_buf, key_load, tail_load, key_sent, key_came, gain_sent, gain_came = (
            *take(1), take(3), *take(11)
        )
    at, row = lax.axis_index("wide"), lax.axis_index("narrow")
    way = {bit: (at ^ bit, row) for bit in (CORE, ALONG_X, ALONG_Y)}
    near, across = (at, row ^ 1), (at, row ^ 3)
    middle = (row == 1) | (row == 2)
    is_keys = [u.source is None for u in units]

    loads = [pltpu.make_async_copy(a, b, load_src.at[i]) for i, (a, b) in enumerate(zip(far_src, src))]
    loads_tgt = [pltpu.make_async_copy(a, b, load_tgt.at[i]) for i, (a, b) in enumerate(zip(far_tgt, tgt))]
    tail_loads = []
    if tail:
        tail_loads = [
            pltpu.make_async_copy(a, b, tail_load.at[i])
            for i, (a, b) in enumerate(zip([*far_w, far_x, far_res], [*w, x, res]))
        ]
    ready = set()

    def need(copies, i):
        if (id(copies), i) not in ready:
            ready.add((id(copies), i))
            copies[i].wait()

    def send(c, slot, a, b, to):
        return pltpu.make_async_remote_copy(
            src_ref=a, dst_ref=b, send_sem=sent.at[c, slot], recv_sem=came.at[c, slot],
            device_id=to, device_id_type=pl.DeviceIdType.MESH,
        )

    def add(dst, other):
        rows = dst.shape[-2]
        most = rows // 16
        step = 16 * max(k for k in (1, 2, 3, 4) if most % k == 0)

        def body(i, carry):
            cut = pl.ds(pl.multiple_of(i * step, 16), step)
            dst[cut, :] = dst[cut, :] + other[cut, :]
            return carry

        lax.fori_loop(0, most * 16 // step, body, 0)
        if rows % 16:
            cut = slice(most * 16, rows)
            dst[cut, :] = dst[cut, :] + other[cut, :]

    def order(c):
        first = units[c].first
        return (0, FAR - first, first, FAR)

    def slot_of(c):
        alike = [i for i in range(n) if not is_keys[i] and units[i].shape == units[c].shape]
        return alike.index(c) % depth[units[c].shape]

    def same_slot(i, c):
        alike = not is_keys[i] and not is_keys[c] and units[i].shape == units[c].shape
        return alike and slot_of(i) == slot_of(c)

    def core_copies(c):
        if is_keys[c]:
            rows = pl.ds(*units[c].rows)
            return [
                pltpu.make_async_remote_copy(
                    src_ref=far_keys.at[at ^ CORE ^ m, rows], dst_ref=core_in[c].at[i],
                    send_sem=key_sent.at[c, i], recv_sem=key_came.at[c, i],
                    device_id=way[CORE], device_id_type=pl.DeviceIdType.MESH,
                )
                for i, m in enumerate(order(c))
            ]
        return [send(c, 0, rings[units[c].shape].at[slot_of(c)], core_in[c], way[CORE])]

    def key_loads(c):
        rows = pl.ds(*units[c].rows)
        return [
            pltpu.make_async_copy(far_keys.at[at ^ m, rows], held[c].at[i], key_load.at[c, i])
            for i, m in enumerate(order(c))
        ]

    def first_copy(c):
        return send(c, 1, held[c].at[pl.ds(2, 2)], one_in[c], way[units[c].first])

    def second_copy(c):
        return send(c, 2, held[c].at[1], two_in[c], way[FAR - units[c].first])

    def inward(c):
        return send(c, 3, held[c].at[0], line_in[c].at[0], near)

    def over(c):
        return send(c, 4, held[c].at[0], line_in[c].at[1], across)

    def outward(c):
        return send(c, 3, line_in[c].at[1], line_in[c].at[0], near)

    def store(c, slot):
        cut = (pl.ds(*units[c].rows), pl.ds(*units[c].cols))
        return pltpu.make_async_copy(line_in[c].at[slot], outs[units[c].out].at[cut], stored.at[c])

    def products(c, mine):
        u = units[c]
        rows, cols = u.shape
        whole = pl.ds(*u.rows)
        if u.source is not None:
            need(loads, u.source)
        b = dkv if u.target is None else tgt[u.target]
        if u.target is not None:
            need(loads_tgt, u.target)
        for i, m in enumerate(order(c)):
            lhs[pl.ds(i * rows, rows), :] = src[u.source][at ^ m ^ mine, whole, :]
        a = lhs[pl.ds(0, 4 * rows), :]
        into = (lambda cut: held[c].at[:, :, cut]) if mine == 0 else (
            lambda cut: rings[u.shape].at[slot_of(c), :, :, cut]
        )

        def one(lo, size, start):
            got = dot(a, b[pl.ds(start, size), :], 1, 1).astype(BF16)
            into(lo)[...] = got.reshape(4, rows, size)

        for lo, size in pieces_of(cols, 256):
            one(pl.ds(lo, size), size, u.cols[0] + lo)

    def s0(c):
        if is_keys[c]:
            for r in core_copies(c) + key_loads(c):
                r.start()
            return
        before = [i for i in range(c) if same_slot(i, c)]
        if before:
            core_copies(before[-1])[0].wait_send()
        products(c, CORE)
        core_copies(c)[0].start()
        products(c, 0)

    def s1(c):
        if is_keys[c]:
            for r in key_loads(c):
                r.wait()
        for r in core_copies(c):
            r.wait_recv()
        for i in (2, 3, 0, 1):
            add(held[c].at[i], core_in[c].at[i])
            if i == 3:
                first_copy(c).start()

    def s2(c):
        first_copy(c).wait_recv()
        add(held[c].at[1], one_in[c].at[1])
        second_copy(c).start()
        add(held[c].at[0], one_in[c].at[0])

    def s3(c):
        second_copy(c).wait_recv()
        add(held[c].at[0], two_in[c])
        if is_keys[c]:
            keys_done(c)
        else:
            pl.when(~middle)(lambda: inward(c).start())

    def s4(c):
        @pl.when(middle)
        def _():
            inward(c).wait_recv()
            add(held[c].at[0], line_in[c].at[0])
            over(c).start()

    def s5(c):
        @pl.when(middle)
        def _():
            over(c).wait_recv()
            add(line_in[c].at[1], held[c].at[0])
            outward(c).start()
            store(c, 1).start()

    def s6(c):
        @pl.when(~middle)
        def _():
            outward(c).wait_recv()
            store(c, 0).start()

    def keys_done(c):
        lanes = slice(c * BLOCK, (c + 1) * BLOCK)
        cs, sn = cos_ref[:, lanes], sin_ref[:, lanes]
        half, kd = HDIM // 2, dkv.shape[0] // 2
        for h in range(0, kd, HDIM):
            one = held[c][0, h : h + half, :].astype(F32)
            two = held[c][0, h + half : h + HDIM, :].astype(F32)
            dkv[h : h + half, lanes] = (one * cs + two * sn).astype(BF16)
            dkv[h + half : h + HDIM, lanes] = (two * cs - one * sn).astype(BF16)
        dkv[kd:, lanes] = held[c][0, kd:, :]

    def input_grad():
        for i in range(len(tail_loads)):
            need(tail_loads, i)
        kd = dkv.shape[0] // 2
        width = x.shape[0]
        rr = rr_ref[...]
        mean = jnp.zeros_like(rr)
        for lo, size in pieces_of(width, 128):
            cut = slice(lo, lo + size)
            d = dot(w[0][cut, :], tgt[0][...], 1, 0)
            d += dot(w[1][cut, :], dkv[:kd, :], 1, 0)
            d += dot(w[2][cut, :], dkv[kd:, :], 1, 0)
            dx[cut, :] = d
            xf = x[cut, :].astype(F32)
            p = d * xf
            mean += jnp.sum(p * gain_ref[cut, :], axis=0, keepdims=True)
            g = jnp.sum(p * rr, axis=1, keepdims=True)
            gain_buf[0, 0:1, cut] = jnp.broadcast_to(g, (size, BLOCK)).T[0:1]
        gain_buf[0, 1:2, :] = gain_two[...]
        mean = mean * (rr * rr * rr / width)
        for lo, size in pieces_of(width, 128):
            cut = slice(lo, lo + size)
            g = res[cut, :] + rr * (dx[cut, :] * gain_ref[cut, :]) - x[cut, :].astype(F32) * mean
            grad[:, cut] = g.T
        pltpu.make_async_copy(grad, far_grad, tail_load.at[len(tail_loads)]).start()

    gain_ways = [way[CORE], way[ALONG_X], way[ALONG_Y], near, across]

    def gain_copy(i):
        return pltpu.make_async_remote_copy(
            src_ref=gain_buf.at[2 * i], dst_ref=gain_buf.at[2 * i + 1], send_sem=gain_sent.at[i],
            recv_sem=gain_came.at[i], device_id=gain_ways[i], device_id_type=pl.DeviceIdType.MESH,
        )

    def gain_step(i):
        if i:
            gain_copy(i - 1).wait_recv()
            gain_buf[2 * i] = gain_buf[2 * i - 2] + gain_buf[2 * i - 1]
        if i < len(gain_ways):
            gain_copy(i).start()

    for r in loads + loads_tgt + tail_loads:
        r.start()
    meet([*way.values(), near, across])
    steps = (s0, s1, s2, s3, s4, s5, s6)
    begins, after = [], 0
    for c in range(n):
        begins.append(c if not begins else begins[-1] + 1)
        if is_keys[c]:
            after = begins[-1] + 3 * LAGS + 1
        elif units[c].target is None:
            begins[-1] = max(begins[-1], after)
    gains_at = 0
    for t in range(begins[-1] + LAGS * (len(steps) - 1) + 1):
        for s, step in enumerate(steps):
            for c in range(n):
                if begins[c] + LAGS * s == t and not (is_keys[c] and s > 3):
                    step(c)
        if tail and t == after:
            input_grad()
        if tail and t >= after and gains_at <= len(gain_ways):
            gain_step(gains_at)
            gains_at += 1
    if tail:
        for i in range(gains_at, len(gain_ways) + 1):
            gain_step(i)
        total[...] = gain_buf[2 * len(gain_ways)]
    for c in range(n):
        if not any(same_slot(c, i) for i in range(c + 1, n)):
            for r in core_copies(c):
                r.wait_send()
        first_copy(c).wait_send()
        second_copy(c).wait_send()
        if not is_keys[c]:
            inward(c).wait_send()
            pl.when(middle)(lambda: over(c).wait_send())
            store(c, 0).wait()
    if tail:
        for i in range(len(gain_ways)):
            gain_copy(i).wait_send()
        pltpu.make_async_copy(grad, far_grad, tail_load.at[len(tail_loads)]).wait()


def sums(units, sources, targets, out_shapes, collective_id, tail=None):
    n = len(units)
    anywhere = pl.BlockSpec(memory_space=pl.ANY)
    vmem = pl.BlockSpec(memory_space=pltpu.VMEM)
    room = lambda *lead: [pltpu.VMEM(lead + u.shape, BF16) for u in units]
    line = [pltpu.VMEM((2,) + u.shape if u.source is not None else (8, BLOCK), BF16) for u in units]
    tokens = sources[0].shape[2]
    rows = max(u.shape[0] for u in units if u.source is not None)
    scratch = room(4) + room(4) + room(2) + room() + line
    scratch += [pltpu.VMEM(a.shape, BF16) for a in (*sources, *targets)]
    scratch += [pltpu.VMEM((4 * rows, tokens), BF16)]
    scratch += [pltpu.VMEM((d, 4) + a, BF16) for a, d in ring_sizes(units).items()]
    scratch += [SEM((len(sources),)), SEM((len(targets),)), SEM((n, 5)), SEM((n, 5)), SEM((n,))]
    args = [*sources, *targets]
    specs = [anywhere] * len(args)
    out_shape = [jax.ShapeDtypeStruct(s, BF16) for s in out_shapes]
    out_specs = [anywhere] * len(out_shapes)
    if tail:
        big, small = tail[:6], tail[6:]
        args += [*big, *small]
        specs += [anywhere] * len(big) + [vmem] * len(small)
        width = big[4].shape[0]
        out_shape += [jax.ShapeDtypeStruct((tokens, width), F32), jax.ShapeDtypeStruct((2, width), F32)]
        out_specs += [anywhere, vmem]
        scratch += [pltpu.VMEM((big[0].shape[1] * BLOCK // tokens, tokens), BF16)]
        scratch += [pltpu.VMEM(a.shape, a.dtype) for a in big[1:]]
        scratch += [pltpu.VMEM((width, tokens), F32), pltpu.VMEM((tokens, width), F32)]
        scratch += [pltpu.VMEM((11, 2, width), F32), SEM((n, 4)), SEM((6,)), SEM((n, 4)), SEM((n, 4))]
        scratch += [SEM((5,)), SEM((5,))]
    return pl.pallas_call(
        functools.partial(sum_kernel, units, len(sources), len(targets), len(out_shapes), bool(tail)),
        in_specs=specs,
        out_specs=out_specs,
        out_shape=out_shape,
        scratch_shapes=scratch,
        compiler_params=pltpu.CompilerParams(
            collective_id=collective_id, has_side_effects=True, vmem_limit_bytes=60 * 1024 * 1024
        ),
        name="sum_with_keys" if tail else "sum_weights",
    )(*args)


def row_sum(part, size):
    if size != 4:
        return lax.psum(part, "narrow")
    add = lambda a, b: (a.astype(F32) + b.astype(F32)).astype(BF16)
    part = add(part, lax.ppermute(part, "narrow", [(0, 1), (3, 2)]))
    part = add(part, lax.ppermute(part, "narrow", [(1, 2), (2, 1)]))
    back = lax.ppermute(part, "narrow", [(1, 0), (2, 3)])
    at = lax.axis_index("narrow")
    return jnp.where((at == 1) | (at == 2), part, back)


def turn(v, cos, sin):
    heads = v.reshape(-1, 2, HDIM // 2, v.shape[1])
    one, two = heads[:, 0], heads[:, 1]
    return jnp.stack([one * cos - two * sin, two * cos + one * sin], axis=1).reshape(v.shape)


def turn_back(v, cos, sin):
    return turn(v, cos, -sin)


def shards(sizes, tokens, lengths, block_plan, attn_gain, w_query, w_key, w_value, w_out, ffn_gain,
           w_gate, w_up, w_down, cotangent):
    n = sizes["wide"]
    at = lax.axis_index("wide")
    micro, _, slots, width = tokens.shape
    total = micro * slots
    kd = w_key.shape[1]
    ff = w_gate.shape[1]
    nq = slots // BLOCK
    nb = nq * n

    plan = block_plan[:, 0]
    sizes_of = lengths[:, 0]
    docs = sizes_of.shape[1]
    upto = jnp.arange(docs)[:, None] >= jnp.arange(docs)[None, :]
    ends = jnp.sum(jnp.where(upto[None], sizes_of[:, None, :], 0), axis=2)
    own_plan = lax.dynamic_slice_in_dim(plan, at * nq, nq, axis=1)
    position = own_plan[:, :, None] * BLOCK + jnp.arange(BLOCK, dtype=jnp.int32)
    start = jnp.sum(
        jnp.where(position[..., None] >= ends[:, None, None, :], sizes_of[:, None, None, :], 0), axis=3
    )
    info = jnp.stack([start[:, :, 0] // BLOCK, own_plan], axis=1)
    slot_block = jnp.arange(nb, dtype=jnp.int32)
    where_is = jnp.sum(
        jnp.where(plan[:, None, :] == slot_block[None, :, None], slot_block[None, None, :], 0), axis=2
    )
    start = start.reshape(1, total)
    local = position.reshape(1, total) - start
    frequency = ROPE_BASE ** (-2.0 * jnp.arange(HDIM // 2, dtype=F32) / HDIM)
    angles = frequency[:, None] * local.astype(F32)
    cos, sin = jnp.cos(angles), jnp.sin(angles)

    cube = n == CUBE and sizes["narrow"] == 4 and nq % 2 == 0

    def whole_rows(*shards_of):
        if cube:
            got = gather(shards_of, weight_chunks([a.shape for a in shards_of]), True, 1)
        else:
            got = [lax.all_gather(a, "wide", axis=0) for a in shards_of]
        return [a.reshape(-1, a.shape[2]) for a in got]

    def whole_keys(own):
        if cube:
            return gather([own], key_chunks(*own.shape[:3]), False, 2)[0]
        return lax.all_gather(own, "wide", axis=0)

    def shared(a):
        return a.reshape(n, -1, a.shape[1])

    def row_part(source, target):
        part = dot(source, target, 1, 1).astype(BF16)
        own = lax.psum_scatter(part, "wide", scatter_dimension=0, tiled=True)
        return row_sum(own, sizes["narrow"])

    x_t = tokens.reshape(total, width).T
    ct_t = cotangent.reshape(total, width).T
    x = x_t.astype(F32)

    g_query, g_key, g_value, g_out, g_gate, g_up, g_down = whole_rows(
        w_query, w_key, w_value, w_out, w_gate, w_up, w_down
    )
    rr1 = lax.rsqrt(jnp.mean(x * x, axis=0, keepdims=True) + EPS)
    xn = (x * rr1 * attn_gain[:, None]).astype(BF16)
    key_t = turn(dot(g_key, xn, 0, 0), cos, sin).astype(BF16)
    value_t = dot(g_value, xn, 0, 0).astype(BF16)
    own_kv = jnp.concatenate([key_t, value_t]).reshape(2 * kd, micro, nq, BLOCK).transpose(1, 2, 0, 3)
    q_t = (turn(dot(g_query, xn, 0, 0), cos, sin).astype(BF16) * HDIM**-0.5).astype(BF16)

    kv = whole_keys(own_kv)
    att_t, lse = attention_fwd(info, where_is, q_t, start, kv)

    res = x + dot(g_out, att_t, 0, 0)
    rr2 = lax.rsqrt(jnp.mean(res * res, axis=0, keepdims=True) + EPS)
    hn = (res * rr2 * ffn_gain[:, None]).astype(BF16)
    gate = dot(g_gate, hn, 0, 0)
    up = dot(g_up, hn, 0, 0)
    sg = 1.0 / (1.0 + jnp.exp(-gate))
    hidden = (gate * sg * up).astype(BF16)
    out = (res + dot(g_down, hidden, 0, 0)).astype(BF16).T

    d_hidden = dot(g_down, ct_t, 1, 0)
    d_gate = (d_hidden * up * sg * (1.0 + gate * (1.0 - sg))).astype(BF16)
    d_up = (d_hidden * gate * sg).astype(BF16)
    d_hn = dot(g_gate, d_gate, 1, 0) + dot(g_up, d_up, 1, 0)
    u = d_hn * ffn_gain[:, None]
    d_res = (
        ct_t.astype(F32) + rr2 * u - res * rr2**3 * jnp.mean(u * res, axis=0, keepdims=True)
    )
    gain_two = jnp.sum(d_hn * res * rr2, axis=1)
    d_attn = d_res.astype(BF16)
    do_t = dot(g_out, d_attn, 1, 0).astype(BF16)

    pairs = [(hidden, ct_t), (hn, d_gate), (hn, d_up), (att_t, d_attn)]
    if cube:
        units = weight_units(
            [(0, 0, 0, ff // n, width), (1, 1, 1, width // n, ff), (1, 2, 2, width // n, ff),
             (2, 3, 3, width // n, width)], 80 * 1024,
        )
        s_down, s_gate, s_up, s_out = sums(
            units,
            [shared(hidden), shared(hn), shared(att_t)],
            [ct_t, d_gate, d_up, d_attn],
            [(ff // n, width), (width // n, ff), (width // n, ff), (width // n, width)],
            3,
        )
    else:
        s_down, s_gate, s_up, s_out = [row_part(*p) for p in pairs]

    dq, dkv = attention_bwd(info, where_is, q_t, do_t, att_t, lse, start, cos, sin, kv)
    if cube:
        blocks = micro * nq
        keys = dkv.reshape(n, blocks * 2 * kd, BLOCK)
        units = [
            Unit(None, None, None, (2 * kd * i, 2 * kd), (0, BLOCK), (ALONG_X, ALONG_Y)[i % 2])
            for i in range(blocks)
        ] + weight_units(
            [(0, 0, 0, width // n, width), (0, None, 1, width // n, 2 * kd)], 80 * 1024
        )
        s_query, s_kv, grad_x, gains = sums(
            units,
            [shared(xn)],
            [dq],
            [(width // n, width), (width // n, 2 * kd)],
            4,
            (keys, g_query, g_key, g_value, x_t, d_res, cos, sin, rr1, attn_gain[:, None], gain_two[None]),
        )
        s_key, s_value = s_kv[:, :kd], s_kv[:, kd:]
    else:
        dkv = lax.psum_scatter(dkv, "wide", scatter_dimension=0).transpose(2, 0, 1, 3).reshape(2 * kd, total)
        dk = turn_back(dkv[:kd].astype(F32), cos, sin).astype(BF16)
        dv = dkv[kd:]
        d_xn = dot(g_query, dq, 1, 0) + dot(g_key, dk, 1, 0) + dot(g_value, dv, 1, 0)
        u = d_xn * attn_gain[:, None]
        grad_x = (d_res + rr1 * u - x * rr1**3 * jnp.mean(u * x, axis=0, keepdims=True)).T
        gain_one = jnp.sum(d_xn * x * rr1, axis=1)
        s_query, s_key, s_value = row_part(xn, dq), row_part(xn, dk), row_part(xn, dv)
        gains = lax.psum(jnp.stack([gain_one, gain_two]), ("wide", "narrow"))

    shape = (micro, 1, slots, width)
    wide_out = lambda a: a.astype(F32)
    return (
        out.reshape(shape),
        grad_x.reshape(shape),
        gains[0],
        wide_out(s_query),
        wide_out(s_key),
        wide_out(s_value),
        wide_out(s_out),
        gains[1],
        wide_out(s_gate),
        wide_out(s_up),
        wide_out(s_down),
    )


def solution(mesh):
    by_slot = P(None, "narrow", "wide", None)
    by_row = P(None, "narrow", None)
    split = P("wide", None)
    in_specs = (
        by_slot, by_row, by_row, P(), split, split, split, split, P(), split, split, split, by_slot,
    )
    out_specs = (
        by_slot, by_slot, P(), split, split, split, split, P(), split, split, split,
    )
    return jax.shard_map(
        functools.partial(shards, dict(mesh.shape)),
        mesh=mesh,
        in_specs=in_specs,
        out_specs=out_specs,
        check_vma=False,
    )
```

time: 511 us -> 415 us (0.81)
  local copies, waits for them, and re-layouts: 67.8 us -> 21.3 us
  matrix products: 68.7 us -> 41.2 us
  Pallas kernels: 353 us -> 331 us
    pallas_call x2, Pallas kernels: 157 us -> 202 us  [sums(): pl.pallas_call(functools.partial(sum_kernel, units, len(sources), len(tar...]
    pallas_call x2 -> x1, Pallas kernels: 53.4 us -> 17.2 us  [attention_bwd(): pl.pallas_call(functools.partial(bwd_kernel, groups, share), grid_spec=pl...]
    pallas_call x2 -> x1, Pallas kernels: 42.5 us -> 11.2 us  [attention_fwd(): pl.pallas_call(functools.partial(fwd_kernel, groups, share), grid_spec=pl...]
    dot_general x21 -> x11, matrix products: 68.7 us -> 41.2 us  [dot(): lax.dot_general(a, b, (((ca,), (cb,)), ((), ())), preferred_element_type=...]
    unnamed x110 -> x80, local copies, waits for them, and re-layouts: 28.1 us -> 11.5 us
    convert_element_type x6 -> x0, local copies, waits for them, and re-layouts: 15.2 us -> none  [the longest x3 11.6 us: shards(): part = lambda a, b, ca, cb: dot(a, b, ca, cb).astype(BF16)]
    convert_element_type x2 -> x9, other arithmetic: 1.24 us -> 10.3 us  [the longest x6 7.38 us: shards(): wide_out = lambda a: a.astype(F32)]
    reshape x5 -> x0, local copies, waits for them, and re-layouts: 5.22 us -> none  [the longest x1 2.52 us: shards(): grad_x.reshape(shape)]
where the time goes in v3:
time: 415 us; the launch traced here: 410 us
  Pallas kernels  331 us (80%)
  matrix products  41.2 us (10%)
  local copies, waits for them, and re-layouts  21.3 us (5%)
  other arithmetic  15.4 us (4%)
    pallas_call x2, Pallas kernels, sums(): pl.pallas_call(functools.partial(sum_kernel, units, len(sources), len(tar...  202 us
    pallas_call x2, Pallas kernels, gather(): pl.pallas_call(functools.partial(gather_kernel, count, chunks, planes), i...  99.7 us
    dot_general x11, matrix products, dot(): lax.dot_general(a, b, (((ca,), (cb,)), ((), ())), preferred_element_type=...  41.2 us
    pallas_call x1, Pallas kernels, attention_bwd(): pl.pallas_call(functools.partial(bwd_kernel, groups, share), grid_spec=pl...  17.2 us
    unnamed x80, local copies, waits for them, and re-layouts  11.5 us
    pallas_call x1, Pallas kernels, attention_fwd(): pl.pallas_call(functools.partial(fwd_kernel, groups, share), grid_spec=pl...  11.2 us

profile of v3, /device:TPU:0, one launch (start us, length us, event | category | flops | bytes accessed | tf_op | source)
XLA Modules:
  0.0 410.1 jit_solution(1086819194252511931)
XLA Ops:
  0.6 2.2 copy.74
  5.7 70.9 %gather_rows.1 = (bf16[8,120,960]{2,1,0:T(8,128)(2,1)}, bf16[8,120,320]{2,1,0:T(8,128)(2,1)}, bf16[8,120,320]{2,1,0:T(8,128)(2,1)}, bf16[8,120,960]{2,1,0:T(8,12...) custom-call(bf16[120,960]{1,0:T(8,128)(2,1)} %refs_0_.1, ...), custom_call_target="tpu_custom_call" | custom-call | tf_op jit(solution)/shard_map/gather_rows/pallas_call | solution.py:358
  76.7 1.4 copy.82
  78.1 1.3 fusion.5
  83.5 28.7 %gather_keys.1.kv_ref = bf16[8,2,2,640,128]{4,3,2,1,0:T(8,128)(2,1)} custom-call(bf16[2,2,640,128]{3,2,1,0:T(8,128)(2,1)} %bitcast.126), custom_call_target="tpu_custom_call" | custom-call | tf_op jit(solution)/shard_map/gather_keys/pallas_call | solution.py:358
  112.3 2.8 copy.81
  115.1 3.0 fusion.7
  121.1 11.2 %attention_fwd.1 = (bf16[960,512]{1,0:T(8,128)(2,1)}, f32[4,5,384]{2,1,0:T(8,128)}) custom-call(s32[2,2,2]{2,1,0:T(2,128)} %pad_add_fusion.info, s32[2,16]{1,0:T(2,128)} %select_reduce_fusion.kvat, bf16[960,512]{1,0:T(8,128)(2,1)} %bitcast.130, s32[1,512]{1,0:T(1,128)} %bitcast.137, bf16[8,2,2,640,128]{4,3,2,1,0:T(8,128)(2,1)} %gather_keys.1.kv_ref), custom_call_target="tpu_custom_call" | custom-call | flops 10000000000 | bytes 8000000 | tf_op jit(solution)/shard_map/attention_fwd/pallas_call | solution.py:97
  132.3 2.4 multiply_reduce_fusion.2
  135.2 4.7 %fusion.12 = f32[2560,512]{1,0:T(8,128)} fusion(bf16[960,2560]{1,0:T(8,128)(2,1)S(1)} %bitcast.156, bf16[960,512]{1,0:T(8,128)(2,1)S(1)} %multiply_convert_fusion.3), kind=kOutput, calls=%fused_computation.59 | convolution fusion | flops 2516582400 | bytes 11141120 | tf_op jit(solution)/shard_map/dot_general | solution.py:21
  139.8 4.6 %fusion.11 = f32[2560,512]{1,0:T(8,128)} fusion(bf16[960,2560]{1,0:T(8,128)(2,1)S(1)} %bitcast.160, bf16[960,512]{1,0:T(8,128)(2,1)S(1)} %multiply_convert_fusion.3), kind=kOutput, calls=%fused_computation.58 | convolution fusion | flops 2516582400 | bytes 11141120 | tf_op jit(solution)/shard_map/dot_general | solution.py:21
  145.8 9.0 %multiply_convert_fusion = (bf16[2560,512]{1,0:T(8,128)(2,1)S(1)}, bf16[2560,512]{1,0:T(8,128)(2,1)S(1)}, bf16[2560,512]{1,0:T(8,128)(2,1)}) fusion(f32[2560,512]{1,0:T(8,128)} %fusion.11, f32[2560,512]{1,0:T(8,128)} %fusion.12, bf16[2560,960]{1,0:T(8,128)(2,1)S(1)} %bitcast.153, bf16[512,960]{0,1:T(8,128)(2,1)S(1)} %bitcast.112), kind=kOutput, calls=%fused_computation | convolution fusion | flops 2537553920 | bytes 24248320 | tf_op jit(solution)/shard_map/dot_general | solution.py:21
  154.9 2.7 fusion.13
  157.6 3.8 multiply_reduce_fusion
  161.4 2.3 fusion.9
  163.6 114.8 %sum_weights.1 = (bf16[320,960]{1,0:T(8,128)(2,1)}, bf16[120,2560]{1,0:T(8,128)(2,1)}, bf16[120,2560]{1,0:T(8,128)(2,1)}, bf16[120,960]{1,0:T(8,128)(2,1)}) custom-call(bf16[8,320,512]{2,1,0:T(8,128)(2,1)} %bitcast.125, bf16[8,120,512]{2,1,0:T(8,128)(2,1)} %bitcast.121, bf16[8,120,512]{2,1,0:T(8,128)(2,1)} %bitcast.132, bf16[960,512]{1,0:T(8,128)(2,1)} %bitcast.114, ...), custom_call_target="tpu_custom_call" | custom-call | tf_op jit(solution)/shard_map/sum_weights/pallas_call | solution.py:755
  278.4 2.4 convert_element_type.96
  284.0 2.1 convolution_convert_fusion.do_ref
  286.1 17.2 %attention_bwd.1 = (bf16[960,512]{1,0:T(8,128)(2,1)}, bf16[8,2,2,640,128]{4,3,2,1,0:T(8,128)(2,1)}) custom-call(s32[2,2,2]{2,1,0:T(2,128)} %pad_add_fusion.info, s32[2,16]{1,0:T(2,128)} %select_reduce_fusion.kvat, bf16[960,512]{1,0:T(8,128)(2,1)} %bitcast.131, bf16[960,512]{1,0:T(8,128)(2,1)} %convolution_convert_fusion.do_ref, ...), custom_call_target="tpu_custom_call" | custom-call | flops 20000000000 | bytes 16000000 | tf_op jit(solution)/shard_map/attention_bwd/pallas_call | solution.py:203
  304.4 87.7 %sum_with_keys.1 = (bf16[120,960]{1,0:T(8,128)(2,1)}, bf16[120,640]{1,0:T(8,128)(2,1)}, f32[512,960]{1,0:T(8,128)}, f32[2,960]{1,0:T(2,128)}) custom-call(bf16[8,120,512]{2,1,0:T(8,128)(2,1)} %bitcast.118, bf16[960,512]{1,0:T(8,128)(2,1)} %get-tuple-element.39.refs_1_, bf16[8,2560,128]{2,1,0:T(8,128)(2,1)} %bitcast.117, bf16[960,960]{1,0:T(8,128)(2,1)} %bitcast.115, ...), custom_call_target="tpu_custom_call" | custom-call | tf_op jit(solution)/shard_map/sum_with_keys/pallas_call | solution.py:755
  392.1 3.0 copy.88
  396.7 1.8 convert_element_type.90
  399.1 7.0 %fusion.4 = bf16[512,960]{0,1:T(8,128)(2,1)} fusion(f32[960,512]{1,0:T(8,128)S(1)} %copy-done.5, bf16[512,960]{0,1:T(8,128)(2,1)S(1)} %bitcast.111, bf16[2560,512]{1,0:T(8,128)(2,1)} %get-tuple-element.101, bf16[2560,960]{1,0:T(8,128)(2,1)} %bitcast.150), kind=kOutput, calls=%fused_computation.12 | convolution fusion | flops 2518548480 | bytes 11468800 | tf_op jit(solution)/shard_map/dot_general | solution.py:21
  406.1 2.5 reshape.321
  (113 shorter events, 18.9 us)
Async XLA Ops:
  3.1 158.2 %copy-start = (bf16[120,8,2,256]{3,1,2,0:T(8,128)(2,1)}, bf16[120,8,2,256]{3,1,2,0:T(8,128)(2,1)S(1)}, u32[]{:S(2)}) copy-start(bf16[120,8,2,256]{3,1,2,0:T(8,128)(2,1)S(1)} %copy.92) | copy-start | bytes 2949124
  3.5 73.1 %copy-start.21 = (f32[512]{0:T(512)}, f32[512]{0:T(512)S(1)}, u32[]{:S(2)}) copy-start(f32[512]{0:T(512)S(1)} %add_rsqrt_fusion.1) | copy-start | bytes 6148
  4.1 77.4 %copy-start.6 = (bf16[960,512]{1,0:T(8,128)(2,1)}, bf16[960,512]{1,0:T(8,128)(2,1)S(1)}, u32[]{:S(2)}) copy-start(bf16[960,512]{1,0:T(8,128)(2,1)S(1)} %fusion.2) | copy-start | bytes 2949124
  78.1 3.5 copy-start.14
  79.8 39.8 %copy-start.22 = (s32[2,2,128]{2,1,0:T(2,128)}, s32[2,2,128]{2,1,0:T(2,128)S(1)}, u32[]{:S(2)}) copy-start(s32[2,2,128]{2,1,0:T(2,128)S(1)} %select_reduce_fusion.1) | copy-start | bytes 6148
  80.2 37.9 %copy-start.11 = (f32[32,512]{1,0:T(8,128)}, f32[32,512]{1,0:T(8,128)S(1)}, u32[]{:S(2)}) copy-start(f32[32,512]{1,0:T(8,128)S(1)} %get-tuple-element.110.cos_ref.refs_8_) | copy-start | bytes 196612
  80.2 37.9 %copy-start.12 = (f32[32,512]{1,0:T(8,128)}, f32[32,512]{1,0:T(8,128)S(1)}, u32[]{:S(2)}) copy-start(f32[32,512]{1,0:T(8,128)S(1)} %get-tuple-element.111.sin_ref.refs_9_) | copy-start | bytes 196612
  83.5 28.8 %copy-start.3 = (bf16[8,120,960]{2,1,0:T(8,128)(2,1)S(1)}, bf16[8,120,960]{2,1,0:T(8,128)(2,1)}, u32[]{:S(2)}) copy-start(bf16[8,120,960]{2,1,0:T(8,128)(2,1)} %get-tuple-element.31) | copy-start | bytes 5529604
  118.4 16.7 %slice-start.2 = ((s8[4915200]{0:T(1024)(128)(4,1)}), s8[4194304]{0:T(1024)(128)(4,1)S(1)}, s32[]{:S(2)}) async-start(s8[4915200]{0:T(1024)(128)(4,1)} %bitcast.154), calls=%async_computation.2 | async-start | bytes 8388608
  121.0 11.2 %copy-start.28 = (bf16[8,120,960]{2,1,0:T(8,128)(2,1)S(1)}, bf16[8,120,960]{2,1,0:T(8,128)(2,1)}, u32[]{:S(2)}) copy-start(bf16[8,120,960]{2,1,0:T(8,128)(2,1)} %get-tuple-element.30) | copy-start | bytes 5529604
  121.1 14.1 %slice-start.3 = ((s8[4915200]{0:T(1024)(128)(4,1)}), s8[720896]{0:T(1024)(128)(4,1)S(1)}, s32[]{:S(2)}) async-start(s8[4915200]{0:T(1024)(128)(4,1)} %bitcast.154), calls=%async_computation.3 | async-start | bytes 1441792
  134.7 26.6 %copy-start.4 = (f32[960,512]{1,0:T(8,128)}, f32[960,512]{1,0:T(8,128)S(1)}, u32[]{:S(2)}) copy-start(f32[960,512]{1,0:T(8,128)S(1)} %get-tuple-element.115) | copy-start | bytes 5898244
  134.7 5.1 %slice-start.4 = ((s8[4915200]{0:T(1024)(128)(4,1)}), s8[4194304]{0:T(1024)(128)(4,1)S(1)}, s32[]{:S(2)}) async-start(s8[4915200]{0:T(1024)(128)(4,1)} %bitcast.158), calls=%async_computation.4 | async-start | bytes 8388608
  135.1 4.7 %copy-start.7 = (bf16[960,512]{1,0:T(8,128)(2,1)}, bf16[960,512]{1,0:T(8,128)(2,1)S(1)}, u32[]{:S(2)}) copy-start(bf16[960,512]{1,0:T(8,128)(2,1)S(1)} %multiply_convert_fusion.3) | copy-start | bytes 2949124
  135.1 4.7 %slice-start.5 = ((s8[4915200]{0:T(1024)(128)(4,1)}), s8[720896]{0:T(1024)(128)(4,1)S(1)}, s32[]{:S(2)}) async-start(s8[4915200]{0:T(1024)(128)(4,1)} %bitcast.158), calls=%async_computation.5 | async-start | bytes 1441792
  135.1 10.6 %slice-start = ((s8[5242880]{0:T(1024)(128)(4,1)}), s8[4194304]{0:T(1024)(128)(4,1)S(1)}, s32[]{:S(2)}) async-start(s8[5242880]{0:T(1024)(128)(4,1)} %bitcast.151), calls=%async_computation | async-start | bytes 8388608
  139.8 4.7 %copy-start.13 = (bf16[2,1,256,960]{2,3,1,0:T(8,128)(2,1)S(1)}, bf16[2,1,256,960]{2,3,1,0:T(8,128)(2,1)}, u32[]{:S(2)}) copy-start(bf16[2,1,256,960]{2,3,1,0:T(8,128)(2,1)} %param.25) | copy-start | bytes 2949124
  139.8 5.9 %slice-start.1 = ((s8[5242880]{0:T(1024)(128)(4,1)}), s8[1048576]{0:T(1024)(128)(4,1)S(1)}, s32[]{:S(2)}) async-start(s8[5242880]{0:T(1024)(128)(4,1)} %bitcast.151), calls=%async_computation.1 | async-start | bytes 2097152
  145.7 15.6 %copy-start.2 = (bf16[120,8,2,256]{3,1,2,0:T(8,128)(2,1)}, bf16[120,8,2,256]{3,1,2,0:T(8,128)(2,1)S(1)}, u32[]{:S(2)}) copy-start(bf16[120,8,2,256]{3,1,2,0:T(8,128)(2,1)S(1)} %copy.93) | copy-start | bytes 2949124
  278.4 3.6 copy-start.15
  280.8 3.1 copy-start.8
  392.1 7.0 %copy-start.5 = (f32[960,512]{1,0:T(8,128)S(1)}, f32[960,512]{1,0:T(8,128)}, u32[]{:S(2)}) copy-start(f32[960,512]{1,0:T(8,128)} %copy-done.4) | copy-start | bytes 5898244
  395.1 3.4 copy-start.25
  395.1 4.1 copy-start.1
  (11 other events, 24.8 us)

commit v4 on v3

--- a/solution.py
+++ b/solution.py
@@ -255,120 +255,6 @@
     pl.semaphore_wait(barrier, len(peers))
 
 
-def gather_kernel(count, chunks, planes, *refs):
-    ins, outs = refs[:count], refs[count : 2 * count]
-    sent, came = refs[2 * count :]
-    at, row = lax.axis_index("wide"), lax.axis_index("narrow")
-    peer = {bit: (at ^ bit, row) for bit in (CORE, ALONG_X, ALONG_Y)}
-    if planes:
-        peer["row"] = (at, row ^ 1)
-
-    def part(ref, c, half):
-        return ref.at[chunks[c][1 + half]]
-
-    def copy(c, m, half, way, slot):
-        a = chunks[c][0]
-        there = part(outs[a].at[at ^ m], c, half)
-        return pltpu.make_async_remote_copy(
-            src_ref=there if m else part(ins[a], c, half),
-            dst_ref=there,
-            send_sem=sent.at[c, slot],
-            recv_sem=came.at[c, m if way == "row" else m ^ way, half],
-            device_id=peer[way],
-            device_id_type=pl.DeviceIdType.MESH,
-        )
-
-    def run(mine):
-        other = 1 - mine
-        used = [0] * len(chunks)
-        begun = []
-
-        def push(c, m, half, way):
-            r = copy(c, m, half, way, used[c])
-            used[c] += 1
-            r.start()
-            begun.append(r)
-
-        def take(c, m, half, *ways):
-            copy(c, m ^ CORE, half, CORE, 0).wait_recv()
-            for way in ways:
-                push(c, m, half, way)
-
-        def first(c):
-            push(c, 0, mine, ALONG_X)
-            push(c, 0, mine, ALONG_Y)
-            if not planes:
-                push(c, 0, other, ALONG_X)
-                push(c, 0, other, ALONG_Y)
-
-        def second(c):
-            if planes:
-                take(c, ALONG_Y, mine, ALONG_X, CORE)
-                push(c, 0, other, ALONG_Y)
-                take(c, ALONG_X, mine, "row", CORE)
-            else:
-                take(c, ALONG_X, mine, ALONG_Y, CORE)
-                take(c, ALONG_Y, other, ALONG_X, CORE)
-                take(c, ALONG_Y, mine, CORE)
-                take(c, ALONG_X, other, CORE)
-            push(c, 0, 0, CORE)
-            push(c, 0, 1, CORE)
-
-        def third(c):
-            take(c, FAR, mine, *(("row", CORE) if planes else (CORE,)))
-            if planes:
-                take(c, ALONG_Y, other, CORE)
-                take(c, ALONG_X, other, CORE)
-            else:
-                take(c, FAR, other, CORE)
-
-        def fourth(c):
-            if planes:
-                take(c, FAR, other, CORE)
-
-        def fifth(c):
-            for half in range(2):
-                take(c, CORE, half, CORE)
-            for m in (ALONG_X, ALONG_Y, FAR):
-                for half in range(2):
-                    take(c, m + CORE, half)
-
-        def sixth(c):
-            for half in range(2):
-                take(c, 0, half)
-
-        steps = (first, second, third, fourth, fifth, sixth)
-        for t in range(len(chunks) + LAG * (len(steps) - 1)):
-            for s, step in enumerate(steps):
-                if 0 <= t - LAG * s < len(chunks):
-                    step(t - LAG * s)
-        for r in begun:
-            r.wait_send()
-
-    meet(list(peer.values()))
-    if planes:
-        for mine in range(2):
-            pl.when(row % 2 == mine)(functools.partial(run, mine))
-    else:
-        run(0)
-
-
-def gather(arrays, chunks, planes, collective_id):
-    count = len(arrays)
-    return pl.pallas_call(
-        functools.partial(gather_kernel, count, chunks, planes),
-        in_specs=[pl.BlockSpec(memory_space=pl.ANY)] * count,
-        out_specs=[pl.BlockSpec(memory_space=pl.ANY)] * count,
-        out_shape=[jax.ShapeDtypeStruct((8,) + a.shape, a.dtype) for a in arrays],
-        scratch_shapes=[
-            SEM((len(chunks), 16)),
-            SEM((len(chunks), 8, 2)),
-        ],
-        compiler_params=pltpu.CompilerParams(collective_id=collective_id, has_side_effects=True),
-        name="gather_rows" if planes else "gather_keys",
-    )(*arrays)
-
-
 def weight_chunks(shapes, most=160 * 1024):
     chunks = []
     for a, (rows, cols) in enumerate(shapes):
@@ -387,19 +273,234 @@
     return chunks
 
 
-def key_chunks(micro, blocks, rows, parts=2):
-    return [
-        (0,) + tuple(
-            (m, pl.ds(blocks // 2 * h, blocks // 2), pl.ds(rows // parts * i, rows // parts))
-            for h in range(2)
-        )
-        for m in range(micro)
-        for i in range(parts)
-    ]
-
-
 def pieces_of(total, size):
     return [(lo, min(size, total - lo)) for lo in range(0, total, size)]
+
+
+def start_kernel(chunks, micro, *refs):
+    refs = list(refs)
+    take_refs = lambda n: [refs.pop(0) for _ in range(n)]
+    ins = take_refs(7)
+    far_x, gain_ref, cos_ref, sin_ref = take_refs(4)
+    outs = take_refs(7)
+    far_q, far_xn, far_kv, rr_ref = take_refs(4)
+    near_w = take_refs(3)
+    x, xn, q_s, own_kv, sent, came, local = take_refs(7)
+    at, row = lax.axis_index("wide"), lax.axis_index("narrow")
+    peer = {bit: (at ^ bit, row) for bit in (CORE, ALONG_X, ALONG_Y)}
+    peer["row"] = (at, row ^ 1)
+    keys = len(ins)
+    source = [*ins, own_kv]
+    land = [*near_w, *outs[3:], far_kv]
+    n = len(chunks)
+    kd = own_kv.shape[2] // 2
+    nq = own_kv.shape[1]
+    width, half = q_s.shape[0], HDIM // 2
+
+    mine_in = [pltpu.make_async_copy(ins[i], near_w[i].at[at], local.at[i]) for i in range(3)]
+    mine_in.append(pltpu.make_async_copy(far_x, x, local.at[3]))
+    give = [pltpu.make_async_copy(near_w[i], outs[i], local.at[4 + i]) for i in range(3)]
+    give_q = pltpu.make_async_copy(q_s, far_q, local.at[7])
+    give_xn = pltpu.make_async_copy(xn, far_xn, local.at[8])
+    give_kv = pltpu.make_async_copy(own_kv, far_kv.at[at], local.at[9])
+
+    def norm():
+        mine_in[3].wait()
+        count = x.shape[0]
+        square = jnp.zeros(rr_ref.shape, F32)
+        for j in range(count):
+            v = x[j].astype(F32)
+            square += jnp.sum(v * v, axis=0, keepdims=True)
+        rr = lax.rsqrt(square / width + EPS)
+        rr_ref[...] = rr
+        for j in range(count):
+            xn[j] = (x[j].astype(F32) * rr * gain_ref[j]).astype(BF16)
+        give_xn.start()
+
+    def turned(w, lo, size):
+        got = sum(dot(w[j, :, lo : lo + size], xn[j], 0, 0) for j in range(w.shape[0]))
+        return got
+
+    def heads(got):
+        cos, sin = cos_ref[...], sin_ref[...]
+        for h in range(0, got.shape[0], HDIM):
+            one, two = got[h : h + half], got[h + half : h + HDIM]
+            yield h, one * cos - two * sin
+            yield h + half, two * cos + one * sin
+
+    def to_keys(at_row, value):
+        value = value.astype(BF16)
+        for m in range(micro):
+            for i in range(nq):
+                lanes = slice((m * nq + i) * BLOCK, (m * nq + i + 1) * BLOCK)
+                own_kv[m, i, at_row : at_row + value.shape[0], :] = value[:, lanes]
+
+    def key_tile(lo, size):
+        for h, v in heads(turned(near_w[1], lo, size)):
+            to_keys(lo + h, v)
+
+    def value_tile(lo, size):
+        to_keys(kd + lo, turned(near_w[2], lo, size))
+
+    def query_tile(lo, size):
+        for h, v in heads(turned(near_w[0], lo, size)):
+            q_s[lo + h : lo + h + half, :] = v.astype(BF16) * HDIM**-0.5
+
+    def run(mine):
+        other = 1 - mine
+        used = [0] * n
+        begun = []
+
+        def part(ref, c, which):
+            return ref.at[chunks[c][1 + which]]
+
+        def copy(c, m, which, way, slot):
+            a = chunks[c][0]
+            there = part(land[a].at[at ^ m], c, which)
+            return pltpu.make_async_remote_copy(
+                src_ref=there if m else part(source[a], c, which),
+                dst_ref=there,
+                send_sem=sent.at[c, slot],
+                recv_sem=came.at[c, m if way == "row" else m ^ way, which],
+                device_id=peer[way],
+                device_id_type=pl.DeviceIdType.MESH,
+            )
+
+        def push(c, m, which, way):
+            r = copy(c, m, which, way, used[c])
+            used[c] += 1
+            r.start()
+            begun.append(r)
+
+        def take(c, m, which, *ways):
+            copy(c, m ^ CORE, which, CORE, 0).wait_recv()
+            for way in ways:
+                push(c, m, which, way)
+
+        planes = [c[0] != keys for c in chunks]
+        bounced = [2 < c[0] < keys for c in chunks]
+
+        def first(c):
+            push(c, 0, mine, ALONG_X)
+            push(c, 0, mine, ALONG_Y)
+            if not planes[c]:
+                push(c, 0, other, ALONG_X)
+                push(c, 0, other, ALONG_Y)
+
+        def second(c):
+            if planes[c]:
+                take(c, ALONG_Y, mine, ALONG_X, CORE)
+                push(c, 0, other, ALONG_Y)
+                take(c, ALONG_X, mine, "row", CORE)
+            else:
+                take(c, ALONG_X, mine, ALONG_Y, CORE)
+                take(c, ALONG_Y, other, ALONG_X, CORE)
+                take(c, ALONG_Y, mine, CORE)
+                take(c, ALONG_X, other, CORE)
+            push(c, 0, 0, CORE)
+            push(c, 0, 1, CORE)
+
+        def third(c):
+            take(c, FAR, mine, *(("row", CORE) if planes[c] else (CORE,)))
+            if planes[c]:
+                take(c, ALONG_Y, other, CORE)
+                take(c, ALONG_X, other, CORE)
+            else:
+                take(c, FAR, other, CORE)
+
+        def fourth(c):
+            if planes[c]:
+                take(c, FAR, other, CORE)
+
+        def fifth(c):
+            for which in range(2):
+                take(c, CORE, which, *((CORE,) if bounced[c] else ()))
+            for m in (ALONG_X, ALONG_Y, FAR):
+                for which in range(2):
+                    take(c, m + CORE, which)
+
+        def sixth(c):
+            if bounced[c]:
+                for which in range(2):
+                    take(c, 0, which)
+
+        steps = (first, second, third, fourth, fifth, sixth)
+        begins, ready = [], 0
+        for c in range(n):
+            begins.append(c)
+            if chunks[c][0] < 3:
+                ready = c + LAG * 4
+            if chunks[c][0] == keys:
+                begins[c] = max(begins[c - 1] + 1, ready + 1)
+        work = {1: [norm], ready: []}
+        for lo, size in pieces_of(kd, 256):
+            work[ready] += [functools.partial(key_tile, lo, size), functools.partial(value_tile, lo, size)]
+        work[ready].append(give_kv.start)
+        for i, (lo, size) in enumerate(pieces_of(width, 256)):
+            work[ready + 2 + i] = [functools.partial(query_tile, lo, size)]
+        for t in range(begins[-1] + LAG * (len(steps) - 1) + 1):
+            for s, step in enumerate(steps):
+                for c in range(n):
+                    if begins[c] + LAG * s == t:
+                        step(c)
+            if t == ready:
+                for r in mine_in[:3]:
+                    r.wait()
+                for r in give:
+                    r.start()
+            for job in work.get(t, ()):
+                job()
+        for r in begun:
+            r.wait_send()
+
+    for r in mine_in:
+        r.start()
+    meet(list(peer.values()))
+    for mine in range(2):
+        pl.when(row % 2 == mine)(functools.partial(run, mine))
+    give_q.start()
+    for r in (*give, give_q, give_xn, give_kv):
+        r.wait()
+
+
+def start_of(weights, x, gain, cos, sin, micro, collective_id):
+    count, high, tokens = x.shape
+    kd = weights[1].shape[1]
+    nq = tokens // micro // BLOCK
+    chunks = weight_chunks([a.shape for a in weights])
+    keys = len(weights)
+    for m in range(micro):
+        for i in range(2):
+            rows = pl.ds(kd * i, kd)
+            halves = [(m, pl.ds(nq // 2 * h, nq // 2), rows) for h in range(2)]
+            chunks.append((keys, *halves))
+    anywhere = pl.BlockSpec(memory_space=pl.ANY)
+    vmem = pl.BlockSpec(memory_space=pltpu.VMEM)
+    shape = jax.ShapeDtypeStruct
+    kv = (micro, nq, 2 * kd, BLOCK)
+    got = pl.pallas_call(
+        functools.partial(start_kernel, chunks, micro),
+        in_specs=[anywhere] * (keys + 1) + [vmem] * 3,
+        out_specs=[anywhere] * (keys + 3) + [vmem],
+        out_shape=[shape((count,) + a.shape, BF16) for a in weights]
+        + [shape((count * high, tokens), BF16), shape(x.shape, BF16), shape((count,) + kv, BF16)]
+        + [shape((1, tokens), F32)],
+        scratch_shapes=[pltpu.VMEM((count,) + a.shape, BF16) for a in weights[:3]]
+        + [
+            pltpu.VMEM(x.shape, BF16),
+            pltpu.VMEM(x.shape, BF16),
+            pltpu.VMEM((count * high, tokens), BF16),
+            pltpu.VMEM(kv, BF16),
+            SEM((len(chunks), 16)),
+            SEM((len(chunks), 8, 2)),
+            SEM((10,)),
+        ],
+        compiler_params=pltpu.CompilerParams(
+            collective_id=collective_id, has_side_effects=True, vmem_limit_bytes=VMEM_LIMIT
+        ),
+        name="gather_and_project",
+    )(*weights, x, gain, cos, sin)
+    return got[:keys], got[keys], got[keys + 1], got[keys + 2], got[keys + 3]
 
 
 class Unit:
@@ -820,18 +921,6 @@
 
     cube = n == CUBE and sizes["narrow"] == 4 and nq % 2 == 0
 
-    def whole_rows(*shards_of):
-        if cube:
-            got = gather(shards_of, weight_chunks([a.shape for a in shards_of]), True, 1)
-        else:
-            got = [lax.all_gather(a, "wide", axis=0) for a in shards_of]
-        return [a.reshape(-1, a.shape[2]) for a in got]
-
-    def whole_keys(own):
-        if cube:
-            return gather([own], key_chunks(*own.shape[:3]), False, 2)[0]
-        return lax.all_gather(own, "wide", axis=0)
-
     def shared(a):
         return a.reshape(n, -1, a.shape[1])
 
@@ -844,17 +933,24 @@
     ct_t = cotangent.reshape(total, width).T
     x = x_t.astype(F32)
 
-    g_query, g_key, g_value, g_out, g_gate, g_up, g_down = whole_rows(
-        w_query, w_key, w_value, w_out, w_gate, w_up, w_down
-    )
-    rr1 = lax.rsqrt(jnp.mean(x * x, axis=0, keepdims=True) + EPS)
-    xn = (x * rr1 * attn_gain[:, None]).astype(BF16)
-    key_t = turn(dot(g_key, xn, 0, 0), cos, sin).astype(BF16)
-    value_t = dot(g_value, xn, 0, 0).astype(BF16)
-    own_kv = jnp.concatenate([key_t, value_t]).reshape(2 * kd, micro, nq, BLOCK).transpose(1, 2, 0, 3)
-    q_t = (turn(dot(g_query, xn, 0, 0), cos, sin).astype(BF16) * HDIM**-0.5).astype(BF16)
-
-    kv = whole_keys(own_kv)
+    weights = (w_query, w_key, w_value, w_out, w_gate, w_up, w_down)
+    if cube:
+        by_device = lambda a: a.reshape(n, width // n, a.shape[1])
+        got, q_t, xn, kv, rr1 = start_of(
+            weights, by_device(x_t), by_device(attn_gain[:, None]), cos, sin, micro, 2
+        )
+        xn = xn.reshape(width, total)
+    else:
+        got = [lax.all_gather(a, "wide", axis=0) for a in weights]
+    g_query, g_key, g_value, g_out, g_gate, g_up, g_down = [a.reshape(-1, a.shape[2]) for a in got]
+    if not cube:
+        rr1 = lax.rsqrt(jnp.mean(x * x, axis=0, keepdims=True) + EPS)
+        xn = (x * rr1 * attn_gain[:, None]).astype(BF16)
+        key_t = turn(dot(g_key, xn, 0, 0), cos, sin).astype(BF16)
+        value_t = dot(g_value, xn, 0, 0).astype(BF16)
+        own_kv = jnp.concatenate([key_t, value_t]).reshape(2 * kd, micro, nq, BLOCK).transpose(1, 2, 0, 3)
+        q_t = (turn(dot(g_query, xn, 0, 0), cos, sin).astype(BF16) * HDIM**-0.5).astype(BF16)
+        kv = lax.all_gather(own_kv, "wide", axis=0)
     att_t, lse = attention_fwd(info, where_is, q_t, start, kv)
 
     res = x + dot(g_out, att_t, 0, 0)
@@ -879,16 +975,14 @@
     do_t = dot(g_out, d_attn, 1, 0).astype(BF16)
 
     pairs = [(hidden, ct_t), (hn, d_gate), (hn, d_up), (att_t, d_attn)]
+    most = 80 * 1024
+    high = width // n
     if cube:
-        units = weight_units(
-            [(0, 0, 0, ff // n, width), (1, 1, 1, width // n, ff), (1, 2, 2, width // n, ff),
-             (2, 3, 3, width // n, width)], 80 * 1024,
-        )
-        s_down, s_gate, s_up, s_out = sums(
-            units,
-            [shared(hidden), shared(hn), shared(att_t)],
-            [ct_t, d_gate, d_up, d_attn],
-            [(ff // n, width), (width // n, ff), (width // n, ff), (width // n, width)],
+        s_down, s_gate = sums(
+            weight_units([(0, 0, 0, ff // n, width), (1, 1, 1, high, ff)], most),
+            [shared(hidden), shared(hn)],
+            [ct_t, d_gate],
+            [(ff // n, width), (high, ff)],
             3,
         )
     else:
@@ -902,13 +996,14 @@
             Unit(None, None, None, (2 * kd * i, 2 * kd), (0, BLOCK), (ALONG_X, ALONG_Y)[i % 2])
             for i in range(blocks)
         ] + weight_units(
-            [(0, 0, 0, width // n, width), (0, None, 1, width // n, 2 * kd)], 80 * 1024
+            [(1, 1, 2, high, ff), (2, 2, 3, high, width), (0, 0, 0, high, width), (0, None, 1, high, 2 * kd)],
+            most,
         )
-        s_query, s_kv, grad_x, gains = sums(
+        s_query, s_kv, s_up, s_out, grad_x, gains = sums(
             units,
-            [shared(xn)],
-            [dq],
-            [(width // n, width), (width // n, 2 * kd)],
+            [shared(xn), shared(hn), shared(att_t)],
+            [dq, d_up, d_attn],
+            [(high, width), (high, 2 * kd), (high, ff), (high, width)],
             4,
             (keys, g_query, g_key, g_value, x_t, d_res, cos, sin, rr1, attn_gain[:, None], gain_two[None]),
         )

time: 415 us -> 386 us (0.930)
  Pallas kernels: 331 us -> 311 us
  matrix products: 41.2 us -> 34 us
    pallas_call x2, Pallas kernels: 202 us -> 185 us  [sums(): pl.pallas_call(functools.partial(sum_kernel, units, len(sources), len(tar...]
    pallas_call x2 -> x1, Pallas kernels: 99.7 us -> 92.2 us  [start_of(): pl.pallas_call(functools.partial(start_kernel, chunks, micro), in_specs=[...]
    dot_general x11 -> x8, matrix products: 41.2 us -> 34 us  [dot(): lax.dot_general(a, b, (((ca,), (cb,)), ((), ())), preferred_element_type=...]
    dot_general x2 -> x0, local copies, waits for them, and re-layouts: 4.22 us -> none  [dot(): lax.dot_general(a, b, (((ca,), (cb,)), ((), ())), preferred_element_type=...]
    unnamed x80 -> x68, local copies, waits for them, and re-layouts: 11.5 us -> 13 us
where the time goes in v4:
time: 386 us; the launch traced here: 382 us
  Pallas kernels  311 us (81%)
  matrix products  34 us (9%)
  local copies, waits for them, and re-layouts  18.4 us (5%)
  other arithmetic  17.8 us (5%)
    pallas_call x2, Pallas kernels, sums(): pl.pallas_call(functools.partial(sum_kernel, units, len(sources), len(tar...  185 us
    pallas_call x1, Pallas kernels, start_of(): pl.pallas_call(functools.partial(start_kernel, chunks, micro), in_specs=[...  92.2 us
    dot_general x8, matrix products, dot(): lax.dot_general(a, b, (((ca,), (cb,)), ((), ())), preferred_element_type=...  34 us
    pallas_call x1, Pallas kernels, attention_bwd(): pl.pallas_call(functools.partial(bwd_kernel, groups, share), grid_spec=pl...  20.2 us
    pallas_call x1, Pallas kernels, attention_fwd(): pl.pallas_call(functools.partial(fwd_kernel, groups, share), grid_spec=pl...  13.7 us
    unnamed x68, local copies, waits for them, and re-layouts  13 us
    convert_element_type x6, other arithmetic, shards(): wide_out = lambda a: a.astype(F32)  10.8 us

profile of v4, /device:TPU:0, one launch (start us, length us, event | category | flops | bytes accessed | tf_op | source)
XLA Modules:
  0.0 382.5 jit_solution(1193520798297854615)
XLA Ops:
  4.1 2.3 copy.69
  6.4 1.2 copy.83
  10.2 92.2 %gather_and_project.1 = (bf16[8,120,960]{2,1,0:T(8,128)(2,1)}, bf16[8,120,320]{2,1,0:T(8,128)(2,1)}, bf16[8,120,320]{2,1,0:T(8,128)(2,1)}, bf16[8,120,960]{2,1,0...) custom-call(bf16[120,960]{1,0:T(8,128)(2,1)} %refs_0_.1, ...), custom_call_target="tpu_custom_call" | custom-call | tf_op jit(solution)/shard_map/gather_and_project/pallas_call | solution.py:481
  103.8 13.7 %attention_fwd.1 = (bf16[960,512]{1,0:T(8,128)(2,1)}, f32[4,5,384]{2,1,0:T(8,128)}) custom-call(s32[2,2,2]{2,1,0:T(2,128)} %pad_add_fusion.info, s32[2,16]{1,0:T(2,128)} %select_reduce_fusion.kvat, bf16[960,512]{1,0:T(8,128)(2,1)} %get-tuple-element.35.q_ref, s32[1,512]{1,0:T(1,128)} %bitcast.103, bf16[8,2,2,640,128]{4,3,2,1,0:T(8,128)(2,1)} %get-tuple-element.36.kv_ref), custom_call_target="tpu_custom_call" | custom-call | flops 10000000000 | bytes 8000000 | tf_op jit(solution)/shard_map/attention_fwd/pallas_call | solution.py:97
  117.6 2.6 multiply_reduce_fusion.2
  120.2 1.2 copy-done.5
  121.9 3.0 fusion.5
  125.0 3.0 fusion.4
  129.3 7.6 %multiply_convert_fusion = (bf16[2560,512]{1,0:T(8,128)(2,1)}, bf16[2560,512]{1,0:T(8,128)(2,1)}, bf16[2560,512]{1,0:T(8,128)(2,1)}) fusion(f32[2560,512]{1,0:T(8,128)S(1)} %fusion.4, f32[2560,512]{1,0:T(8,128)S(1)} %fusion.5, bf16[2560,960]{1,0:T(8,128)(2,1)S(1)} %bitcast.119, bf16[512,960]{0,1:T(8,128)(2,1)S(1)} %bitcast.91), kind=kOutput, calls=%fused_computation | convolution fusion | flops 2537553920 | bytes 24248320 | tf_op jit(solution)/shard_map/dot_general | solution.py:21
  136.9 76.2 %sum_weights.1 = (bf16[320,960]{1,0:T(8,128)(2,1)}, bf16[120,2560]{1,0:T(8,128)(2,1)}) custom-call(bf16[8,320,512]{2,1,0:T(8,128)(2,1)} %bitcast.97, bf16[8,120,512]{2,1,0:T(8,128)(2,1)} %bitcast.89, bf16[960,512]{1,0:T(8,128)(2,1)} %bitcast.92, bf16[2560,512]{1,0:T(8,128)(2,1)} %get-tuple-element.108.refs_3_), custom_call_target="tpu_custom_call" | custom-call | tf_op jit(solution)/shard_map/sum_weights/pallas_call | solution.py:856
  213.1 2.4 convert_element_type.81
  215.5 2.4 convert_element_type.79
  218.0 4.9 %fusion.6 = f32[960,512]{1,0:T(8,128)S(1)} fusion(bf16[960,2560]{1,0:T(8,128)(2,1)} %bitcast.126, bf16[2560,512]{1,0:T(8,128)(2,1)S(1)} %copy-done.8), kind=kOutput, calls=%fused_computation.42 | convolution fusion | flops 2516582400 | bytes 9502720 | tf_op jit(solution)/shard_map/dot_general | solution.py:21
  223.0 3.7 multiply_reduce_fusion
  226.7 1.9 fusion.2
  228.6 2.1 convolution_convert_fusion.do_ref
  230.7 20.2 %attention_bwd.1 = (bf16[960,512]{1,0:T(8,128)(2,1)}, bf16[8,2,2,640,128]{4,3,2,1,0:T(8,128)(2,1)}) custom-call(s32[2,2,2]{2,1,0:T(2,128)} %pad_add_fusion.info, s32[2,16]{1,0:T(2,128)} %select_reduce_fusion.kvat, bf16[960,512]{1,0:T(8,128)(2,1)} %get-tuple-element.35.q_ref, bf16[960,512]{1,0:T(8,128)(2,1)} %convolution_convert_fusion.do_ref, ...), custom_call_target="tpu_custom_call" | custom-call | flops 20000000000 | bytes 16000000 | tf_op jit(solution)/shard_map/attention_bwd/pallas_call | solution.py:203
  252.0 108.5 %sum_with_keys.1 = (bf16[120,960]{1,0:T(8,128)(2,1)}, bf16[120,640]{1,0:T(8,128)(2,1)}, bf16[120,2560]{1,0:T(8,128)(2,1)}, bf16[120,960]{1,0:T(8,128)(2,1)}, f32[512,960]{1,0:T(8,128)}, /*index=5*/f32[2,960]{1,0:T(2,128)}) custom-call(bf16[8,120,512]{2,1,0:T(8,128)(2,1)} %get-tuple-element.41.refs_0_, bf16[8,120,512]{2,1,0:T(8,128)(2,1)} %bitcast.90, ...), custom_call_target="tpu_custom_call" | custom-call | tf_op jit(solution)/shard_map/sum_with_keys/pallas_call | solution.py:856
  360.5 2.9 copy.80
  363.3 2.3 convert_element_type.80
  367.3 1.8 convert_element_type.75
  369.1 1.8 convert_element_type.78
  371.5 7.0 %fusion.1 = bf16[512,960]{0,1:T(8,128)(2,1)} fusion(f32[960,512]{1,0:T(8,128)S(1)} %copy-done.6, bf16[512,960]{0,1:T(8,128)(2,1)S(1)} %bitcast.88, bf16[2560,512]{1,0:T(8,128)(2,1)} %get-tuple-element.109, bf16[2560,960]{1,0:T(8,128)(2,1)} %bitcast.116), kind=kOutput, calls=%fused_computation.6 | convolution fusion | flops 2518548480 | bytes 11468800 | tf_op jit(solution)/shard_map/dot_general | solution.py:21
  378.5 2.5 reshape.229
  (87 shorter events, 13.5 us)
Async XLA Ops:
  0.6 6.9 %copy-start.15 = (f32[960]{0:T(1024)S(1)}, f32[960]{0:T(1024)}, u32[]{:S(2)}) copy-start(f32[960]{0:T(1024)} %param.16) | copy-start | bytes 11524
  3.1 99.3 %copy-start.14 = (s32[2,2,128]{2,1,0:T(2,128)}, s32[2,2,128]{2,1,0:T(2,128)S(1)}, u32[]{:S(2)}) copy-start(s32[2,2,128]{2,1,0:T(2,128)S(1)} %select_reduce_fusion.1) | copy-start | bytes 6148
  4.1 4.5 %copy-start.12 = (bf16[120,320]{0,1:T(8,128)(2,1)S(1)}, bf16[120,320]{0,1:T(8,128)(2,1)}, u32[]{:S(2)}) copy-start(bf16[120,320]{0,1:T(8,128)(2,1)} %param.18) | copy-start | bytes 230404
  4.1 5.3 %copy-start.13 = (bf16[120,320]{0,1:T(8,128)(2,1)S(1)}, bf16[120,320]{0,1:T(8,128)(2,1)}, u32[]{:S(2)}) copy-start(bf16[120,320]{0,1:T(8,128)(2,1)} %param.19) | copy-start | bytes 230404
  10.2 92.9 %copy-start.18 = (s32[2,1,16]{2,1,0:T(1,128)S(1)}, s32[2,1,16]{2,1,0:T(1,128)}, u32[]{:S(2)}) copy-start(s32[2,1,16]{2,1,0:T(1,128)} %param.15) | copy-start | bytes 388
  103.8 13.7 %copy-start = (bf16[120,8,2,256]{3,1,2,0:T(8,128)(2,1)S(1)}, bf16[120,8,2,256]{3,1,2,0:T(8,128)(2,1)}, u32[]{:S(2)}) copy-start(bf16[120,8,2,256]{3,1,2,0:T(8,128)(2,1)} %copy.83) | copy-start | bytes 2949124
  103.8 13.7 %copy-start.19 = (bf16[8,120,960]{2,1,0:T(8,128)(2,1)S(1)}, bf16[8,120,960]{2,1,0:T(8,128)(2,1)}, u32[]{:S(2)}) copy-start(bf16[8,120,960]{2,1,0:T(8,128)(2,1)} %get-tuple-element.34) | copy-start | bytes 5529604
  117.5 4.3 %slice-start.2 = ((s8[4915200]{0:T(1024)(128)(4,1)}), s8[4194304]{0:T(1024)(128)(4,1)S(1)}, s32[]{:S(2)}) async-start(s8[4915200]{0:T(1024)(128)(4,1)} %bitcast.120), calls=%async_computation.2 | async-start | bytes 8388608
  117.5 3.9 %copy-start.16 = (f32[960]{0:T(1024)S(1)}, f32[960]{0:T(1024)}, u32[]{:S(2)}) copy-start(f32[960]{0:T(1024)} %param.21) | copy-start | bytes 11524
  117.6 4.3 %slice-start.3 = ((s8[4915200]{0:T(1024)(128)(4,1)}), s8[720896]{0:T(1024)(128)(4,1)S(1)}, s32[]{:S(2)}) async-start(s8[4915200]{0:T(1024)(128)(4,1)} %bitcast.120), calls=%async_computation.3 | async-start | bytes 1441792
  121.5 3.4 slice-start.6
  121.8 3.1 copy-start.2
  124.9 4.4 %slice-start = ((s8[5242880]{0:T(1024)(128)(4,1)}), s8[4194304]{0:T(1024)(128)(4,1)S(1)}, s32[]{:S(2)}) async-start(s8[5242880]{0:T(1024)(128)(4,1)} %bitcast.117), calls=%async_computation | async-start | bytes 8388608
  125.0 4.3 %slice-start.1 = ((s8[5242880]{0:T(1024)(128)(4,1)}), s8[1048576]{0:T(1024)(128)(4,1)S(1)}, s32[]{:S(2)}) async-start(s8[5242880]{0:T(1024)(128)(4,1)} %bitcast.117), calls=%async_computation.1 | async-start | bytes 2097152
  129.3 7.6 %copy-start.3 = (bf16[120,8,2,256]{3,1,2,0:T(8,128)(2,1)}, bf16[120,8,2,256]{3,1,2,0:T(8,128)(2,1)S(1)}, u32[]{:S(2)}) copy-start(bf16[120,8,2,256]{3,1,2,0:T(8,128)(2,1)S(1)} %copy.84) | copy-start | bytes 2949124
  213.1 4.9 %copy-start.8 = (bf16[2560,512]{1,0:T(8,128)(2,1)S(1)}, bf16[2560,512]{1,0:T(8,128)(2,1)}, u32[]{:S(2)}) copy-start(bf16[2560,512]{1,0:T(8,128)(2,1)} %get-tuple-element.108.refs_3_) | copy-start | bytes 7864324
  213.1 9.8 %slice-start.4 = ((s8[4915200]{0:T(1024)(128)(4,1)}), s8[4194304]{0:T(1024)(128)(4,1)S(1)}, s32[]{:S(2)}) async-start(s8[4915200]{0:T(1024)(128)(4,1)} %bitcast.123), calls=%async_computation.4 | async-start | bytes 8388608
  218.0 5.0 %copy-start.6 = (f32[960,512]{1,0:T(8,128)S(1)}, f32[960,512]{1,0:T(8,128)}, u32[]{:S(2)}) copy-start(f32[960,512]{1,0:T(8,128)} %copy-done.5) | copy-start | bytes 5898244
  218.0 5.0 %copy-start.9 = (bf16[2560,512]{1,0:T(8,128)(2,1)S(1)}, bf16[2560,512]{1,0:T(8,128)(2,1)}, u32[]{:S(2)}) copy-start(bf16[2560,512]{1,0:T(8,128)(2,1)} %get-tuple-element.107.refs_4_) | copy-start | bytes 7864324
  218.0 5.0 %slice-start.5 = ((s8[4915200]{0:T(1024)(128)(4,1)}), s8[720896]{0:T(1024)(128)(4,1)S(1)}, s32[]{:S(2)}) async-start(s8[4915200]{0:T(1024)(128)(4,1)} %bitcast.123), calls=%async_computation.5 | async-start | bytes 1441792
  223.0 3.7 copy-start.4
  360.5 5.2 %copy-start.11 = (bf16[120,640]{1,0:T(8,128)(2,1)S(1)}, bf16[120,640]{1,0:T(8,128)(2,1)}, u32[]{:S(2)}) copy-start(bf16[120,640]{1,0:T(8,128)(2,1)} %get-tuple-element.52) | copy-start | bytes 460804
  363.3 7.5 %copy-start.17 = (f32[2,960]{1,0:T(2,128)S(1)}, f32[2,960]{1,0:T(2,128)}, u32[]{:S(2)}) copy-start(f32[2,960]{1,0:T(2,128)} %get-tuple-element.50) | copy-start | bytes 23044
  363.3 8.1 %copy-start.1 = (bf16[120,8,2,256]{3,1,2,0:T(8,128)(2,1)S(1)}, bf16[120,8,2,256]{3,1,2,0:T(8,128)(2,1)}, u32[]{:S(2)}) copy-start(bf16[120,8,2,256]{3,1,2,0:T(8,128)(2,1)} %copy.83) | copy-start | bytes 2949124
  (5 other events, 11.5 us)
